TPU v7x, 32 devices: a whole 2x2x4 slice. The times are simulated.
32 devices in a mesh: replica: 8 (over y, x, core), tensor: 4 (over z).
Axes of the slice: x: 2, y: 2, z: 4, core: 2. Of those that a mesh axis runs over, the one named last changes fastest.
Arguments:
- train_hidden: bfloat16 [1024, 14784], P(None, 'replica'), may hold values from -6 to 6
- out_grad: bfloat16 [1024, 4096], P('tensor'), may hold values from -6 to 6
- master: float32 [14784, 4096], P('replica', 'tensor'), may hold values from -0.046875 to 0.046875
- first_moment: float32 [14784, 4096], P('replica', 'tensor'), may hold values from -6 to 6
- second_moment: float32 [14784, 4096], P('replica', 'tensor'), may hold values from 0.25 to 4
- decode_hidden: bfloat16 [2048, 14784], P('replica'), may hold values from -6 to 6
Outputs:
- new_master: float32 [14784, 4096], P('replica', 'tensor')
- new_first: float32 [14784, 4096], P('replica', 'tensor')
- new_second: float32 [14784, 4096], P('replica', 'tensor')
- decoded: bfloat16 [2048, 4096], P('replica', 'tensor')
All inputs are finite; a program needn't handle non-finite values.
Results may differ from a plain program's by a relative error of at most 0.0049.
Values may be sent and summed in bfloat16 or wider, within the bound.
No kernel may reach another device: no remote copies, remote signals or barrier semaphores. Data moves between devices by JAX's collectives and lax.ppermute only.
A program may use at most 128 MiB of HBM per device.

v0:
```python
import math

import jax
import jax.numpy as jnp
from jax import lax
from jax.sharding import PartitionSpec as P


def per_device(train_hidden, out_grad, master, first_moment, second_moment, decode_hidden):
    tokens_all = train_hidden.shape[0]
    columns = lax.all_to_all(out_grad, "tensor", split_axis=1, concat_axis=0, tiled=True)
    grad = lax.dot_general(
        train_hidden, columns, (((0,), (0,)), ((), ())), preferred_element_type=jnp.float32
    )
    grad = grad * (1.0 / math.sqrt(tokens_all))
    new_first = 0.9 * first_moment + 0.1 * grad
    new_second = 0.95 * second_moment + 0.05 * grad * grad
    new_master = master - 0.002 * new_first / (jnp.sqrt(new_second) + 1e-08)
    weights = new_master.astype(jnp.bfloat16)
    summed = jnp.dot(
        decode_hidden,
        lax.all_gather(weights, "replica", axis=0, tiled=True),
        preferred_element_type=jnp.float32,
    )
    return (new_master, new_first, new_second, summed.astype(jnp.bfloat16))


def solution(mesh):
    placed = (
        P(None, "replica"),
        P("tensor", None),
        P("replica", "tensor"),
        P("replica", "tensor"),
        P("replica", "tensor"),
        P("replica", None),
    )
    return jax.shard_map(
        per_device,
        mesh=mesh,
        in_specs=placed,
        out_specs=(
            P("replica", "tensor"),
            P("replica", "tensor"),
            P("replica", "tensor"),
            P("replica", "tensor"),
        ),
        check_vma=False,
    )
```

profile of v0, /device:TPU:0, one launch (start us, length us, event | category | flops | bytes accessed | tf_op | source)
XLA Modules:
  0.0 258.9 jit_solution(10671093832744189837)
XLA Ops:
  7.2 0.0 all-gather.2.cloned.1.call-start
  7.2 4.1 %copy.12 = bf16[256,4096]{0,1:T(8,128)(2,1)} copy(bf16[256,4096]{1,0:T(8,128)(2,1)} %param.7) | data formatting | bytes 4194304 | tf_op args[1]
  11.3 54.5 %all_to_all.19 = bf16[256,4,1024]{0,2,1:T(8,128)(2,1)S(1)} all-to-all(bf16[256,4,1024]{0,2,1:T(8,128)(2,1)} %bitcast.10), channel_id=1, replica_groups=mesh['replica'=8,'tensor'=4] {'tensor'}, dimensions={1} | all-to-all | bytes 4194304 | tf_op jit(solution)/shard_map/all_to_all | solution.py:11
  65.8 2.5 copy.13
  68.3 20.5 %fusion.1 = (bf16[1848,1024]{1,0:T(8,128)(2,1)}, f32[1848,1024]{1,0:T(8,128)}, f32[1848,1024]{1,0:T(8,128)}, f32[1848,1024]{1,0:T(8,128)}) fusion(f32[1848,1024]{1,0:T(8,128)} %param.8, f32[1848,1024]{1,0:T(8,128)} %param.9, f32[1848,1024]{1,0:T(8,128)} %param.10, bf16[1024,1848]{0,1:T(8,128)(2,1)} %param.6, bf16[1024,1024]{1,0:T(8,128)(2,1)} %bitcast.11), kind=kOutput, calls=%fused_computation.5 | convolution fusion | flops 3900137472 | bytes 55083008 | tf_op jit(solution)/shard_map/dot_general | solution.py:12
  88.8 0.0 all-gather.2.cloned.1.call-update
  88.8 146.3 %all-gather.2.cloned.1.call-done = bf16[14784,1024]{1,0:T(8,128)(2,1)} async-done(((bf16[1848,1024]{1,0:T(8,128)(2,1)}), bf16[14784,1024]{1,0:T(8,128)(2,1)}) %all-gather.2.cloned.1.call-update) | async-done | bytes 30277648 | tf_op jit(solution)/shard_map/all_gather | solution.py:22
  235.1 15.9 %fusion = bf16[256,1024]{0,1:T(8,128)(2,1)S(1)} fusion(bf16[14784,1024]{1,0:T(8,128)(2,1)} %all-gather.2.cloned.1.call-done, bf16[256,14784]{0,1:T(8,128)(2,1)} %param.11), kind=kOutput, calls=%fused_computation.4 | convolution fusion | flops 7751335936 | bytes 38371328 | tf_op jit(solution)/shard_map/dot_general | solution.py:20
  251.1 1.0 copy.14
Async XLA Ops:
  7.2 228.0 %all-gather.2.cloned.1.call-start = ((), (), s32[]{:S(2)}) async-start(), calls=%async_computation.1 | async-start | bytes 34062336 | tf_op jit(solution)/shard_map/all_gather | solution.py:22
Sparse Core Ops, SparseCore 0:
  88.9 146.1 all-gather.1
where the time goes:
time: 259 us
  waiting for transfers between devices  146 us (56%)
  blocking collectives  54.5 us (21%)
  matrix products  36.4 us (14%)
  between operations  14 us (5%)
  local copies, waits for them, and re-layouts  7.56 us (3%)
    all_gather x1, waiting for transfers between devices, per_device(): lax.all_gather(weights, 'replica', axis=0, tiled=True)  146 us
    all_to_all x1, blocking collectives, per_device(): lax.all_to_all(out_grad, 'tensor', split_axis=1, concat_axis=0, tiled=True)  54.5 us
    dot_general x1, matrix products, per_device(): lax.dot_general(train_hidden, columns, (((0,), (0,)), ((), ())), preferre...  20.5 us
    dot_general x1, matrix products, per_device(): jnp.dot(decode_hidden, lax.all_gather(weights, 'replica', axis=0, tiled=T...  15.9 us
  transfers between devices with their start and end apart: 1, of which 1 were waited for; matrix products, arithmetic and copies ran while one was open for 0% of the time, Pallas kernels for 0%

commit v1 on v0

--- a/solution.py
+++ b/solution.py
@@ -6,9 +6,69 @@
 from jax.sharding import PartitionSpec as P
 
 
+def xor_permute(array, axis, size, mask):
+    return lax.ppermute(array, axis, [(i, i ^ mask) for i in range(size)])
+
+
+def gather_columns(out_grad, devices, planes):
+    mine = lax.axis_index("tensor")
+    half = lax.rem(lax.axis_index("replica"), 2)
+    tokens, width = out_grad.shape[0], out_grad.shape[1] // planes
+    own = lax.dynamic_slice(out_grad, (0, mine * width), (tokens, width))
+    pieces = []
+    for mask in range(1, planes):
+        block = lax.dynamic_slice(
+            out_grad, (half * (tokens // 2), (mine ^ mask) * width), (tokens // 2, width)
+        )
+        pieces.append(xor_permute(block, "tensor", planes, mask))
+    fetched = jnp.stack(pieces)
+    other = xor_permute(fetched, "replica", devices, 1)
+    both = jnp.where(
+        half == 0,
+        jnp.concatenate([fetched, other], axis=1),
+        jnp.concatenate([other, fetched], axis=1),
+    )
+    stacked = jnp.concatenate([own[None], both], axis=0)
+    ordered = [
+        lax.dynamic_index_in_dim(stacked, mine ^ plane, 0, keepdims=False)
+        for plane in range(planes)
+    ]
+    return jnp.concatenate(ordered, axis=0)
+
+
 def per_device(train_hidden, out_grad, master, first_moment, second_moment, decode_hidden):
+    devices, planes = lax.axis_size("replica"), lax.axis_size("tensor")
+    chips = devices // 2
+    chip = lax.axis_index("replica") // 2
+    parity = lax.rem(lax.axis_index("tensor"), 2)
     tokens_all = train_hidden.shape[0]
-    columns = lax.all_to_all(out_grad, "tensor", split_axis=1, concat_axis=0, tiled=True)
+    rows, hidden = decode_hidden.shape
+    block = hidden // chips
+
+    windows = jnp.stack(
+        [decode_hidden[:, k * block : (k + 1) * block] for k in range(chips)]
+    )
+
+    def part(mask, start, count):
+        return lax.dynamic_slice(windows, (chip ^ mask, start, 0), (1, count, block))[0]
+
+    columns = gather_columns(out_grad, devices, planes)
+
+    held = {}
+    order = sorted(range(1, chips), key=lambda m: -m.bit_count())
+    for mask in order:
+        direct = 0 if mask.bit_count() > 1 else rows // 2
+        shared = (rows - direct) // 2
+        pieces = []
+        if direct:
+            sent = part(mask, 0, direct)
+            pieces.append(xor_permute(sent, "replica", devices, 2 * mask))
+        sent = part(mask, direct + parity * shared, shared)
+        mine = xor_permute(sent, "replica", devices, 2 * mask)
+        pieces.append(mine)
+        pieces.append(xor_permute(mine, "tensor", planes, 1))
+        held[mask] = (direct, shared, jnp.concatenate(pieces, axis=0))
+
     grad = lax.dot_general(
         train_hidden, columns, (((0,), (0,)), ((), ())), preferred_element_type=jnp.float32
     )
@@ -17,12 +77,25 @@
     new_second = 0.95 * second_moment + 0.05 * grad * grad
     new_master = master - 0.002 * new_first / (jnp.sqrt(new_second) + 1e-08)
     weights = new_master.astype(jnp.bfloat16)
-    summed = jnp.dot(
-        decode_hidden,
-        lax.all_gather(weights, "replica", axis=0, tiled=True),
-        preferred_element_type=jnp.float32,
+
+    swapped = xor_permute(weights, "replica", devices, 1)
+    first = lax.rem(lax.axis_index("replica"), 2) == 0
+    pair = jnp.concatenate(
+        [jnp.where(first, weights, swapped), jnp.where(first, swapped, weights)], axis=0
     )
-    return (new_master, new_first, new_second, summed.astype(jnp.bfloat16))
+
+    def partial(held_rows):
+        return jnp.dot(held_rows, pair, preferred_element_type=jnp.float32)
+
+    total = partial(part(0, 0, rows))
+    for mask in order:
+        direct, shared, held_rows = held[mask]
+        sums = partial(held_rows).astype(jnp.bfloat16)
+        back = xor_permute(sums, "replica", devices, 2 * mask).astype(jnp.float32)
+        low, high = back[direct : direct + shared], back[direct + shared :]
+        low, high = jnp.where(parity == 0, low, high), jnp.where(parity == 0, high, low)
+        total = total + jnp.concatenate([back[:direct], low, high], axis=0)
+    return (new_master, new_first, new_second, total.astype(jnp.bfloat16))
 
 
 def solution(mesh):

time: 259 us -> 155 us (0.60)
  waiting for transfers between devices: 146 us -> 68.6 us
  blocking collectives: 54.5 us -> 0 us
  starting transfers between devices: 0.04 us -> 24.2 us
  between operations: 14 us -> 0.97 us
  other arithmetic: 0 us -> 7.51 us
  local copies, waits for them, and re-layouts: 7.56 us -> 14.3 us
    all_gather x1 -> x0, waiting for transfers between devices: 146 us -> none  [per_device(): lax.all_gather(weights, 'replica', axis=0, tiled=True)]
    ppermute x0 -> x16, waiting for transfers between devices: none -> 68.6 us  [xor_permute(): return lax.ppermute(array, axis, [(i, i ^ mask) for i in range(size)])]
    all_to_all x1 -> x0, blocking collectives: 54.5 us -> none  [per_device(): lax.all_to_all(out_grad, 'tensor', split_axis=1, concat_axis=0, tiled=True)]
    ppermute x0 -> x16, starting transfers between devices: none -> 24.2 us  [xor_permute(): return lax.ppermute(array, axis, [(i, i ^ mask) for i in range(size)])]
    select_n x0 -> x5, other arithmetic: none -> 4.7 us  [the longest x1 3.72 us: per_device(): jnp.where(first, weights, swapped)]
    ppermute x0 -> x4, local copies, waits for them, and re-layouts: none -> 3.68 us  [xor_permute(): return lax.ppermute(array, axis, [(i, i ^ mask) for i in range(size)])]
    squeeze x0 -> x1, local copies, waits for them, and re-layouts: none -> 3.39 us  [part(): lax.dynamic_slice(windows, (chip ^ mask, start, 0), (1, count, block))[0]]
    dot_general x1 -> x4, matrix products: 15.9 us -> 16.8 us  [partial(): return jnp.dot(held_rows, pair, preferred_element_type=jnp.float32)]
  transfers between devices with their start and end apart: 1 -> 16, of which waited for: 1 -> 10; matrix products, arithmetic and copies ran while one was open for 0% -> 18% of each run, Pallas kernels for 0% -> 0%
where the time goes in v1:
time: 155 us; the launch traced here: 153 us
  waiting for transfers between devices  68.6 us (44%)
  matrix products  37.4 us (24%)
  starting transfers between devices  24.2 us (16%)
  local copies, waits for them, and re-layouts  14.3 us (9%)
  other arithmetic  7.51 us (5%)
    ppermute x16, waiting for transfers between devices, xor_permute(): return lax.ppermute(array, axis, [(i, i ^ mask) for i in range(size)])  68.6 us
    ppermute x16, starting transfers between devices, xor_permute(): return lax.ppermute(array, axis, [(i, i ^ mask) for i in range(size)])  24.2 us
    dot_general x1, matrix products, per_device(): lax.dot_general(train_hidden, columns, (((0,), (0,)), ((), ())), preferre...  20.6 us
    dot_general x4, matrix products, partial(): return jnp.dot(held_rows, pair, preferred_element_type=jnp.float32)  16.8 us
    select_n x1, other arithmetic, per_device(): jnp.where(first, weights, swapped)  3.72 us
    ppermute x4, local copies, waits for them, and re-layouts, xor_permute(): return lax.ppermute(array, axis, [(i, i ^ mask) for i in range(size)])  3.68 us
    squeeze x1, local copies, waits for them, and re-layouts, part(): lax.dynamic_slice(windows, (chip ^ mask, start, 0), (1, count, block))[0]  3.39 us
  transfers between devices with their start and end apart: 16, of which 10 were waited for; matrix products, arithmetic and copies ran while one was open for 18% of the time, Pallas kernels for 0%

profile of v1, /device:TPU:0, one launch (start us, length us, event | category | flops | bytes accessed | tf_op | source)
XLA Modules:
  0.0 152.9 jit_solution(17313376166789808536)
XLA Ops:
  1.8 3.1 %collective-permute-start = (bf16[128,1024]{1,0:T(8,128)(2,1)S(1)}, bf16[128,1024]{1,0:T(8,128)(2,1)S(1)}, u32[]{:S(2)}, u32[]{:S(2)}) collective-permute-start(bf16[128,1024]{1,0:T(8,128)(2,1)S(1)} %get-tuple-element.23), channel_id=1, source_target_pairs={{0,1},{1,0},{2,3},{3,2},{4,5},{5,4},{6,7},{7,6},{8,9},{9,8},{10,11... | collective-permute-start | bytes 786440 | tf_op jit(solution)/shard_map/ppermute | solution.py:10
  4.9 2.6 %collective-permute-start.1 = (bf16[128,1024]{1,0:T(8,128)(2,1)S(1)}, bf16[128,1024]{1,0:T(8,128)(2,1)S(1)}, u32[]{:S(2)}, u32[]{:S(2)}) collective-permute-start(bf16[128,1024]{1,0:T(8,128)(2,1)S(1)} %get-tuple-element.25), channel_id=1, source_target_pairs={{0,2},{1,3},{2,0},{3,1},{4,6},{5,7},{6,4},{7,5},{8,10},{9,11},{10,... | collective-permute-start | bytes 786440 | tf_op jit(solution)/shard_map/ppermute | solution.py:10
  7.5 8.6 %collective-permute-done = bf16[128,1024]{1,0:T(8,128)(2,1)S(1)} collective-permute-done((bf16[128,1024]{1,0:T(8,128)(2,1)S(1)}, bf16[128,1024]{1,0:T(8,128)(2,1)S(1)}, u32[]{:S(2)}, u32[]{:S(2)}) %collective-permute-start) | collective-permute-done | bytes 262176 | tf_op jit(solution)/shard_map/ppermute | solution.py:10
  16.1 10.2 %collective-permute-done.1 = bf16[128,1024]{1,0:T(8,128)(2,1)S(1)} collective-permute-done((bf16[128,1024]{1,0:T(8,128)(2,1)S(1)}, bf16[128,1024]{1,0:T(8,128)(2,1)S(1)}, u32[]{:S(2)}, u32[]{:S(2)}) %collective-permute-start.1) | collective-permute-done | bytes 262176 | tf_op jit(solution)/shard_map/ppermute | solution.py:10
  30.4 20.6 %fusion.61 = (bf16[1848,1024]{1,0:T(8,128)(2,1)}, f32[1848,1024]{1,0:T(8,128)}, f32[1848,1024]{1,0:T(8,128)}, f32[1848,1024]{1,0:T(8,128)}) fusion(f32[1848,1024]{1,0:T(8,128)} %param.8, f32[1848,1024]{1,0:T(8,128)} %param.9, f32[1848,1024]{1,0:T(8,128)} %param.10, bf16[1024,1848]{0,1:T(8,128)(2,1)} %param.6, bf16[256,1024]{1,0:T(8,128)(2,1)S(1)} %get-tuple-element.22, ...), kind=kOutput, calls=%fused_computation.80 | convolution fusion | flops 3908526080 | bytes 55083008 | tf_op jit(solution)/shard_map/dot_general | solution.py:72
  51.7 1.6 %pad_maximum_fusion = bf16[4,256,3696]{1,2,0:T(8,128)(2,1)S(1)} fusion(bf16[1,256,3696]{1,2,0:T(8,128)(2,1)S(1)} %get-tuple-element.17, bf16[1,256,3696]{1,2,0:T(8,128)(2,1)S(1)} %get-tuple-element.18, bf16[1,256,3696]{1,2,0:T(8,128)(2,1)S(1)} %get-tuple-element.16, bf16[1,256,3696]{1,2,0:T(8,128)(2,1)S(1)} %get-tuple-element.15), kind=kLoop, calls=%fused_computation | loop fusion | flops 11354112 | bytes 15138816 | tf_op jit(solution)/shard_map/stack | solution.py:48
  53.3 2.9 %copy-done = bf16[4,256,3696]{1,2,0:T(8,128)(2,1)} copy-done((bf16[4,256,3696]{1,2,0:T(8,128)(2,1)}, bf16[4,256,3696]{1,2,0:T(8,128)(2,1)S(1)}, u32[]{:S(2)}) %copy-start) | copy-done | bytes 7569432
  57.3 1.6 %collective-permute-start.13 = (bf16[64,3696]{1,0:T(8,128)(2,1)S(1)}, bf16[64,3696]{1,0:T(8,128)(2,1)S(1)}, u32[]{:S(2)}, u32[]{:S(2)}) collective-permute-start(bf16[64,3696]{1,0:T(8,128)(2,1)S(1)} %bitcast.56), channel_id=1, source_target_pairs={{0,16},{4,20},{8,24},{12,28},{16,0},{20,4},{24,8},{28,12},{1,17},{... | collective-permute-start | bytes 1419272 | tf_op jit(solution)/shard_map/ppermute | solution.py:10
  60.8 3.4 %dynamic-slice_bitcast_fusion = (bf16[128,3696]{0,1:T(8,128)(2,1)}, bf16[128,3696]{0,1:T(8,128)(2,1)}, bf16[128,3696]{0,1:T(8,128)(2,1)}) fusion(bf16[4,256,3696]{1,2,0:T(8,128)(2,1)} %copy-done, s32[]{:T(128)S(6)} %select_n.134, s32[]{:T(128)S(6)} %select_n.129, s32[]{:T(128)S(6)} %select_n.125, s32[]{:T(128)S(6)} %select_n.126), kind=kLoop, calls=%fused_computation.54 | loop fusion | bytes 5677072 | tf_op jit(solution)/shard_map/squeeze | solution.py:53
  64.6 5.8 %collective-permute-done.13 = bf16[64,3696]{1,0:T(8,128)(2,1)S(1)} collective-permute-done((bf16[64,3696]{1,0:T(8,128)(2,1)S(1)}, bf16[64,3696]{1,0:T(8,128)(2,1)S(1)}, u32[]{:S(2)}, u32[]{:S(2)}) %collective-permute-start.13) | collective-permute-done | bytes 473120 | tf_op jit(solution)/shard_map/ppermute | solution.py:10
  70.5 4.8 %collective-permute-start.14 = (bf16[64,3696]{1,0:T(8,128)(2,1)S(1)}, bf16[64,3696]{1,0:T(8,128)(2,1)S(1)}, u32[]{:S(2)}, u32[]{:S(2)}) collective-permute-start(bf16[64,3696]{1,0:T(8,128)(2,1)S(1)} %collective-permute-done.13), channel_id=1, source_target_pairs={{0,1},{1,0},{2,3},{3,2},{4,5},{5,4},{6,7},{7,6},{8,9},{9,8},{10,11... | collective-permute-start | bytes 1419272 | tf_op jit(solution)/shard_map/ppermute | solution.py:10
  75.2 2.5 %collective-permute-start.10 = (bf16[64,3696]{1,0:T(8,128)(2,1)S(1)}, bf16[64,3696]{1,0:T(8,128)(2,1)}, u32[]{:S(2)}, u32[]{:S(2)}) collective-permute-start(bf16[64,3696]{1,0:T(8,128)(2,1)S(1)} %collective-permute-done.9), channel_id=1, source_target_pairs={{0,1},{1,0},{2,3},{3,2},{4,5},{5,4},{6,7},{7,6},{8,9},{9,8},{10,11... | collective-permute-start | bytes 1419272 | tf_op jit(solution)/shard_map/ppermute | solution.py:10
  79.2 7.8 %collective-permute-done.14 = bf16[64,3696]{1,0:T(8,128)(2,1)S(1)} collective-permute-done((bf16[64,3696]{1,0:T(8,128)(2,1)S(1)}, bf16[64,3696]{1,0:T(8,128)(2,1)S(1)}, u32[]{:S(2)}, u32[]{:S(2)}) %collective-permute-start.14) | collective-permute-done | bytes 473120 | tf_op jit(solution)/shard_map/ppermute | solution.py:10
  89.7 6.3 %collective-permute-done.10 = bf16[64,3696]{1,0:T(8,128)(2,1)} collective-permute-done((bf16[64,3696]{1,0:T(8,128)(2,1)S(1)}, bf16[64,3696]{1,0:T(8,128)(2,1)}, u32[]{:S(2)}, u32[]{:S(2)}) %collective-permute-start.10) | collective-permute-done | bytes 473120 | tf_op jit(solution)/shard_map/ppermute | solution.py:10
  97.6 1.8 %collective-permute-start.6 = (bf16[128,3696]{0,1:T(8,128)(2,1)}, bf16[128,3696]{0,1:T(8,128)(2,1)S(1)}, u32[]{:S(2)}, u32[]{:S(2)}) collective-permute-start(bf16[128,3696]{0,1:T(8,128)(2,1)} %collective-permute-done.5), channel_id=1, source_target_pairs={{0,1},{1,0},{2,3},{3,2},{4,5},{5,4},{6,7},{7,6},{8,9},{9,8},{10,11... | collective-permute-start | bytes 2838536 | tf_op jit(solution)/shard_map/ppermute | solution.py:10
  99.4 3.7 %broadcast_select_fusion.1 = (bf16[1848,1024]{1,0:T(8,128)(2,1)S(1)}, bf16[1848,1024]{1,0:T(8,128)(2,1)S(1)}) fusion(bf16[1848,1024]{1,0:T(8,128)(2,1)} %get-tuple-element.4, bf16[1848,1024]{1,0:T(8,128)(2,1)} %collective-permute-done.4, pred[]{:T(512)S(6)} %eq.4), kind=kLoop, calls=%fused_computation.6 | loop fusion | flops 3784704 | bytes 15138817 | tf_op jit(solution)/shard_map/jit(_where)/select_n | solution.py:84
  103.2 9.6 %collective-permute-done.12 = bf16[128,3696]{0,1:T(8,128)(2,1)} collective-permute-done((bf16[128,3696]{0,1:T(8,128)(2,1)}, bf16[128,3696]{0,1:T(8,128)(2,1)}, u32[]{:S(2)}, u32[]{:S(2)}) %collective-permute-start.12) | collective-permute-done | bytes 946208 | tf_op jit(solution)/shard_map/ppermute | solution.py:10
  112.8 4.3 %fusion.36 = bf16[256,1024]{1,0:T(8,128)(2,1)} fusion(bf16[64,3696]{0,1:T(8,128)(2,1)S(1)} %copy-done.5, bf16[64,3696]{0,1:T(8,128)(2,1)S(1)} %copy.14, bf16[128,3696]{0,1:T(8,128)(2,1)} %collective-permute-done.12, bf16[1848,1024]{1,0:T(8,128)(2,1)S(1)} %get-tuple-element.14, bf16[1848,1024]{1,0:T(8,128)(2,1)S(1)} %get-tuple-element.13), kind=kOutput, calls=%fused_computation.50 | convolution fusion | flops 1958846464 | bytes 9986048 | tf_op jit(solution)/shard_map/dot_general | solution.py:88
  118.6 4.3 %fusion.39 = bf16[256,1024]{1,0:T(8,128)(2,1)} fusion(bf16[64,3696]{0,1:T(8,128)(2,1)S(1)} %copy.12, bf16[64,3696]{0,1:T(8,128)(2,1)S(1)} %copy.11, bf16[128,3696]{0,1:T(8,128)(2,1)} %collective-permute-done.8, bf16[1848,1024]{1,0:T(8,128)(2,1)S(1)} %get-tuple-element.14, bf16[1848,1024]{1,0:T(8,128)(2,1)S(1)} %get-tuple-element.13), kind=kOutput, calls=%fused_computation.51 | convolution fusion | flops 1958846464 | bytes 9986048 | tf_op jit(solution)/shard_map/dot_general | solution.py:88
  124.4 3.4 %fusion.42 = bf16[256,1024]{1,0:T(8,128)(2,1)S(1)} fusion(bf16[128,3696]{0,1:T(8,128)(2,1)S(1)} %collective-permute-done.6, bf16[128,3696]{0,1:T(8,128)(2,1)} %collective-permute-done.5, bf16[1848,1024]{1,0:T(8,128)(2,1)S(1)} %get-tuple-element.14, bf16[1848,1024]{1,0:T(8,128)(2,1)S(1)} %get-tuple-element.13), kind=kOutput, calls=%fused_computation.52 | convolution fusion | flops 1956954112 | bytes 9986048 | tf_op jit(solution)/shard_map/dot_general | solution.py:88
  128.4 2.8 %collective-permute-done.15 = bf16[256,1024]{1,0:T(8,128)(2,1)S(1)} collective-permute-done((bf16[256,1024]{1,0:T(8,128)(2,1)}, bf16[256,1024]{1,0:T(8,128)(2,1)S(1)}, u32[]{:S(2)}, u32[]{:S(2)}) %collective-permute-start.15) | collective-permute-done | bytes 524320 | tf_op jit(solution)/shard_map/ppermute | solution.py:10
  131.2 6.7 %collective-permute-done.11 = bf16[256,1024]{1,0:T(8,128)(2,1)S(1)} collective-permute-done((bf16[256,1024]{1,0:T(8,128)(2,1)}, bf16[256,1024]{1,0:T(8,128)(2,1)S(1)}, u32[]{:S(2)}, u32[]{:S(2)}) %collective-permute-start.11) | collective-permute-done | bytes 524320 | tf_op jit(solution)/shard_map/ppermute | solution.py:10
  138.2 9.7 %collective-permute-done.7 = bf16[256,1024]{1,0:T(8,128)(2,1)S(1)} collective-permute-done((bf16[256,1024]{1,0:T(8,128)(2,1)S(1)}, bf16[256,1024]{1,0:T(8,128)(2,1)S(1)}, u32[]{:S(2)}, u32[]{:S(2)}) %collective-permute-start.7) | collective-permute-done | bytes 524320 | tf_op jit(solution)/shard_map/ppermute | solution.py:10
  148.2 4.7 %fusion.45 = bf16[256,1024]{1,0:T(8,128)(2,1)} fusion(bf16[4,256,3696]{1,2,0:T(8,128)(2,1)} %copy-done, s32[]{:T(128)S(6)} %select_n.120, f32[128,1024]{1,0:T(8,128)S(1)} %get-tuple-element.31, f32[128,1024]{1,0:T(8,128)S(1)} %get-tuple-element.30, f32[64,1024]{1,0:T(8,128)S(1)} %get-tuple-element.29, f32[64,1024]{1,0:T(8,128)S(1)} %get-tuple-element.28, ...), kind=kOutput, calls=%fused_computation.53 | convolution fusion | flops 1955266560 | bytes 13131780 | tf_op jit(solution)/shard_map/dot_general | solution.py:88
  (54 shorter events, 19.0 us)
Async XLA Ops:
  1.8 14.2 %collective-permute-start = (bf16[128,1024]{1,0:T(8,128)(2,1)S(1)}, bf16[128,1024]{1,0:T(8,128)(2,1)S(1)}, u32[]{:S(2)}, u32[]{:S(2)}) collective-permute-start(bf16[128,1024]{1,0:T(8,128)(2,1)S(1)} %get-tuple-element.23), channel_id=1, source_target_pairs={{0,1},{1,0},{2,3},{3,2},{4,5},{5,4},{6,7},{7,6},{8,9},{9,8},{10,11... | collective-permute-start | bytes 786440 | tf_op jit(solution)/shard_map/ppermute | solution.py:10
  4.9 21.4 %collective-permute-start.1 = (bf16[128,1024]{1,0:T(8,128)(2,1)S(1)}, bf16[128,1024]{1,0:T(8,128)(2,1)S(1)}, u32[]{:S(2)}, u32[]{:S(2)}) collective-permute-start(bf16[128,1024]{1,0:T(8,128)(2,1)S(1)} %get-tuple-element.25), channel_id=1, source_target_pairs={{0,2},{1,3},{2,0},{3,1},{4,6},{5,7},{6,4},{7,5},{8,10},{9,11},{10,... | collective-permute-start | bytes 786440 | tf_op jit(solution)/shard_map/ppermute | solution.py:10
  7.5 18.8 %collective-permute-start.2 = (bf16[128,1024]{1,0:T(8,128)(2,1)S(1)}, bf16[128,1024]{1,0:T(8,128)(2,1)S(1)}, u32[]{:S(2)}, u32[]{:S(2)}) collective-permute-start(bf16[128,1024]{1,0:T(8,128)(2,1)S(1)} %get-tuple-element.24), channel_id=1, source_target_pairs={{0,3},{1,2},{2,1},{3,0},{4,7},{5,6},{6,5},{7,4},{8,11},{9,10},{10,... | collective-permute-start | bytes 786440 | tf_op jit(solution)/shard_map/ppermute | solution.py:10
  26.4 2.4 %collective-permute-start.3 = (bf16[3,128,1024]{2,1,0:T(8,128)(2,1)S(1)}, bf16[3,128,1024]{2,1,0:T(8,128)(2,1)S(1)}, u32[]{:S(2)}, u32[]{:S(2)}) collective-permute-start(bf16[3,128,1024]{2,1,0:T(8,128)(2,1)S(1)} %pad_maximum_fusion.2), channel_id=1, source_target_pairs={{0,4},{4,0},{8,12},{12,8},{16,20},{20,16},{24,28},{28,24},{1,5},{5... | collective-permute-start | bytes 2359304 | tf_op jit(solution)/shard_map/ppermute | solution.py:10
  30.4 20.8 %slice-start = ((s8[7569408]{0:T(1024)(128)(4,1)}), s8[4194304]{0:T(1024)(128)(4,1)S(1)}, s32[]{:S(2)}) async-start(s8[7569408]{0:T(1024)(128)(4,1)} %bitcast.47), calls=%async_computation | async-start | bytes 8388608
  30.4 20.8 %slice-start.1 = ((s8[7569408]{0:T(1024)(128)(4,1)}), s8[3375104]{0:T(1024)(128)(4,1)S(1)}, s32[]{:S(2)}) async-start(s8[7569408]{0:T(1024)(128)(4,1)} %bitcast.47), calls=%async_computation.1 | async-start | bytes 6750208
  51.0 48.4 %collective-permute-start.4 = (bf16[1848,1024]{1,0:T(8,128)(2,1)}, bf16[1848,1024]{1,0:T(8,128)(2,1)}, u32[]{:S(2)}, u32[]{:S(2)}) collective-permute-start(bf16[1848,1024]{1,0:T(8,128)(2,1)} %get-tuple-element.4), channel_id=1, source_target_pairs={{0,4},{4,0},{8,12},{12,8},{16,20},{20,16},{24,28},{28,24},{1,5},{5... | collective-permute-start | bytes 11354120 | tf_op jit(solution)/shard_map/ppermute | solution.py:10
  53.3 3.0 %copy-start = (bf16[4,256,3696]{1,2,0:T(8,128)(2,1)}, bf16[4,256,3696]{1,2,0:T(8,128)(2,1)S(1)}, u32[]{:S(2)}) copy-start(bf16[4,256,3696]{1,2,0:T(8,128)(2,1)S(1)} %pad_maximum_fusion) | copy-start | bytes 22708228
  57.3 13.2 %collective-permute-start.13 = (bf16[64,3696]{1,0:T(8,128)(2,1)S(1)}, bf16[64,3696]{1,0:T(8,128)(2,1)S(1)}, u32[]{:S(2)}, u32[]{:S(2)}) collective-permute-start(bf16[64,3696]{1,0:T(8,128)(2,1)S(1)} %bitcast.56), channel_id=1, source_target_pairs={{0,16},{4,20},{8,24},{12,28},{16,0},{20,4},{24,8},{28,12},{1,17},{... | collective-permute-start | bytes 1419272 | tf_op jit(solution)/shard_map/ppermute | solution.py:10
  59.2 16.0 %collective-permute-start.9 = (bf16[64,3696]{1,0:T(8,128)(2,1)S(1)}, bf16[64,3696]{1,0:T(8,128)(2,1)S(1)}, u32[]{:S(2)}, u32[]{:S(2)}) collective-permute-start(bf16[64,3696]{1,0:T(8,128)(2,1)S(1)} %bitcast.55), channel_id=1, source_target_pairs={{0,8},{4,12},{8,0},{12,4},{16,24},{20,28},{24,16},{28,20},{1,9},{5... | collective-permute-start | bytes 1419272 | tf_op jit(solution)/shard_map/ppermute | solution.py:10
  64.2 33.4 %collective-permute-start.5 = (bf16[128,3696]{0,1:T(8,128)(2,1)}, bf16[128,3696]{0,1:T(8,128)(2,1)}, u32[]{:S(2)}, u32[]{:S(2)}) collective-permute-start(bf16[128,3696]{0,1:T(8,128)(2,1)} %get-tuple-element.10), channel_id=1, source_target_pairs={{0,24},{4,28},{8,16},{12,20},{16,8},{20,12},{24,0},{28,4},{1,25},{... | collective-permute-start | bytes 2838536 | tf_op jit(solution)/shard_map/ppermute | solution.py:10
  70.5 16.5 %collective-permute-start.14 = (bf16[64,3696]{1,0:T(8,128)(2,1)S(1)}, bf16[64,3696]{1,0:T(8,128)(2,1)S(1)}, u32[]{:S(2)}, u32[]{:S(2)}) collective-permute-start(bf16[64,3696]{1,0:T(8,128)(2,1)S(1)} %collective-permute-done.13), channel_id=1, source_target_pairs={{0,1},{1,0},{2,3},{3,2},{4,5},{5,4},{6,7},{7,6},{8,9},{9,8},{10,11... | collective-permute-start | bytes 1419272 | tf_op jit(solution)/shard_map/ppermute | solution.py:10
  75.2 20.9 %collective-permute-start.10 = (bf16[64,3696]{1,0:T(8,128)(2,1)S(1)}, bf16[64,3696]{1,0:T(8,128)(2,1)}, u32[]{:S(2)}, u32[]{:S(2)}) collective-permute-start(bf16[64,3696]{1,0:T(8,128)(2,1)S(1)} %collective-permute-done.9), channel_id=1, source_target_pairs={{0,1},{1,0},{2,3},{3,2},{4,5},{5,4},{6,7},{7,6},{8,9},{9,8},{10,11... | collective-permute-start | bytes 1419272 | tf_op jit(solution)/shard_map/ppermute | solution.py:10
  77.8 35.0 %collective-permute-start.12 = (bf16[128,3696]{0,1:T(8,128)(2,1)}, bf16[128,3696]{0,1:T(8,128)(2,1)}, u32[]{:S(2)}, u32[]{:S(2)}) collective-permute-start(bf16[128,3696]{0,1:T(8,128)(2,1)} %get-tuple-element.8), channel_id=1, source_target_pairs={{0,16},{4,20},{8,24},{12,28},{16,0},{20,4},{24,8},{28,12},{1,17},{... | collective-permute-start | bytes 2838536 | tf_op jit(solution)/shard_map/ppermute | solution.py:10
  87.0 31.6 %collective-permute-start.8 = (bf16[128,3696]{0,1:T(8,128)(2,1)}, bf16[128,3696]{0,1:T(8,128)(2,1)}, u32[]{:S(2)}, u32[]{:S(2)}) collective-permute-start(bf16[128,3696]{0,1:T(8,128)(2,1)} %get-tuple-element.9), channel_id=1, source_target_pairs={{0,8},{4,12},{8,0},{12,4},{16,24},{20,28},{24,16},{28,20},{1,9},{5... | collective-permute-start | bytes 2838536 | tf_op jit(solution)/shard_map/ppermute | solution.py:10
  97.6 15.2 %copy-start.5 = (bf16[64,3696]{0,1:T(8,128)(2,1)S(1)}, bf16[64,3696]{0,1:T(8,128)(2,1)}, u32[]{:S(2)}) copy-start(bf16[64,3696]{0,1:T(8,128)(2,1)} %copy.15) | copy-start | bytes 1419268
  97.6 26.8 %collective-permute-start.6 = (bf16[128,3696]{0,1:T(8,128)(2,1)}, bf16[128,3696]{0,1:T(8,128)(2,1)S(1)}, u32[]{:S(2)}, u32[]{:S(2)}) collective-permute-start(bf16[128,3696]{0,1:T(8,128)(2,1)} %collective-permute-done.5), channel_id=1, source_target_pairs={{0,1},{1,0},{2,3},{3,2},{4,5},{5,4},{6,7},{7,6},{8,9},{9,8},{10,11... | collective-permute-start | bytes 2838536 | tf_op jit(solution)/shard_map/ppermute | solution.py:10
  103.1 21.2 %copy-start.1 = (bf16[1848,1024]{1,0:T(8,128)(2,1)}, bf16[1848,1024]{1,0:T(8,128)(2,1)S(1)}, u32[]{:S(2)}) copy-start(bf16[1848,1024]{1,0:T(8,128)(2,1)S(1)} %get-tuple-element.13) | copy-start | bytes 11354116
  103.2 21.2 %copy-start.3 = (bf16[1848,1024]{1,0:T(8,128)(2,1)}, bf16[1848,1024]{1,0:T(8,128)(2,1)S(1)}, u32[]{:S(2)}) copy-start(bf16[1848,1024]{1,0:T(8,128)(2,1)S(1)} %get-tuple-element.14) | copy-start | bytes 11354116
  117.1 14.1 %collective-permute-start.15 = (bf16[256,1024]{1,0:T(8,128)(2,1)}, bf16[256,1024]{1,0:T(8,128)(2,1)S(1)}, u32[]{:S(2)}, u32[]{:S(2)}) collective-permute-start(bf16[256,1024]{1,0:T(8,128)(2,1)} %fusion.36), channel_id=1, source_target_pairs={{0,16},{4,20},{8,24},{12,28},{16,0},{20,4},{24,8},{28,12},{1,17},{... | collective-permute-start | bytes 1572872 | tf_op jit(solution)/shard_map/ppermute | solution.py:10
  122.9 15.0 %collective-permute-start.11 = (bf16[256,1024]{1,0:T(8,128)(2,1)}, bf16[256,1024]{1,0:T(8,128)(2,1)S(1)}, u32[]{:S(2)}, u32[]{:S(2)}) collective-permute-start(bf16[256,1024]{1,0:T(8,128)(2,1)} %fusion.39), channel_id=1, source_target_pairs={{0,8},{4,12},{8,0},{12,4},{16,24},{20,28},{24,16},{28,20},{1,9},{5... | collective-permute-start | bytes 1572872 | tf_op jit(solution)/shard_map/ppermute | solution.py:10
  127.8 20.0 %collective-permute-start.7 = (bf16[256,1024]{1,0:T(8,128)(2,1)S(1)}, bf16[256,1024]{1,0:T(8,128)(2,1)S(1)}, u32[]{:S(2)}, u32[]{:S(2)}) collective-permute-start(bf16[256,1024]{1,0:T(8,128)(2,1)S(1)} %fusion.42), channel_id=1, source_target_pairs={{0,24},{4,28},{8,16},{12,20},{16,8},{20,12},{24,0},{28,4},{1,25},{... | collective-permute-start | bytes 1572872 | tf_op jit(solution)/shard_map/ppermute | solution.py:10
  138.0 10.1 %copy-start.2 = (bf16[1848,1024]{1,0:T(8,128)(2,1)S(1)}, bf16[1848,1024]{1,0:T(8,128)(2,1)}, u32[]{:S(2)}) copy-start(bf16[1848,1024]{1,0:T(8,128)(2,1)} %copy-done.1) | copy-start | bytes 11354116
  138.1 10.1 %copy-start.4 = (bf16[1848,1024]{1,0:T(8,128)(2,1)S(1)}, bf16[1848,1024]{1,0:T(8,128)(2,1)}, u32[]{:S(2)}) copy-start(bf16[1848,1024]{1,0:T(8,128)(2,1)} %copy-done.3) | copy-start | bytes 11354116

commit v2 on v0

v2 whole, which is shorter than its diff:
```python
import functools
import math

import jax
import jax.numpy as jnp
from jax import lax
from jax.experimental import pallas as pl
from jax.experimental.pallas import tpu as pltpu
from jax.sharding import PartitionSpec as P

OVER_FIRST = (((0,), (0,)), ((), ()))


def xor_permute(array, axis, size, mask):
    return lax.ppermute(array, axis, [(i, i ^ mask) for i in range(size)])


def adam_kernel(planes, scale, waits, place_ref, hidden_ref, own_ref, fetched_ref, swapped_ref, *refs):
    master_ref, first_ref, second_ref = refs[:3]
    new_master_ref, new_first_ref, new_second_ref, weights_ref, columns_ref = refs[3 + waits :]
    tokens = own_ref.shape[0]
    half = tokens // 2

    @pl.when(pl.program_id(0) == 0)
    def _():
        plane, core = place_ref[0], place_ref[1]
        columns_ref[pl.ds(pl.multiple_of(plane * tokens, tokens), tokens), :] = own_ref[...]
        for mask in range(1, planes):
            start = (plane ^ mask) * tokens
            mine = pl.multiple_of(start + core * half, half)
            other = pl.multiple_of(start + (1 - core) * half, half)
            columns_ref[pl.ds(mine, half), :] = fetched_ref[mask - 1]
            columns_ref[pl.ds(other, half), :] = swapped_ref[mask - 1]

    grad = jnp.dot(hidden_ref[...], columns_ref[...], preferred_element_type=jnp.float32)
    grad = grad * scale
    new_first = 0.9 * first_ref[...] + 0.1 * grad
    new_second = 0.95 * second_ref[...] + 0.05 * grad * grad
    new_master = master_ref[...] - 0.002 * new_first / (jnp.sqrt(new_second) + 1e-08)
    new_master_ref[...] = new_master
    new_first_ref[...] = new_first
    new_second_ref[...] = new_second
    weights_ref[...] = new_master.astype(jnp.bfloat16)


def adam(place, planes, hidden, out_grad, fetched, swapped, state, step, blocks, before, after):
    rows, tokens_all = hidden.shape
    width = state[0].shape[1]
    tokens = tokens_all // planes
    start, stop = blocks
    block = pl.BlockSpec((step, width), lambda i, s: (i + start, 0))
    whole = pl.BlockSpec(fetched.shape, lambda i, s: (0, 0, 0))
    full = jax.ShapeDtypeStruct((rows, width), jnp.float32)
    waits = len(before) + len(after)
    size = (stop - start) * step * width
    return pl.pallas_call(
        functools.partial(adam_kernel, planes, 1.0 / math.sqrt(tokens_all), waits),
        out_shape=[full] * 3 + [jax.ShapeDtypeStruct((rows, width), jnp.bfloat16)],
        grid_spec=pltpu.PrefetchScalarGridSpec(
            num_scalar_prefetch=1,
            grid=(stop - start,),
            in_specs=[
                pl.BlockSpec((step, tokens_all), lambda i, s: (i + start, 0)),
                pl.BlockSpec((tokens, width), lambda i, s: (0, s[0])),
                whole,
                whole,
                block,
                block,
                block,
            ]
            + [pl.BlockSpec(memory_space=pl.ANY)] * waits,
            out_specs=[block] * 4,
            scratch_shapes=[pltpu.VMEM((tokens_all, width), jnp.bfloat16)],
        ),
        input_output_aliases={8 + i: i for i in range(len(before))},
        compiler_params=pltpu.CompilerParams(vmem_limit_bytes=40 * 1024 * 1024),
        cost_estimate=pl.CostEstimate(
            flops=2 * size * tokens_all, bytes_accessed=28 * size, transcendentals=2 * size
        ),
    )(place, hidden, out_grad, fetched, swapped, *state, *before, *after)


def per_device(train_hidden, out_grad, master, first_moment, second_moment, decode_hidden):
    devices, planes = lax.axis_size("replica"), lax.axis_size("tensor")
    chips = devices // 2
    plane, device = lax.axis_index("tensor"), lax.axis_index("replica")
    chip, core = lax.div(device, 2), lax.rem(device, 2)
    parity = lax.rem(plane, 2)
    even = parity == 0
    tokens, width = out_grad.shape[0], out_grad.shape[1] // planes
    rows, hidden = decode_hidden.shape
    block = hidden // devices
    cut = block // 2 // 8 * 8

    pieces = []
    for mask in range(1, planes):
        part = lax.dynamic_slice(
            out_grad,
            (core * (tokens // 2), (plane ^ mask) * width),
            (tokens // 2, width),
        )
        pieces.append(xor_permute(part, "tensor", planes, mask))

    windows = decode_hidden.T.reshape(chips, 2, block, rows)

    def part(mask, to_core, low, high):
        return lax.dynamic_slice(
            windows, (chip ^ mask, to_core, low, 0), (1, 1, high - low, rows)
        ).reshape(high - low, rows)

    def to_peer(array, mask, cross):
        return xor_permute(array, "replica", devices, 2 * mask + cross)

    def to_peer_by_plane(array, mask):
        pairs = [
            (r * planes + z, (r ^ (2 * mask + z % 2)) * planes + z)
            for r in range(devices)
            for z in range(planes)
        ]
        return lax.ppermute(array, ("replica", "tensor"), pairs)

    order = sorted(range(1, chips), key=lambda m: -m.bit_count())
    far = [mask for mask in order if mask.bit_count() > 1]
    near = [mask for mask in order if mask.bit_count() == 1]
    shared, straight = {}, {}
    for mask in far:
        shared[mask] = to_peer_by_plane(part(mask, core ^ parity, 0, block), mask)
    for mask in near:
        shared[mask] = to_peer_by_plane(part(mask, core ^ parity, 0, cut), mask)
    for mask in near:
        straight[mask] = [
            to_peer(part(mask, core, cut, block), mask, 0),
            to_peer(part(mask, 1 - core, cut, block), mask, 1),
        ]
    passed = {mask: xor_permute(shared[mask], "tensor", planes, 1) for mask in order}
    beside = xor_permute(part(0, 1 - core, 0, block), "replica", devices, 1)

    fetched = jnp.stack(pieces)
    swapped = xor_permute(fetched, "replica", devices, 1)
    place = jnp.stack([plane, core]).astype(jnp.int32)
    state = (master, first_moment, second_moment)
    step = 320 if master.shape[0] > 320 else master.shape[0]
    blocks = pl.cdiv(master.shape[0], step)
    middle = (blocks + 1) // 2
    common = (place, planes, train_hidden.T, out_grad, fetched, swapped, state, step)
    out = adam(*common, (0, middle), (), [shared[mask] for mask in far])
    if middle < blocks:
        out = adam(*common, (middle, blocks), out, [shared[mask] for mask in near])
    new_master, new_first, new_second, weights = out

    def times_weights(held):
        return lax.dot_general(held, weights, OVER_FIRST, preferred_element_type=jnp.float32)

    def partial(mask):
        if mask == 0:
            keep, give = [part(0, core, 0, block)], [beside]
        else:
            keep = [jnp.where(even, shared[mask], passed[mask])]
            give = [jnp.where(even, passed[mask], shared[mask])]
        if mask in straight:
            keep.append(straight[mask][0])
            give.append(straight[mask][1])
        given = times_weights(jnp.concatenate(give, axis=0))
        kept = times_weights(jnp.concatenate(keep, axis=0))
        return kept + xor_permute(given, "replica", devices, 1)

    total = partial(0)
    for mask in order:
        sums = partial(mask).astype(jnp.bfloat16)
        total = total + to_peer(sums, mask, 0).astype(jnp.float32)
    return (new_master, new_first, new_second, total.astype(jnp.bfloat16))


def solution(mesh):
    placed = (
        P(None, "replica"),
        P("tensor", None),
        P("replica", "tensor"),
        P("replica", "tensor"),
        P("replica", "tensor"),
        P("replica", None),
    )
    return jax.shard_map(
        per_device,
        mesh=mesh,
        in_specs=placed,
        out_specs=(
            P("replica", "tensor"),
            P("replica", "tensor"),
            P("replica", "tensor"),
            P("replica", "tensor"),
        ),
        check_vma=False,
    )
```

time: 259 us -> 120 us (0.46)
  waiting for transfers between devices: 146 us -> 36.1 us
  blocking collectives: 54.5 us -> 0 us
  starting transfers between devices: 0.04 us -> 28.8 us
  Pallas kernels: 0 us -> 25.1 us
  matrix products: 36.4 us -> 14.9 us
  between operations: 14 us -> 0.8 us
  local copies, waits for them, and re-layouts: 7.56 us -> 10.8 us
    all_gather x1 -> x0, waiting for transfers between devices: 146 us -> none  [per_device(): lax.all_gather(weights, 'replica', axis=0, tiled=True)]
    all_to_all x1 -> x0, blocking collectives: 54.5 us -> none  [per_device(): lax.all_to_all(out_grad, 'tensor', split_axis=1, concat_axis=0, tiled=True)]
    ppermute x0 -> x22, waiting for transfers between devices: none -> 36.1 us  [the longest x19 32.5 us: xor_permute(): return lax.ppermute(array, axis, [(i, i ^ mask) for i in range(size)])]
    ppermute x0 -> x22, starting transfers between devices: none -> 28.8 us  [the longest x19 21.9 us: xor_permute(): return lax.ppermute(array, axis, [(i, i ^ mask) for i in range(size)])]
    pallas_call x0 -> x2, Pallas kernels: none -> 25.1 us  [adam(): pl.pallas_call(functools.partial(adam_kernel, planes, 1.0 / math.sqrt(tok...]
    dot_general x2 -> x8, matrix products: 36.4 us -> 14.9 us  [times_weights(): lax.dot_general(held, weights, OVER_FIRST, preferred_element_type=jnp.flo...]
    reshape x0 -> x3, local copies, waits for them, and re-layouts: none -> 7.57 us  [part(): return lax.dynamic_slice(windows, (chip ^ mask, to_core, low, 0), (1, 1,...]
    unnamed x2 -> x6, local copies, waits for them, and re-layouts: 5.08 us -> 2.08 us
  transfers between devices with their start and end apart: 1 -> 22, of which waited for: 1 -> 5; matrix products, arithmetic and copies ran while one was open for 0% -> 17% of each run, Pallas kernels for 0% -> 21%
where the time goes in v2:
time: 120 us; the launch traced here: 119 us
  waiting for transfers between devices  36.1 us (30%)
  starting transfers between devices  28.8 us (24%)
  Pallas kernels  25.1 us (21%)
  matrix products  14.9 us (12%)
  local copies, waits for them, and re-layouts  10.8 us (9%)
  other arithmetic  2.48 us (2%)
    ppermute x19, waiting for transfers between devices, xor_permute(): return lax.ppermute(array, axis, [(i, i ^ mask) for i in range(size)])  32.5 us
    pallas_call x2, Pallas kernels, adam(): pl.pallas_call(functools.partial(adam_kernel, planes, 1.0 / math.sqrt(tok...  25.1 us
    ppermute x19, starting transfers between devices, xor_permute(): return lax.ppermute(array, axis, [(i, i ^ mask) for i in range(size)])  21.9 us
    dot_general x8, matrix products, times_weights(): lax.dot_general(held, weights, OVER_FIRST, preferred_element_type=jnp.flo...  14.9 us
    reshape x3, local copies, waits for them, and re-layouts, part(): return lax.dynamic_slice(windows, (chip ^ mask, to_core, low, 0), (1, 1,...  7.57 us
    ppermute x3, starting transfers between devices, to_peer_by_plane(): return lax.ppermute(array, ('replica', 'tensor'), pairs)  6.93 us
    ppermute x3, waiting for transfers between devices, to_peer_by_plane(): return lax.ppermute(array, ('replica', 'tensor'), pairs)  3.65 us
  transfers between devices with their start and end apart: 22, of which 5 were waited for; matrix products, arithmetic and copies ran while one was open for 17% of the time, Pallas kernels for 21%

profile of v2, /device:TPU:0, one launch (start us, length us, event | category | flops | bytes accessed | tf_op | source)
XLA Modules:
  0.0 119.0 jit_solution(13366117302487039342)
XLA Ops:
  0.7 2.0 %dynamic-slice_bitcast_fusion.6 = (bf16[920,256]{1,0:T(8,128)(2,1)}, bf16[920,256]{1,0:T(8,128)(2,1)S(1)}) fusion(bf16[4,2,1848,256]{3,2,1,0:T(8,128)(2,1)} %bitcast.39, s32[]{:T(128)S(6)} %select_n.85, s32[]{:T(128)S(6)} %select_n.83, s32[]{:T(128)S(6)} %select_n.84), kind=kLoop, calls=%fused_computation.39 | loop fusion | bytes 1884172 | tf_op jit(solution)/shard_map/reshape | solution.py:109
  2.7 2.9 %collective-permute-start.5 = (bf16[920,256]{1,0:T(8,128)(2,1)S(1)}, bf16[920,256]{1,0:T(8,128)(2,1)S(1)}, u32[]{:S(2)}, u32[]{:S(2)}) collective-permute-start(bf16[920,256]{1,0:T(8,128)(2,1)S(1)} %get-tuple-element.27), channel_id=1, source_target_pairs={{0,8},{1,13},{2,10},{3,15},{4,12},{5,9},{6,14},{7,11},{8,0},{9,5},... | collective-permute-start | bytes 1413128 | tf_op jit(solution)/shard_map/ppermute | solution.py:120
  5.6 1.5 %collective-permute-start.6 = (bf16[920,256]{1,0:T(8,128)(2,1)}, bf16[920,256]{1,0:T(8,128)(2,1)}, u32[]{:S(2)}, u32[]{:S(2)}) collective-permute-start(bf16[920,256]{1,0:T(8,128)(2,1)} %get-tuple-element.26), channel_id=1, source_target_pairs={{0,16},{1,21},{2,18},{3,23},{4,20},{5,17},{6,22},{7,19},{8,24},{9,... | collective-permute-start | bytes 1413128 | tf_op jit(solution)/shard_map/ppermute | solution.py:120
  9.6 2.6 %collective-permute-start.1 = (bf16[128,1024]{1,0:T(8,128)(2,1)S(1)}, bf16[128,1024]{1,0:T(8,128)(2,1)S(1)}, u32[]{:S(2)}, u32[]{:S(2)}) collective-permute-start(bf16[128,1024]{1,0:T(8,128)(2,1)S(1)} %get-tuple-element.30), channel_id=1, source_target_pairs={{0,2},{1,3},{2,0},{3,1},{4,6},{5,7},{6,4},{7,5},{8,10},{9,11},{10,... | collective-permute-start | bytes 786440 | tf_op jit(solution)/shard_map/ppermute | solution.py:15
  12.7 3.6 %collective-permute-done.5.refs_7_ = bf16[920,256]{1,0:T(8,128)(2,1)S(1)} collective-permute-done((bf16[920,256]{1,0:T(8,128)(2,1)S(1)}, bf16[920,256]{1,0:T(8,128)(2,1)S(1)}, u32[]{:S(2)}, u32[]{:S(2)}) %collective-permute-start.5) | collective-permute-done | bytes 471072 | tf_op jit(solution)/shard_map/ppermute | solution.py:120
  16.4 2.3 %collective-permute-start.12 = (bf16[920,256]{1,0:T(8,128)(2,1)S(1)}, bf16[920,256]{1,0:T(8,128)(2,1)}, u32[]{:S(2)}, u32[]{:S(2)}) collective-permute-start(bf16[920,256]{1,0:T(8,128)(2,1)S(1)} %collective-permute-done.5.refs_7_), channel_id=1, source_target_pairs={{0,1},{1,0},{2,3},{3,2},{4,5},{5,4},{6,7},{7,6},{8,9},{9,8},{10,11... | collective-permute-start | bytes 1413128 | tf_op jit(solution)/shard_map/ppermute | solution.py:15
  18.7 2.8 %dynamic-slice_bitcast_fusion = (bf16[1848,256]{1,0:T(8,128)(2,1)}, bf16[1848,256]{1,0:T(8,128)(2,1)}) fusion(bf16[4,2,1848,256]{3,2,1,0:T(8,128)(2,1)} %bitcast.40, s32[]{:T(128)S(6)} %select_n.86, s32[]{:T(128)S(6)} %select_n.88, s32[]{:T(128)S(6)} %select_n.82, s32[]{:T(128)S(6)} %select_n.83), kind=kLoop, calls=%fused_computation.29 | loop fusion | bytes 3784720 | tf_op jit(solution)/shard_map/reshape | solution.py:109
  21.6 2.5 %collective-permute-start.4 = (bf16[1848,256]{1,0:T(8,128)(2,1)}, bf16[1848,256]{1,0:T(8,128)(2,1)}, u32[]{:S(2)}, u32[]{:S(2)}) collective-permute-start(bf16[1848,256]{1,0:T(8,128)(2,1)} %get-tuple-element.25), channel_id=1, source_target_pairs={{0,24},{1,29},{2,26},{3,31},{4,28},{5,25},{6,30},{7,27},{8,16},{9,... | collective-permute-start | bytes 2838536 | tf_op jit(solution)/shard_map/ppermute | solution.py:120
  24.0 7.0 %collective-permute-done.1 = bf16[128,1024]{1,0:T(8,128)(2,1)S(1)} collective-permute-done((bf16[128,1024]{1,0:T(8,128)(2,1)S(1)}, bf16[128,1024]{1,0:T(8,128)(2,1)S(1)}, u32[]{:S(2)}, u32[]{:S(2)}) %collective-permute-start.1) | collective-permute-done | bytes 262176 | tf_op jit(solution)/shard_map/ppermute | solution.py:15
  31.3 4.8 %collective-permute-start.17 = (bf16[920,256]{1,0:T(8,128)(2,1)}, bf16[920,256]{1,0:T(8,128)(2,1)}, u32[]{:S(2)}, u32[]{:S(2)}) collective-permute-start(bf16[920,256]{1,0:T(8,128)(2,1)} %collective-permute-done.6.refs_8_), channel_id=1, source_target_pairs={{0,1},{1,0},{2,3},{3,2},{4,5},{5,4},{6,7},{7,6},{8,9},{9,8},{10,11... | collective-permute-start | bytes 1413128 | tf_op jit(solution)/shard_map/ppermute | solution.py:15
  36.1 2.7 %dynamic-slice_bitcast_fusion.5 = (bf16[928,256]{1,0:T(8,128)(2,1)}, bf16[928,256]{1,0:T(8,128)(2,1)}, bf16[928,256]{1,0:T(8,128)(2,1)}, bf16[928,256]{1,0:T(8,128)(2,1)}) fusion(bf16[4,2,1848,256]{3,2,1,0:T(8,128)(2,1)} %bitcast.41, s32[]{:T(128)S(6)} %select_n.84, s32[]{:T(128)S(6)} %select_n.87, s32[]{:T(128)S(6)} %select_n.85, s32[]{:T(128)S(6)} %select_n.88), kind=kLoop, calls=%fused_computation.38 | loop fusion | bytes 3801104 | tf_op jit(solution)/shard_map/reshape | solution.py:109
  39.2 1.5 %collective-permute-start.13 = (bf16[928,256]{1,0:T(8,128)(2,1)}, bf16[928,256]{1,0:T(8,128)(2,1)S(1)}, u32[]{:S(2)}, u32[]{:S(2)}) collective-permute-start(bf16[928,256]{1,0:T(8,128)(2,1)} %get-tuple-element.20), channel_id=1, source_target_pairs={{0,8},{4,12},{8,0},{12,4},{16,24},{20,28},{24,16},{28,20},{1,9},{5... | collective-permute-start | bytes 1425416 | tf_op jit(solution)/shard_map/ppermute | solution.py:15
  41.8 6.0 %collective-permute-done.17 = bf16[920,256]{1,0:T(8,128)(2,1)} collective-permute-done((bf16[920,256]{1,0:T(8,128)(2,1)}, bf16[920,256]{1,0:T(8,128)(2,1)}, u32[]{:S(2)}, u32[]{:S(2)}) %collective-permute-start.17) | collective-permute-done | bytes 471072 | tf_op jit(solution)/shard_map/ppermute | solution.py:15
  49.0 1.5 %collective-permute-start.18 = (bf16[928,256]{1,0:T(8,128)(2,1)}, bf16[928,256]{1,0:T(8,128)(2,1)S(1)}, u32[]{:S(2)}, u32[]{:S(2)}) collective-permute-start(bf16[928,256]{1,0:T(8,128)(2,1)} %get-tuple-element.22), channel_id=1, source_target_pairs={{0,16},{4,20},{8,24},{12,28},{16,0},{20,4},{24,8},{28,12},{1,17},{... | collective-permute-start | bytes 1425416 | tf_op jit(solution)/shard_map/ppermute | solution.py:15
  50.5 1.6 %collective-permute-start.9 = (bf16[1848,256]{1,0:T(8,128)(2,1)}, bf16[1848,256]{1,0:T(8,128)(2,1)S(1)}, u32[]{:S(2)}, u32[]{:S(2)}) collective-permute-start(bf16[1848,256]{1,0:T(8,128)(2,1)} %collective-permute-done.4.refs_3_), channel_id=1, source_target_pairs={{0,1},{1,0},{2,3},{3,2},{4,5},{5,4},{6,7},{7,6},{8,9},{9,8},{10,11... | collective-permute-start | bytes 2838536 | tf_op jit(solution)/shard_map/ppermute | solution.py:15
  52.1 2.1 %copy-done = bf16[1024,1848]{0,1:T(8,128)(2,1)S(1)} copy-done((bf16[1024,1848]{0,1:T(8,128)(2,1)S(1)}, bf16[1024,1848]{0,1:T(8,128)(2,1)}, u32[]{:S(2)}) %copy-start) | copy-done | bytes 3784728
  54.2 13.0 %shard_map.93 = (f32[1848,1024]{1,0:T(8,128)}, f32[1848,1024]{1,0:T(8,128)}, f32[1848,1024]{1,0:T(8,128)}, bf16[1848,1024]{1,0:T(8,128)(2,1)S(1)}) custom-call(s32[2]{0:T(128)S(1)} %pad_add_fusion.place_ref, bf16[1848,1024]{1,0:T(8,128)(2,1)S(1)} %bitcast.37, bf16[256,4096]{1,0:T(8,128)(2,1)S(1)} %copy-done.1, ...), custom_call_target="tpu_custom_call" | custom-call | flops 2013265920 | bytes 27525120 | tf_op jit(solution)/shard_map/pallas_call | solution.py:56
  67.2 12.0 %shard_map.94 = (f32[1848,1024]{1,0:T(8,128)}, f32[1848,1024]{1,0:T(8,128)}, f32[1848,1024]{1,0:T(8,128)}, bf16[1848,1024]{1,0:T(8,128)(2,1)S(1)}) custom-call(s32[2]{0:T(128)S(1)} %pad_add_fusion.place_ref, bf16[1848,1024]{1,0:T(8,128)(2,1)S(1)} %bitcast.38, ...), custom_call_target="tpu_custom_call", output_to_operand_aliasing={{0}: (8, {}), {1}: (9, {}), {2}: (10, {}), {3}: (11, {})} | custom-call | flops 2013265920 | bytes 27525120 | tf_op jit(solution)/shard_map/pallas_call | solution.py:56
  79.6 2.3 %fusion.10 = f32[256,1024]{1,0:T(8,128)S(1)} fusion(bf16[1848,1024]{1,0:T(8,128)(2,1)S(1)} %get-tuple-element.19, bf16[928,256]{1,0:T(8,128)(2,1)} %collective-permute-done.14, bf16[920,256]{1,0:T(8,128)(2,1)S(1)} %get-tuple-element.32), kind=kOutput, calls=%fused_computation.14 | convolution fusion | flops 970776576 | bytes 5779456 | tf_op jit(solution)/shard_map/dot_general | solution.py:152
  91.1 2.5 %fusion.3 = bf16[256,1024]{1,0:T(8,128)(2,1)S(1)} fusion(f32[256,1024]{1,0:T(8,128)S(1)} %collective-permute-done.10, bf16[1848,1024]{1,0:T(8,128)(2,1)S(1)} %get-tuple-element.19, bf16[1848,256]{1,0:T(8,128)(2,1)} %collective-permute-done.4.refs_3_, bf16[1848,256]{1,0:T(8,128)(2,1)S(1)} %collective-permute-done.9, pred[]{:T(512)S(6)} %eq.3), kind=kOutput, calls=%fused_computation.7 | convolution fusion | flops 969881600 | bytes 7249921 | tf_op jit(solution)/shard_map/dot_general | solution.py:152
  93.7 2.5 %collective-permute-start.11 = (bf16[256,1024]{1,0:T(8,128)(2,1)S(1)}, bf16[256,1024]{1,0:T(8,128)(2,1)S(1)}, u32[]{:S(2)}, u32[]{:S(2)}) collective-permute-start(bf16[256,1024]{1,0:T(8,128)(2,1)S(1)} %fusion.3), channel_id=1, source_target_pairs={{0,24},{4,28},{8,16},{12,20},{16,8},{20,12},{24,0},{28,4},{1,25},{... | collective-permute-start | bytes 1572872 | tf_op jit(solution)/shard_map/ppermute | solution.py:15
  96.2 7.3 %collective-permute-done.16 = bf16[256,1024]{1,0:T(8,128)(2,1)S(1)} collective-permute-done((bf16[256,1024]{1,0:T(8,128)(2,1)S(1)}, bf16[256,1024]{1,0:T(8,128)(2,1)S(1)}, u32[]{:S(2)}, u32[]{:S(2)}) %collective-permute-start.16) | collective-permute-done | bytes 524320 | tf_op jit(solution)/shard_map/ppermute | solution.py:15
  103.4 12.2 %collective-permute-done.21 = bf16[256,1024]{1,0:T(8,128)(2,1)S(1)} collective-permute-done((bf16[256,1024]{1,0:T(8,128)(2,1)S(1)}, bf16[256,1024]{1,0:T(8,128)(2,1)S(1)}, u32[]{:S(2)}, u32[]{:S(2)}) %collective-permute-start.21) | collective-permute-done | bytes 524320 | tf_op jit(solution)/shard_map/ppermute | solution.py:15
  115.6 3.4 %fusion.6 = bf16[256,1024]{1,0:T(8,128)(2,1)} fusion(f32[256,1024]{1,0:T(8,128)S(1)} %collective-permute-done.8, bf16[1848,1024]{1,0:T(8,128)(2,1)S(1)} %get-tuple-element.19, bf16[256,1024]{1,0:T(8,128)(2,1)S(1)} %collective-permute-done.21, bf16[256,1024]{1,0:T(8,128)(2,1)S(1)} %collective-permute-done.16, ...), kind=kOutput, calls=%fused_computation.10 | convolution fusion | flops 970981376 | bytes 7876616 | tf_op jit(solution)/shard_map/dot_general | solution.py:152
  (44 shorter events, 15.5 us)
Async XLA Ops:
  2.7 13.7 %collective-permute-start.5 = (bf16[920,256]{1,0:T(8,128)(2,1)S(1)}, bf16[920,256]{1,0:T(8,128)(2,1)S(1)}, u32[]{:S(2)}, u32[]{:S(2)}) collective-permute-start(bf16[920,256]{1,0:T(8,128)(2,1)S(1)} %get-tuple-element.27), channel_id=1, source_target_pairs={{0,8},{1,13},{2,10},{3,15},{4,12},{5,9},{6,14},{7,11},{8,0},{9,5},... | collective-permute-start | bytes 1413128 | tf_op jit(solution)/shard_map/ppermute | solution.py:120
  5.6 25.6 %collective-permute-start.6 = (bf16[920,256]{1,0:T(8,128)(2,1)}, bf16[920,256]{1,0:T(8,128)(2,1)}, u32[]{:S(2)}, u32[]{:S(2)}) collective-permute-start(bf16[920,256]{1,0:T(8,128)(2,1)} %get-tuple-element.26), channel_id=1, source_target_pairs={{0,16},{1,21},{2,18},{3,23},{4,20},{5,17},{6,22},{7,19},{8,24},{9,... | collective-permute-start | bytes 1413128 | tf_op jit(solution)/shard_map/ppermute | solution.py:120
  8.3 13.3 %collective-permute-start = (bf16[128,1024]{1,0:T(8,128)(2,1)S(1)}, bf16[128,1024]{1,0:T(8,128)(2,1)S(1)}, u32[]{:S(2)}, u32[]{:S(2)}) collective-permute-start(bf16[128,1024]{1,0:T(8,128)(2,1)S(1)} %get-tuple-element.28), channel_id=1, source_target_pairs={{0,1},{1,0},{2,3},{3,2},{4,5},{5,4},{6,7},{7,6},{8,9},{9,8},{10,11... | collective-permute-start | bytes 786440 | tf_op jit(solution)/shard_map/ppermute | solution.py:15
  9.6 21.4 %collective-permute-start.1 = (bf16[128,1024]{1,0:T(8,128)(2,1)S(1)}, bf16[128,1024]{1,0:T(8,128)(2,1)S(1)}, u32[]{:S(2)}, u32[]{:S(2)}) collective-permute-start(bf16[128,1024]{1,0:T(8,128)(2,1)S(1)} %get-tuple-element.30), channel_id=1, source_target_pairs={{0,2},{1,3},{2,0},{3,1},{4,6},{5,7},{6,4},{7,5},{8,10},{9,11},{10,... | collective-permute-start | bytes 786440 | tf_op jit(solution)/shard_map/ppermute | solution.py:15
  12.2 18.8 %collective-permute-start.2 = (bf16[128,1024]{1,0:T(8,128)(2,1)S(1)}, bf16[128,1024]{1,0:T(8,128)(2,1)S(1)}, u32[]{:S(2)}, u32[]{:S(2)}) collective-permute-start(bf16[128,1024]{1,0:T(8,128)(2,1)S(1)} %get-tuple-element.29), channel_id=1, source_target_pairs={{0,3},{1,2},{2,1},{3,0},{4,7},{5,6},{6,5},{7,4},{8,11},{9,10},{10,... | collective-permute-start | bytes 786440 | tf_op jit(solution)/shard_map/ppermute | solution.py:15
  16.4 22.8 %collective-permute-start.12 = (bf16[920,256]{1,0:T(8,128)(2,1)S(1)}, bf16[920,256]{1,0:T(8,128)(2,1)}, u32[]{:S(2)}, u32[]{:S(2)}) collective-permute-start(bf16[920,256]{1,0:T(8,128)(2,1)S(1)} %collective-permute-done.5.refs_7_), channel_id=1, source_target_pairs={{0,1},{1,0},{2,3},{3,2},{4,5},{5,4},{6,7},{7,6},{8,9},{9,8},{10,11... | collective-permute-start | bytes 1413128 | tf_op jit(solution)/shard_map/ppermute | solution.py:15
  21.6 27.4 %collective-permute-start.4 = (bf16[1848,256]{1,0:T(8,128)(2,1)}, bf16[1848,256]{1,0:T(8,128)(2,1)}, u32[]{:S(2)}, u32[]{:S(2)}) collective-permute-start(bf16[1848,256]{1,0:T(8,128)(2,1)} %get-tuple-element.25), channel_id=1, source_target_pairs={{0,24},{1,29},{2,26},{3,31},{4,28},{5,25},{6,30},{7,27},{8,16},{9,... | collective-permute-start | bytes 2838536 | tf_op jit(solution)/shard_map/ppermute | solution.py:120
  31.1 21.0 %copy-start.1 = (bf16[256,4096]{1,0:T(8,128)(2,1)S(1)}, bf16[256,4096]{1,0:T(8,128)(2,1)}, u32[]{:S(2)}) copy-start(bf16[256,4096]{1,0:T(8,128)(2,1)} %own_ref.3) | copy-start | bytes 6291460
  31.2 19.4 %collective-permute-start.3 = (bf16[3,128,1024]{2,1,0:T(8,128)(2,1)S(1)}, bf16[3,128,1024]{2,1,0:T(8,128)(2,1)}, u32[]{:S(2)}, u32[]{:S(2)}) collective-permute-start(bf16[3,128,1024]{2,1,0:T(8,128)(2,1)S(1)} %pad_maximum_fusion.fetched_ref), channel_id=1, source_target_pairs={{0,4},{4,0},{8,12},{12,8},{16,20},{20,16},{24,28},{28,24},{1,5},{5... | collective-permute-start | bytes 2359304 | tf_op jit(solution)/shard_map/ppermute | solution.py:15
  31.3 16.5 %collective-permute-start.17 = (bf16[920,256]{1,0:T(8,128)(2,1)}, bf16[920,256]{1,0:T(8,128)(2,1)}, u32[]{:S(2)}, u32[]{:S(2)}) collective-permute-start(bf16[920,256]{1,0:T(8,128)(2,1)} %collective-permute-done.6.refs_8_), channel_id=1, source_target_pairs={{0,1},{1,0},{2,3},{3,2},{4,5},{5,4},{6,7},{7,6},{8,9},{9,8},{10,11... | collective-permute-start | bytes 1413128 | tf_op jit(solution)/shard_map/ppermute | solution.py:15
  38.8 40.4 %collective-permute-start.14 = (bf16[928,256]{1,0:T(8,128)(2,1)}, bf16[928,256]{1,0:T(8,128)(2,1)}, u32[]{:S(2)}, u32[]{:S(2)}) collective-permute-start(bf16[928,256]{1,0:T(8,128)(2,1)} %get-tuple-element.23), channel_id=1, source_target_pairs={{0,12},{4,8},{8,4},{12,0},{16,28},{20,24},{24,20},{28,16},{1,13},{... | collective-permute-start | bytes 1425416 | tf_op jit(solution)/shard_map/ppermute | solution.py:15
  39.2 47.7 %collective-permute-start.13 = (bf16[928,256]{1,0:T(8,128)(2,1)}, bf16[928,256]{1,0:T(8,128)(2,1)S(1)}, u32[]{:S(2)}, u32[]{:S(2)}) collective-permute-start(bf16[928,256]{1,0:T(8,128)(2,1)} %get-tuple-element.20), channel_id=1, source_target_pairs={{0,8},{4,12},{8,0},{12,4},{16,24},{20,28},{24,16},{28,20},{1,9},{5... | collective-permute-start | bytes 1425416 | tf_op jit(solution)/shard_map/ppermute | solution.py:15
  47.8 34.2 %collective-permute-start.19 = (bf16[928,256]{1,0:T(8,128)(2,1)}, bf16[928,256]{1,0:T(8,128)(2,1)S(1)}, u32[]{:S(2)}, u32[]{:S(2)}) collective-permute-start(bf16[928,256]{1,0:T(8,128)(2,1)} %get-tuple-element.21), channel_id=1, source_target_pairs={{0,20},{4,16},{8,28},{12,24},{16,4},{20,0},{24,12},{28,8},{1,21},{... | collective-permute-start | bytes 1425416 | tf_op jit(solution)/shard_map/ppermute | solution.py:15
  49.0 40.2 %collective-permute-start.18 = (bf16[928,256]{1,0:T(8,128)(2,1)}, bf16[928,256]{1,0:T(8,128)(2,1)S(1)}, u32[]{:S(2)}, u32[]{:S(2)}) collective-permute-start(bf16[928,256]{1,0:T(8,128)(2,1)} %get-tuple-element.22), channel_id=1, source_target_pairs={{0,16},{4,20},{8,24},{12,28},{16,0},{20,4},{24,8},{28,12},{1,17},{... | collective-permute-start | bytes 1425416 | tf_op jit(solution)/shard_map/ppermute | solution.py:15
  50.5 33.0 %collective-permute-start.9 = (bf16[1848,256]{1,0:T(8,128)(2,1)}, bf16[1848,256]{1,0:T(8,128)(2,1)S(1)}, u32[]{:S(2)}, u32[]{:S(2)}) collective-permute-start(bf16[1848,256]{1,0:T(8,128)(2,1)} %collective-permute-done.4.refs_3_), channel_id=1, source_target_pairs={{0,1},{1,0},{2,3},{3,2},{4,5},{5,4},{6,7},{7,6},{8,9},{9,8},{10,11... | collective-permute-start | bytes 2838536 | tf_op jit(solution)/shard_map/ppermute | solution.py:15
  67.2 12.1 %copy-start.2 = (bf16[1848,256]{1,0:T(8,128)(2,1)S(1)}, bf16[1848,256]{1,0:T(8,128)(2,1)}, u32[]{:S(2)}) copy-start(bf16[1848,256]{1,0:T(8,128)(2,1)} %get-tuple-element.24) | copy-start | bytes 2838532
  79.2 6.0 %collective-permute-start.7 = (bf16[1848,256]{1,0:T(8,128)(2,1)S(1)}, bf16[1848,256]{1,0:T(8,128)(2,1)S(1)}, u32[]{:S(2)}, u32[]{:S(2)}) collective-permute-start(bf16[1848,256]{1,0:T(8,128)(2,1)S(1)} %copy-done.2), channel_id=1, source_target_pairs={{0,4},{4,0},{8,12},{12,8},{16,20},{20,16},{24,28},{28,24},{1,5},{5... | collective-permute-start | bytes 2838536 | tf_op jit(solution)/shard_map/ppermute | solution.py:15
  81.9 5.3 %collective-permute-start.15 = (f32[256,1024]{1,0:T(8,128)S(1)}, f32[256,1024]{1,0:T(8,128)S(1)}, u32[]{:S(2)}, u32[]{:S(2)}) collective-permute-start(f32[256,1024]{1,0:T(8,128)S(1)} %fusion.10), channel_id=1, source_target_pairs={{0,4},{4,0},{8,12},{12,8},{16,20},{20,16},{24,28},{28,24},{1,5},{5... | collective-permute-start | bytes 3145736 | tf_op jit(solution)/shard_map/ppermute | solution.py:15
  83.5 5.7 %collective-permute-start.20 = (f32[256,1024]{1,0:T(8,128)S(1)}, f32[256,1024]{1,0:T(8,128)S(1)}, u32[]{:S(2)}, u32[]{:S(2)}) collective-permute-start(f32[256,1024]{1,0:T(8,128)S(1)} %fusion.17), channel_id=1, source_target_pairs={{0,4},{4,0},{8,12},{12,8},{16,20},{20,16},{24,28},{28,24},{1,5},{5... | collective-permute-start | bytes 3145736 | tf_op jit(solution)/shard_map/ppermute | solution.py:15
  85.3 5.9 %collective-permute-start.10 = (f32[256,1024]{1,0:T(8,128)S(1)}, f32[256,1024]{1,0:T(8,128)S(1)}, u32[]{:S(2)}, u32[]{:S(2)}) collective-permute-start(f32[256,1024]{1,0:T(8,128)S(1)} %fusion.22), channel_id=1, source_target_pairs={{0,4},{4,0},{8,12},{12,8},{16,20},{20,16},{24,28},{28,24},{1,5},{5... | collective-permute-start | bytes 3145736 | tf_op jit(solution)/shard_map/ppermute | solution.py:15
  86.9 9.3 %collective-permute-start.8 = (f32[256,1024]{1,0:T(8,128)S(1)}, f32[256,1024]{1,0:T(8,128)S(1)}, u32[]{:S(2)}, u32[]{:S(2)}) collective-permute-start(f32[256,1024]{1,0:T(8,128)S(1)} %fusion.34), channel_id=1, source_target_pairs={{0,4},{4,0},{8,12},{12,8},{16,20},{20,16},{24,28},{28,24},{1,5},{5... | collective-permute-start | bytes 3145736 | tf_op jit(solution)/shard_map/ppermute | solution.py:15
  88.6 14.8 %collective-permute-start.16 = (bf16[256,1024]{1,0:T(8,128)(2,1)S(1)}, bf16[256,1024]{1,0:T(8,128)(2,1)S(1)}, u32[]{:S(2)}, u32[]{:S(2)}) collective-permute-start(bf16[256,1024]{1,0:T(8,128)(2,1)S(1)} %fusion.4), channel_id=1, source_target_pairs={{0,8},{4,12},{8,0},{12,4},{16,24},{20,28},{24,16},{28,20},{1,9},{5... | collective-permute-start | bytes 1572872 | tf_op jit(solution)/shard_map/ppermute | solution.py:15
  90.5 25.1 %collective-permute-start.21 = (bf16[256,1024]{1,0:T(8,128)(2,1)S(1)}, bf16[256,1024]{1,0:T(8,128)(2,1)S(1)}, u32[]{:S(2)}, u32[]{:S(2)}) collective-permute-start(bf16[256,1024]{1,0:T(8,128)(2,1)S(1)} %fusion.5), channel_id=1, source_target_pairs={{0,16},{4,20},{8,24},{12,28},{16,0},{20,4},{24,8},{28,12},{1,17},{... | collective-permute-start | bytes 1572872 | tf_op jit(solution)/shard_map/ppermute | solution.py:15
  93.7 21.9 %collective-permute-start.11 = (bf16[256,1024]{1,0:T(8,128)(2,1)S(1)}, bf16[256,1024]{1,0:T(8,128)(2,1)S(1)}, u32[]{:S(2)}, u32[]{:S(2)}) collective-permute-start(bf16[256,1024]{1,0:T(8,128)(2,1)S(1)} %fusion.3), channel_id=1, source_target_pairs={{0,24},{4,28},{8,16},{12,20},{16,8},{20,12},{24,0},{28,4},{1,25},{... | collective-permute-start | bytes 1572872 | tf_op jit(solution)/shard_map/ppermute | solution.py:15
  (1 other events, 2.1 us)

commit v3 on v0

v3 whole, which is shorter than its diff:
```python
import functools
import math

import jax
import jax.numpy as jnp
from jax import lax
from jax.experimental import pallas as pl
from jax.experimental.pallas import tpu as pltpu
from jax.sharding import PartitionSpec as P

FREE = pl.CostEstimate(flops=0, bytes_accessed=0, transcendentals=0)
OVER_FIRST = (((0,), (0,)), ((), ()))


def xor_permute(array, axis, size, mask):
    return lax.ppermute(array, axis, [(i, i ^ mask) for i in range(size)])


def adam_kernel(planes, scale, waits, place_ref, hidden_ref, own_ref, *refs):
    crossed = planes - 1
    fetched_refs, swapped_refs = refs[:crossed], refs[crossed : 2 * crossed]
    master_ref, first_ref, second_ref = refs[2 * crossed : 2 * crossed + 3]
    new_master_ref, new_first_ref, new_second_ref, weights_ref, columns_ref = refs[2 * crossed + 3 + waits :]
    tokens = own_ref.shape[0]
    half = tokens // 2

    @pl.when(pl.program_id(0) == 0)
    def _():
        plane, core = place_ref[0], place_ref[1]
        columns_ref[pl.ds(pl.multiple_of(plane * tokens, tokens), tokens), :] = own_ref[...]
        for mask in range(1, planes):
            start = (plane ^ mask) * tokens
            mine = pl.multiple_of(start + core * half, half)
            other = pl.multiple_of(start + (1 - core) * half, half)
            columns_ref[pl.ds(mine, half), :] = fetched_refs[mask - 1][...]
            columns_ref[pl.ds(other, half), :] = swapped_refs[mask - 1][...]

    grad = jnp.dot(hidden_ref[...], columns_ref[...], preferred_element_type=jnp.float32)
    grad = grad * scale
    new_first = 0.9 * first_ref[...] + 0.1 * grad
    new_second = 0.95 * second_ref[...] + 0.05 * grad * grad
    new_master = master_ref[...] - 0.002 * new_first / (jnp.sqrt(new_second) + 1e-08)
    new_master_ref[...] = new_master
    new_first_ref[...] = new_first
    new_second_ref[...] = new_second
    weights_ref[...] = new_master.astype(jnp.bfloat16)


def adam(place, planes, hidden, out_grad, fetched, swapped, state, step, blocks, before):
    rows, tokens_all = hidden.shape
    width = state[0].shape[1]
    tokens = tokens_all // planes
    start, stop = blocks
    block = pl.BlockSpec((step, width), lambda i, s: (i + start, 0))
    full = pltpu.HBM((rows, width), jnp.float32)
    operands = [hidden, out_grad, *fetched, *swapped, *state, *before]
    operands = [
        x if 2 <= i < 2 * planes else pltpu.with_memory_space_constraint(x, pltpu.HBM)
        for i, x in enumerate(operands)
    ]
    return pl.pallas_call(
        functools.partial(adam_kernel, planes, 1.0 / math.sqrt(tokens_all), len(before)),
        out_shape=[full] * 3 + [pltpu.HBM((rows, width), jnp.bfloat16)],
        grid_spec=pltpu.PrefetchScalarGridSpec(
            num_scalar_prefetch=1,
            grid=(stop - start,),
            in_specs=[
                pl.BlockSpec((step, tokens_all), lambda i, s: (i + start, 0)),
                pl.BlockSpec((tokens, width), lambda i, s: (0, s[0])),
            ]
            + [pl.BlockSpec((tokens // 2, width), lambda i, s: (0, 0))] * (2 * planes - 2)
            + [block] * 3
            + [pl.BlockSpec(memory_space=pl.ANY)] * len(before),
            out_specs=[block] * 4,
            scratch_shapes=[pltpu.VMEM((tokens_all, width), jnp.bfloat16)],
        ),
        input_output_aliases={4 + 2 * planes + i: i for i in range(len(before))},
        compiler_params=pltpu.CompilerParams(vmem_limit_bytes=32 * 1024 * 1024),
        cost_estimate=FREE,
    )(place, *operands)


def product_kernel(crossed, straight, place_ref, *refs):
    held_refs, (own_ref, other_ref), out_refs = refs[: crossed * 2 + straight], refs[-4:-2], refs[-2:]
    parity, core = lax.rem(place_ref[0], 2), place_ref[1]
    cut = held_refs[0].shape[0] if crossed else 0

    def dot(held, weights):
        return lax.dot_general(held, weights, OVER_FIRST, preferred_element_type=jnp.float32)

    def write(first_ref, second_ref):
        total = 0.0
        if crossed:
            total = dot(held_refs[0][...], first_ref[:cut]) + dot(held_refs[1][...], second_ref[:cut])
        if straight:
            total = total + dot(held_refs[-1][core], own_ref[cut:]) + dot(held_refs[-1][1 - core], other_ref[cut:])
        half = out_refs[0].shape[0]
        out_refs[0][...] = total[:half].astype(out_refs[0].dtype)
        out_refs[1][...] = total[half:].astype(out_refs[1].dtype)

    if crossed:
        pl.when(parity == 0)(lambda: write(own_ref, other_ref))
        pl.when(parity != 0)(lambda: write(other_ref, own_ref))
    else:
        write(own_ref, other_ref)


def product(place, crossed, straight, own, other, dtype, cost):
    block, width = own.shape
    columns = min(512, width)
    rows = (crossed or straight)[0].shape[-1]
    weights = pl.BlockSpec((block, columns), lambda j, s: (0, j))
    half = pl.BlockSpec((rows // 2, columns), lambda j, s: (0, j))
    specs = [pl.BlockSpec(array.shape, lambda j, s: (0, 0)) for array in crossed]
    if straight:
        chip = straight[1]
        specs.append(pl.BlockSpec((2, *straight[0].shape[1:]), lambda j, s: (s[2] if chip else 0, 0, 0)))
    return pl.pallas_call(
        functools.partial(product_kernel, bool(crossed), bool(straight)),
        out_shape=[jax.ShapeDtypeStruct((rows // 2, width), dtype)] * 2,
        grid_spec=pltpu.PrefetchScalarGridSpec(
            num_scalar_prefetch=1,
            grid=(width // columns,),
            in_specs=[*specs, weights, weights],
            out_specs=[half, half],
        ),
        compiler_params=pltpu.CompilerParams(vmem_limit_bytes=28 * 1024 * 1024),
        cost_estimate=cost,
    )(place, *crossed, *straight[:1], own, other)


def hold(token, *arrays, flops=10**12):
    anywhere = pl.BlockSpec(memory_space=pl.ANY)
    return pl.pallas_call(
        lambda *refs: None,
        out_shape=jax.ShapeDtypeStruct(token.shape, token.dtype),
        in_specs=[anywhere] * (1 + len(arrays)),
        out_specs=anywhere,
        input_output_aliases={0: 0},
        compiler_params=pltpu.CompilerParams(vmem_limit_bytes=1024 * 1024),
        cost_estimate=pl.CostEstimate(flops=flops, bytes_accessed=0, transcendentals=0),
    )(token, *arrays)


def after(token, arrays):
    return lax.optimization_barrier((token, arrays))


def per_device(train_hidden, out_grad, master, first_moment, second_moment, decode_hidden):
    devices, planes = lax.axis_size("replica"), lax.axis_size("tensor")
    chips = devices // 2
    plane, device = lax.axis_index("tensor"), lax.axis_index("replica")
    chip, core = lax.div(device, 2), lax.rem(device, 2)
    parity = lax.rem(plane, 2)
    rows, hidden = decode_hidden.shape
    block = hidden // devices
    tokens, width = out_grad.shape[0], out_grad.shape[1] // planes
    token = jnp.stack([plane, core, chip]).astype(jnp.int32)

    near = 1
    sides = [mask for mask in range(2, chips) if mask % 2 == 0]
    fars = [mask for mask in range(2, chips) if mask % 2 == 1]

    def to_peer(array, mask, cross=0):
        return xor_permute(array, "replica", devices, 2 * mask + cross)

    windows = decode_hidden.T.reshape(devices, block, rows)

    def part(mask, to_core):
        return lax.dynamic_index_in_dim(windows, (chip ^ mask) * 2 + to_core, 0, keepdims=False)

    far_cuts = [part(mask, core ^ parity) for mask in fars]
    column_cuts = [
        lax.dynamic_slice(
            out_grad,
            (core * (tokens // 2), (plane ^ mask) * width),
            (tokens // 2, width),
        )
        for mask in range(1, planes)
    ]
    shared = {mask: to_peer(cut, mask) for mask, cut in zip(fars, far_cuts, strict=True)}
    pieces = [xor_permute(cut, "tensor", planes, mask + 1) for mask, cut in enumerate(column_cuts)]
    token = hold(token, *far_cuts, *column_cuts)

    cut = block // 2 // 16 * 16

    def straight_part(mask, low):
        return lax.dynamic_slice(windows, ((chip ^ mask) * 2, low, 0), (2, block - low, rows))

    token, windows = after(token, windows)
    near_cut = part(near, core ^ parity)[:cut]
    side_cuts = {mask: straight_part(mask, 0) for mask in sides}
    rest_cut = straight_part(near, cut)
    shared[near] = to_peer(near_cut, near)
    straight = {mask: to_peer(cut, mask) for mask, cut in side_cuts.items()}
    token = hold(token, near_cut, rest_cut, *side_cuts.values())

    passed = {}
    for mask in fars:
        token, shared[mask] = after(token, shared[mask])
        passed[mask] = xor_permute(shared[mask], "tensor", planes, 1)
    token = hold(token, *(shared[mask] for mask in fars))

    token, pieces = after(token, pieces)
    swapped = [to_peer(piece, 0, 1) for piece in pieces]
    state = (master, first_moment, second_moment)
    step = min(320, block)
    blocks = pl.cdiv(block, step)
    middle = (blocks + 1) // 2
    common = (planes, train_hidden.T, out_grad, pieces, swapped, state, step)
    out = list(adam(token, *common, (0, middle), ()))
    shared[near], rest_cut, out[0] = lax.optimization_barrier((shared[near], rest_cut, out[0]))
    straight[near] = to_peer(rest_cut, near)
    passed[near] = xor_permute(shared[near], "tensor", planes, 1)
    if middle < blocks:
        out = adam(token, *common, (middle, blocks), out)
    new_master, new_first, new_second, weights = out

    other = to_peer(weights, 0, 1)
    token = hold(token, *(passed[mask] for mask in fars), flops=2 * 10**9)
    token = hold(token, passed[near], *straight.values(), flops=10**11)

    low = {near: [], **{mask: [] for mask in sides}}
    high = {near: [], **{mask: [] for mask in sides}}
    for mask in fars:
        out = product(token, (shared[mask], passed[mask]), (), weights, other, jnp.bfloat16, FREE)
        low[mask ^ near].append(to_peer(out[0], near))
        high[near].append(to_peer(out[1], mask ^ near))
    back = []
    for mask in (near, *sides):
        crossed = (shared[near], passed[near]) if mask == near else ()
        out = product(token, crossed, (straight[mask], False), weights, other, jnp.float32, FREE)
        sums = [
            functools.reduce(jnp.add, [array.astype(jnp.float32) for array in arrays], mine)
            for mine, arrays in zip(out, (low[mask], high[mask]), strict=True)
        ]
        back.append(to_peer(jnp.concatenate(sums, axis=0).astype(jnp.bfloat16), mask))
    cost = pl.CostEstimate(flops=4 * rows * block * width, bytes_accessed=4 * block * width, transcendentals=0)
    total = product(token, (), (windows, True), weights, other, jnp.float32, cost)
    total = lax.optimization_barrier(jnp.concatenate(total, axis=0))
    for sums in back:
        total = total + sums.astype(jnp.float32)
    decoded = total.astype(jnp.bfloat16)
    return (new_master, new_first, new_second, decoded)


def solution(mesh):
    placed = (
        P(None, "replica"),
        P("tensor", None),
        P("replica", "tensor"),
        P("replica", "tensor"),
        P("replica", "tensor"),
        P("replica", None),
    )
    return jax.shard_map(
        per_device,
        mesh=mesh,
        in_specs=placed,
        out_specs=(
            P("replica", "tensor"),
            P("replica", "tensor"),
            P("replica", "tensor"),
            P("replica", "tensor"),
        ),
        check_vma=False,
    )
```

time: 259 us -> 106 us (0.41)
  waiting for transfers between devices: 146 us -> 27.2 us
  blocking collectives: 54.5 us -> 0 us
  Pallas kernels: 0 us -> 45.6 us
  matrix products: 36.4 us -> 0 us
  starting transfers between devices: 0.04 us -> 20.7 us
  between operations: 14 us -> 0.82 us
  local copies, waits for them, and re-layouts: 7.56 us -> 10.2 us
    all_gather x1 -> x0, waiting for transfers between devices: 146 us -> none  [per_device(): lax.all_gather(weights, 'replica', axis=0, tiled=True)]
    all_to_all x1 -> x0, blocking collectives: 54.5 us -> none  [per_device(): lax.all_to_all(out_grad, 'tensor', split_axis=1, concat_axis=0, tiled=True)]
    pallas_call x0 -> x11, Pallas kernels: none -> 45.6 us  [the longest x2 27.2 us: adam(): pl.pallas_call(functools.partial(adam_kernel, planes, 1.0 / math.sqrt(tok...]
    dot_general x2 -> x0, matrix products: 36.4 us -> none  [the longest x1 20.5 us: per_device(): lax.dot_general(train_hidden, columns, (((0,), (0,)), ((), ())), preferre...]
    ppermute x0 -> x17, waiting for transfers between devices: none -> 27.2 us  [xor_permute(): return lax.ppermute(array, axis, [(i, i ^ mask) for i in range(size)])]
    ppermute x0 -> x17, starting transfers between devices: none -> 20.7 us  [xor_permute(): return lax.ppermute(array, axis, [(i, i ^ mask) for i in range(size)])]
    dynamic_slice x0 -> x3, local copies, waits for them, and re-layouts: none -> 6.17 us  [the longest x2 4.16 us: straight_part(): lax.dynamic_slice(windows, ((chip ^ mask) * 2, low, 0), (2, block - low,...]
    unnamed x2 -> x6, local copies, waits for them, and re-layouts: 5.08 us -> 0.02 us
  transfers between devices with their start and end apart: 1 -> 17, of which waited for: 1 -> 9; matrix products, arithmetic and copies ran while one was open for 0% -> 8% of each run, Pallas kernels for 0% -> 39%
where the time goes in v3:
time: 106 us
  Pallas kernels  45.6 us (43%)
  waiting for transfers between devices  27.2 us (26%)
  starting transfers between devices  20.7 us (20%)
  local copies, waits for them, and re-layouts  10.2 us (10%)
  other arithmetic  1.45 us (1%)
    ppermute x17, waiting for transfers between devices, xor_permute(): return lax.ppermute(array, axis, [(i, i ^ mask) for i in range(size)])  27.2 us
    pallas_call x2, Pallas kernels, adam(): pl.pallas_call(functools.partial(adam_kernel, planes, 1.0 / math.sqrt(tok...  27.2 us
    ppermute x17, starting transfers between devices, xor_permute(): return lax.ppermute(array, axis, [(i, i ^ mask) for i in range(size)])  20.7 us
    pallas_call x4, Pallas kernels, product(): pl.pallas_call(functools.partial(product_kernel, bool(crossed), bool(stra...  18.4 us
    dynamic_slice x2, local copies, waits for them, and re-layouts, straight_part(): lax.dynamic_slice(windows, ((chip ^ mask) * 2, low, 0), (2, block - low,...  4.16 us
    squeeze x1, local copies, waits for them, and re-layouts, part(): lax.dynamic_index_in_dim(windows, (chip ^ mask) * 2 + to_core, 0, keepdim...  2.19 us
  transfers between devices with their start and end apart: 17, of which 9 were waited for; matrix products, arithmetic and copies ran while one was open for 8% of the time, Pallas kernels for 39%

profile of v3, /device:TPU:0, one launch (start us, length us, event | category | flops | bytes accessed | tf_op | source)
XLA Modules:
  0.0 106.0 jit_solution(13002261586099765765)
XLA Ops:
  0.6 2.2 %dynamic-slice_bitcast_fusion.refs_1_ = bf16[1848,256]{1,0:T(8,128)(2,1)} fusion(bf16[8,1848,256]{2,1,0:T(8,128)(2,1)} %bitcast.11, s32[]{:T(128)S(6)} %select_n.27), kind=kLoop, calls=%fused_computation.2 | loop fusion | bytes 1892356 | tf_op jit(solution)/shard_map/jit(dynamic_index_in_dim)/squeeze | solution.py:170
  2.8 3.9 %collective-permute-start = (bf16[1848,256]{1,0:T(8,128)(2,1)}, bf16[1848,256]{1,0:T(8,128)(2,1)}, u32[]{:S(2)}, u32[]{:S(2)}) collective-permute-start(bf16[1848,256]{1,0:T(8,128)(2,1)} %dynamic-slice_bitcast_fusion.refs_1_), channel_id=1, source_target_pairs={{0,24},{4,28},{8,16},{12,20},{16,8},{20,12},{24,0},{28,4},{1,25},{... | collective-permute-start | bytes 2838536 | tf_op jit(solution)/shard_map/ppermute | solution.py:16
  6.7 2.0 %fusion = (bf16[128,1024]{1,0:T(8,128)(2,1)}, bf16[128,1024]{1,0:T(8,128)(2,1)}, bf16[128,1024]{1,0:T(8,128)(2,1)}) fusion(bf16[256,4096]{1,0:T(8,128)(2,1)} %own_ref.3, s32[]{:T(128)S(6)} %select_n.28, s32[]{:T(128)S(6)} %select_n.31, s32[]{:T(128)S(6)} %select_n.30, s32[]{:T(128)S(6)} %select_n.29), kind=kLoop, calls=%fused_computation.11 | loop fusion | bytes 1572880 | tf_op jit(solution)/shard_map/dynamic_slice | solution.py:174
  8.7 1.6 %collective-permute-start.1 = (bf16[128,1024]{1,0:T(8,128)(2,1)}, bf16[128,1024]{1,0:T(8,128)(2,1)}, u32[]{:S(2)}, u32[]{:S(2)}) collective-permute-start(bf16[128,1024]{1,0:T(8,128)(2,1)} %get-tuple-element.60.refs_2_), channel_id=1, source_target_pairs={{0,1},{1,0},{2,3},{3,2},{4,5},{5,4},{6,7},{7,6},{8,9},{9,8},{10,11... | collective-permute-start | bytes 786440 | tf_op jit(solution)/shard_map/ppermute | solution.py:16
  10.3 2.6 %collective-permute-start.2 = (bf16[128,1024]{1,0:T(8,128)(2,1)}, bf16[128,1024]{1,0:T(8,128)(2,1)}, u32[]{:S(2)}, u32[]{:S(2)}) collective-permute-start(bf16[128,1024]{1,0:T(8,128)(2,1)} %get-tuple-element.59.refs_3_), channel_id=1, source_target_pairs={{0,2},{1,3},{2,0},{3,1},{4,6},{5,7},{6,4},{7,5},{8,10},{9,11},{10,... | collective-permute-start | bytes 786440 | tf_op jit(solution)/shard_map/ppermute | solution.py:16
  13.2 1.8 %dynamic-slice_bitcast_fusion.1.refs_1_ = bf16[912,256]{1,0:T(8,128)(2,1)} fusion(bf16[8,1848,256]{2,1,0:T(8,128)(2,1)} %bitcast.12, s32[]{:T(128)S(6)} %select_n.32), kind=kLoop, calls=%fused_computation.7 | loop fusion | bytes 933892 | tf_op jit(solution)/shard_map/slice | solution.py:191
  15.6 1.3 %constant_dynamic-slice_fusion.1.refs_2_ = bf16[2,936,256]{2,1,0:T(8,128)(2,1)S(1)} fusion(bf16[8,1848,256]{2,1,0:T(8,128)(2,1)} %bitcast.13, s32[]{:T(128)S(6)} %select_n.33), kind=kLoop, calls=%fused_computation.9 | loop fusion | bytes 1916932 | tf_op jit(solution)/shard_map/dynamic_slice | solution.py:188
  16.8 2.9 %constant_dynamic-slice_fusion.refs_3_ = bf16[2,1848,256]{2,1,0:T(8,128)(2,1)} fusion(bf16[8,1848,256]{2,1,0:T(8,128)(2,1)} %bitcast.14, s32[]{:T(128)S(6)} %select_n.34), kind=kLoop, calls=%fused_computation.8 | loop fusion | bytes 3784708 | tf_op jit(solution)/shard_map/dynamic_slice | solution.py:188
  19.7 9.1 %collective-permute-done.refs_1_.refs_0_ = bf16[1848,256]{1,0:T(8,128)(2,1)} collective-permute-done((bf16[1848,256]{1,0:T(8,128)(2,1)}, bf16[1848,256]{1,0:T(8,128)(2,1)}, u32[]{:S(2)}, u32[]{:S(2)}) %collective-permute-start) | collective-permute-done | bytes 946208 | tf_op jit(solution)/shard_map/ppermute | solution.py:16
  28.8 2.0 %collective-permute-start.10 = (bf16[2,1848,256]{2,1,0:T(8,128)(2,1)}, bf16[2,1848,256]{2,1,0:T(8,128)(2,1)}, u32[]{:S(2)}, u32[]{:S(2)}) collective-permute-start(bf16[2,1848,256]{2,1,0:T(8,128)(2,1)} %constant_dynamic-slice_fusion.refs_3_), channel_id=1, source_target_pairs={{0,16},{4,20},{8,24},{12,28},{16,0},{20,4},{24,8},{28,12},{1,17},{... | collective-permute-start | bytes 5677064 | tf_op jit(solution)/shard_map/ppermute | solution.py:16
  30.9 1.1 %collective-permute-done.2.refs_1_ = bf16[128,1024]{1,0:T(8,128)(2,1)} collective-permute-done((bf16[128,1024]{1,0:T(8,128)(2,1)}, bf16[128,1024]{1,0:T(8,128)(2,1)}, u32[]{:S(2)}, u32[]{:S(2)}) %collective-permute-start.2) | collective-permute-done | bytes 262176 | tf_op jit(solution)/shard_map/ppermute | solution.py:16
  32.5 1.2 %collective-permute-done.4.refs_3_ = bf16[128,1024]{1,0:T(8,128)(2,1)S(1)} collective-permute-done((bf16[128,1024]{1,0:T(8,128)(2,1)}, bf16[128,1024]{1,0:T(8,128)(2,1)S(1)}, u32[]{:S(2)}, u32[]{:S(2)}) %collective-permute-start.4) | collective-permute-done | bytes 262176 | tf_op jit(solution)/shard_map/ppermute | solution.py:16
  33.8 4.5 %collective-permute-start.8 = (bf16[1848,256]{1,0:T(8,128)(2,1)}, bf16[1848,256]{1,0:T(8,128)(2,1)S(1)}, u32[]{:S(2)}, u32[]{:S(2)}) collective-permute-start(bf16[1848,256]{1,0:T(8,128)(2,1)} %collective-permute-done.refs_1_.refs_0_), channel_id=1, source_target_pairs={{0,1},{1,0},{2,3},{3,2},{4,5},{5,4},{6,7},{7,6},{8,9},{9,8},{10,11... | collective-permute-start | bytes 2838536 | tf_op jit(solution)/shard_map/ppermute | solution.py:16
  38.2 14.2 %shard_map.96 = (f32[1848,1024]{1,0:T(8,128)}, f32[1848,1024]{1,0:T(8,128)}, f32[1848,1024]{1,0:T(8,128)}, bf16[1848,1024]{1,0:T(8,128)(2,1)}) custom-call(s32[3]{0:T(128)S(1)} %shard_map.95.place_ref.refs_0_, bf16[1848,1024]{1,0:T(8,128)(2,1)} %bitcast.18, bf16[256,4096]{1,0:T(8,128)(2,1)} %own_ref.3, bf16[128,1024]{1,0:T(8,128)(2,1)} %collective-permute-done.1.refs_0_, ...), custom_call_target="tpu_custom_call" | custom-call | tf_op jit(solution)/shard_map/pallas_call | solution.py:61
  53.8 13.0 %shard_map.97 = (f32[1848,1024]{1,0:T(8,128)}, f32[1848,1024]{1,0:T(8,128)}, f32[1848,1024]{1,0:T(8,128)}, bf16[1848,1024]{1,0:T(8,128)(2,1)}) custom-call(s32[3]{0:T(128)S(1)} %shard_map.95.place_ref.refs_0_, bf16[1848,1024]{1,0:T(8,128)(2,1)} %bitcast.19, ...), custom_call_target="tpu_custom_call", output_to_operand_aliasing={{0}: (12, {}), {1}: (13, {}), {2}: (14, {}), {3}: (15, {})} | custom-call | tf_op jit(solution)/shard_map/pallas_call | solution.py:61
  66.8 2.9 %collective-permute-done.9.refs_1_ = bf16[912,256]{1,0:T(8,128)(2,1)S(1)} collective-permute-done((bf16[912,256]{1,0:T(8,128)(2,1)}, bf16[912,256]{1,0:T(8,128)(2,1)S(1)}, u32[]{:S(2)}, u32[]{:S(2)}) %collective-permute-start.9) | collective-permute-done | bytes 466976 | tf_op jit(solution)/shard_map/ppermute | solution.py:16
  69.7 1.0 collective-permute-done.10.refs_2_.refs_0_
  70.7 4.7 %collective-permute-done.11.refs_3_.refs_2_ = bf16[2,936,256]{2,1,0:T(8,128)(2,1)S(1)} collective-permute-done((bf16[2,936,256]{2,1,0:T(8,128)(2,1)S(1)}, bf16[2,936,256]{2,1,0:T(8,128)(2,1)S(1)}, u32[]{:S(2)}, u32[]{:S(2)}) %collective-permute-start.11) | collective-permute-done | bytes 958496 | tf_op jit(solution)/shard_map/ppermute | solution.py:16
  75.5 4.6 %shard_map.102 = (bf16[128,1024]{1,0:T(8,128)(2,1)S(1)}, bf16[128,1024]{1,0:T(8,128)(2,1)S(1)}) custom-call(s32[3]{0:T(128)S(1)} %shard_map.99.place_ref, bf16[1848,256]{1,0:T(8,128)(2,1)} %collective-permute-done.refs_1_.refs_0_, bf16[1848,256]{1,0:T(8,128)(2,1)S(1)} %collective-permute-done.8.refs_1_, bf16[1848,1024]{1,0:T(8,128)(2,1)S(1)} %copy-done, ...), custom_call_target="tpu_custom_call" | custom-call | tf_op jit(solution)/shard_map/pallas_call | solution.py:118
  80.7 5.0 %shard_map.103 = (f32[128,1024]{1,0:T(8,128)S(1)}, f32[128,1024]{1,0:T(8,128)S(1)}) custom-call(s32[3]{0:T(128)S(1)} %shard_map.99.place_ref, bf16[2,1848,256]{2,1,0:T(8,128)(2,1)} %collective-permute-done.10.refs_2_.refs_0_, bf16[1848,1024]{1,0:T(8,128)(2,1)S(1)} %copy-done, bf16[1848,1024]{1,0:T(8,128)(2,1)S(1)} %collective-permute-done.12.refs_2_.refs_4_.refs_3_), custom_call_target="tpu_custom_call" | custom-call | tf_op jit(solution)/shard_map/pallas_call | solution.py:118
  86.3 5.1 %shard_map.101 = (f32[128,1024]{1,0:T(8,128)S(1)}, f32[128,1024]{1,0:T(8,128)S(1)}) custom-call(s32[3]{0:T(128)S(1)} %shard_map.99.place_ref, bf16[912,256]{1,0:T(8,128)(2,1)} %collective-permute-done.7.refs_0_, bf16[912,256]{1,0:T(8,128)(2,1)S(1)} %collective-permute-done.9.refs_1_, bf16[2,936,256]{2,1,0:T(8,128)(2,1)S(1)} %collective-permute-done.11.refs_3_.refs_2_, ...), custom_call_target="tpu_custom_call" | custom-call | tf_op jit(solution)/shard_map/pallas_call | solution.py:118
  93.1 1.4 %collective-permute-start.14 = (bf16[256,1024]{1,0:T(8,128)(2,1)S(1)}, bf16[256,1024]{1,0:T(8,128)(2,1)S(1)}, u32[]{:S(2)}, u32[]{:S(2)}) collective-permute-start(bf16[256,1024]{1,0:T(8,128)(2,1)S(1)} %pad_maximum_fusion.1), channel_id=1, source_target_pairs={{0,8},{4,12},{8,0},{12,4},{16,24},{20,28},{24,16},{28,20},{1,9},{5... | collective-permute-start | bytes 1572872 | tf_op jit(solution)/shard_map/ppermute | solution.py:16
  94.5 3.7 %shard_map.100 = (f32[128,1024]{1,0:T(8,128)S(1)}, f32[128,1024]{1,0:T(8,128)S(1)}) custom-call(s32[3]{0:T(128)S(1)} %shard_map.99.place_ref, bf16[8,1848,256]{2,1,0:T(8,128)(2,1)S(1)} %bitcast.17, bf16[1848,1024]{1,0:T(8,128)(2,1)S(1)} %copy-done, bf16[1848,1024]{1,0:T(8,128)(2,1)S(1)} %collective-permute-done.12.refs_2_.refs_4_.refs_3_), custom_call_target="tpu_custom_call" | custom-call | flops 1937768448 | bytes 7569408 | tf_op jit(solution)/shard_map/pallas_call | solution.py:118
  98.3 5.9 %collective-permute-done.16 = bf16[256,1024]{1,0:T(8,128)(2,1)S(1)} collective-permute-done((bf16[256,1024]{1,0:T(8,128)(2,1)S(1)}, bf16[256,1024]{1,0:T(8,128)(2,1)S(1)}, u32[]{:S(2)}, u32[]{:S(2)}) %collective-permute-start.16) | collective-permute-done | bytes 524320 | tf_op jit(solution)/shard_map/ppermute | solution.py:16
  (42 shorter events, 7.4 us)
Async XLA Ops:
  2.8 26.0 %collective-permute-start = (bf16[1848,256]{1,0:T(8,128)(2,1)}, bf16[1848,256]{1,0:T(8,128)(2,1)}, u32[]{:S(2)}, u32[]{:S(2)}) collective-permute-start(bf16[1848,256]{1,0:T(8,128)(2,1)} %dynamic-slice_bitcast_fusion.refs_1_), channel_id=1, source_target_pairs={{0,24},{4,28},{8,16},{12,20},{16,8},{20,12},{24,0},{28,4},{1,25},{... | collective-permute-start | bytes 2838536 | tf_op jit(solution)/shard_map/ppermute | solution.py:16
  8.7 22.1 %collective-permute-start.1 = (bf16[128,1024]{1,0:T(8,128)(2,1)}, bf16[128,1024]{1,0:T(8,128)(2,1)}, u32[]{:S(2)}, u32[]{:S(2)}) collective-permute-start(bf16[128,1024]{1,0:T(8,128)(2,1)} %get-tuple-element.60.refs_2_), channel_id=1, source_target_pairs={{0,1},{1,0},{2,3},{3,2},{4,5},{5,4},{6,7},{7,6},{8,9},{9,8},{10,11... | collective-permute-start | bytes 786440 | tf_op jit(solution)/shard_map/ppermute | solution.py:16
  10.3 21.7 %collective-permute-start.2 = (bf16[128,1024]{1,0:T(8,128)(2,1)}, bf16[128,1024]{1,0:T(8,128)(2,1)}, u32[]{:S(2)}, u32[]{:S(2)}) collective-permute-start(bf16[128,1024]{1,0:T(8,128)(2,1)} %get-tuple-element.59.refs_3_), channel_id=1, source_target_pairs={{0,2},{1,3},{2,0},{3,1},{4,6},{5,7},{6,4},{7,5},{8,10},{9,11},{10,... | collective-permute-start | bytes 786440 | tf_op jit(solution)/shard_map/ppermute | solution.py:16
  12.9 19.1 %collective-permute-start.3 = (bf16[128,1024]{1,0:T(8,128)(2,1)}, bf16[128,1024]{1,0:T(8,128)(2,1)}, u32[]{:S(2)}, u32[]{:S(2)}) collective-permute-start(bf16[128,1024]{1,0:T(8,128)(2,1)} %get-tuple-element.58.refs_4_), channel_id=1, source_target_pairs={{0,3},{1,2},{2,1},{3,0},{4,7},{5,6},{6,5},{7,4},{8,11},{9,10},{10,... | collective-permute-start | bytes 786440 | tf_op jit(solution)/shard_map/ppermute | solution.py:16
  15.0 37.4 %collective-permute-start.7 = (bf16[912,256]{1,0:T(8,128)(2,1)}, bf16[912,256]{1,0:T(8,128)(2,1)}, u32[]{:S(2)}, u32[]{:S(2)}) collective-permute-start(bf16[912,256]{1,0:T(8,128)(2,1)} %dynamic-slice_bitcast_fusion.1.refs_1_), channel_id=1, source_target_pairs={{0,8},{4,12},{8,0},{12,4},{16,24},{20,28},{24,16},{28,20},{1,9},{5... | collective-permute-start | bytes 1400840 | tf_op jit(solution)/shard_map/ppermute | solution.py:16
  28.8 41.9 %collective-permute-start.10 = (bf16[2,1848,256]{2,1,0:T(8,128)(2,1)}, bf16[2,1848,256]{2,1,0:T(8,128)(2,1)}, u32[]{:S(2)}, u32[]{:S(2)}) collective-permute-start(bf16[2,1848,256]{2,1,0:T(8,128)(2,1)} %constant_dynamic-slice_fusion.refs_3_), channel_id=1, source_target_pairs={{0,16},{4,20},{8,24},{12,28},{16,0},{20,4},{24,8},{28,12},{1,17},{... | collective-permute-start | bytes 5677064 | tf_op jit(solution)/shard_map/ppermute | solution.py:16
  32.0 1.7 %collective-permute-start.4 = (bf16[128,1024]{1,0:T(8,128)(2,1)}, bf16[128,1024]{1,0:T(8,128)(2,1)S(1)}, u32[]{:S(2)}, u32[]{:S(2)}) collective-permute-start(bf16[128,1024]{1,0:T(8,128)(2,1)} %collective-permute-done.1.refs_0_), channel_id=1, source_target_pairs={{0,4},{4,0},{8,12},{12,8},{16,20},{20,16},{24,28},{28,24},{1,5},{5... | collective-permute-start | bytes 786440 | tf_op jit(solution)/shard_map/ppermute | solution.py:16
  32.0 6.2 %collective-permute-start.5 = (bf16[128,1024]{1,0:T(8,128)(2,1)}, bf16[128,1024]{1,0:T(8,128)(2,1)S(1)}, u32[]{:S(2)}, u32[]{:S(2)}) collective-permute-start(bf16[128,1024]{1,0:T(8,128)(2,1)} %collective-permute-done.2.refs_1_), channel_id=1, source_target_pairs={{0,4},{4,0},{8,12},{12,8},{16,20},{20,16},{24,28},{28,24},{1,5},{5... | collective-permute-start | bytes 786440 | tf_op jit(solution)/shard_map/ppermute | solution.py:16
  32.5 5.7 %collective-permute-start.6 = (bf16[128,1024]{1,0:T(8,128)(2,1)}, bf16[128,1024]{1,0:T(8,128)(2,1)S(1)}, u32[]{:S(2)}, u32[]{:S(2)}) collective-permute-start(bf16[128,1024]{1,0:T(8,128)(2,1)} %collective-permute-done.3.refs_2_), channel_id=1, source_target_pairs={{0,4},{4,0},{8,12},{12,8},{16,20},{20,16},{24,28},{28,24},{1,5},{5... | collective-permute-start | bytes 786440 | tf_op jit(solution)/shard_map/ppermute | solution.py:16
  33.8 33.0 %collective-permute-start.8 = (bf16[1848,256]{1,0:T(8,128)(2,1)}, bf16[1848,256]{1,0:T(8,128)(2,1)S(1)}, u32[]{:S(2)}, u32[]{:S(2)}) collective-permute-start(bf16[1848,256]{1,0:T(8,128)(2,1)} %collective-permute-done.refs_1_.refs_0_), channel_id=1, source_target_pairs={{0,1},{1,0},{2,3},{3,2},{4,5},{5,4},{6,7},{7,6},{8,9},{9,8},{10,11... | collective-permute-start | bytes 2838536 | tf_op jit(solution)/shard_map/ppermute | solution.py:16
  52.4 23.1 %collective-permute-start.11 = (bf16[2,936,256]{2,1,0:T(8,128)(2,1)S(1)}, bf16[2,936,256]{2,1,0:T(8,128)(2,1)S(1)}, u32[]{:S(2)}, u32[]{:S(2)}) collective-permute-start(bf16[2,936,256]{2,1,0:T(8,128)(2,1)S(1)} %constant_dynamic-slice_fusion.1.refs_2_), channel_id=1, source_target_pairs={{0,8},{4,12},{8,0},{12,4},{16,24},{20,28},{24,16},{28,20},{1,9},{5... | collective-permute-start | bytes 2875400 | tf_op jit(solution)/shard_map/ppermute | solution.py:16
  53.0 16.7 %collective-permute-start.9 = (bf16[912,256]{1,0:T(8,128)(2,1)}, bf16[912,256]{1,0:T(8,128)(2,1)S(1)}, u32[]{:S(2)}, u32[]{:S(2)}) collective-permute-start(bf16[912,256]{1,0:T(8,128)(2,1)} %collective-permute-done.7.refs_0_), channel_id=1, source_target_pairs={{0,1},{1,0},{2,3},{3,2},{4,5},{5,4},{6,7},{7,6},{8,9},{9,8},{10,11... | collective-permute-start | bytes 1400840 | tf_op jit(solution)/shard_map/ppermute | solution.py:16
  66.7 8.7 %collective-permute-start.12 = (bf16[1848,1024]{1,0:T(8,128)(2,1)}, bf16[1848,1024]{1,0:T(8,128)(2,1)S(1)}, u32[]{:S(2)}, u32[]{:S(2)}) collective-permute-start(bf16[1848,1024]{1,0:T(8,128)(2,1)} %get-tuple-element.49.refs_1_.refs_3_.refs_2_), channel_id=1, source_target_pairs={{0,4},{4,0},{8,12},{12,8},{16,20},{20,16},{24,28},{28,24},{1,5},{5... | collective-permute-start | bytes 11354120 | tf_op jit(solution)/shard_map/ppermute | solution.py:16
  66.8 8.7 %copy-start = (bf16[1848,1024]{1,0:T(8,128)(2,1)S(1)}, bf16[1848,1024]{1,0:T(8,128)(2,1)}, u32[]{:S(2)}) copy-start(bf16[1848,1024]{1,0:T(8,128)(2,1)} %get-tuple-element.49.refs_1_.refs_3_.refs_2_) | copy-start | bytes 11354116
  80.1 11.4 %collective-permute-start.15 = (bf16[128,1024]{1,0:T(8,128)(2,1)S(1)}, bf16[128,1024]{1,0:T(8,128)(2,1)S(1)}, u32[]{:S(2)}, u32[]{:S(2)}) collective-permute-start(bf16[128,1024]{1,0:T(8,128)(2,1)S(1)} %get-tuple-element.56), channel_id=1, source_target_pairs={{0,8},{4,12},{8,0},{12,4},{16,24},{20,28},{24,16},{28,20},{1,9},{5... | collective-permute-start | bytes 786440 | tf_op jit(solution)/shard_map/ppermute | solution.py:16
  85.7 8.8 %slice-start = ((s8[7569408]{0:T(1024)(128)(4,1)}), s8[4194304]{0:T(1024)(128)(4,1)S(1)}, s32[]{:S(2)}) async-start(s8[7569408]{0:T(1024)(128)(4,1)} %bitcast.15), calls=%async_computation | async-start | bytes 8388608
  85.8 8.7 %slice-start.1 = ((s8[7569408]{0:T(1024)(128)(4,1)}), s8[3375104]{0:T(1024)(128)(4,1)S(1)}, s32[]{:S(2)}) async-start(s8[7569408]{0:T(1024)(128)(4,1)} %bitcast.15), calls=%async_computation.1 | async-start | bytes 6750208
  85.8 7.2 %collective-permute-start.13 = (bf16[128,1024]{1,0:T(8,128)(2,1)S(1)}, bf16[128,1024]{1,0:T(8,128)(2,1)S(1)}, u32[]{:S(2)}, u32[]{:S(2)}) collective-permute-start(bf16[128,1024]{1,0:T(8,128)(2,1)S(1)} %get-tuple-element.54), channel_id=1, source_target_pairs={{0,16},{4,20},{8,24},{12,28},{16,0},{20,4},{24,8},{28,12},{1,17},{... | collective-permute-start | bytes 786440 | tf_op jit(solution)/shard_map/ppermute | solution.py:16
  91.7 12.5 %collective-permute-start.16 = (bf16[256,1024]{1,0:T(8,128)(2,1)S(1)}, bf16[256,1024]{1,0:T(8,128)(2,1)S(1)}, u32[]{:S(2)}, u32[]{:S(2)}) collective-permute-start(bf16[256,1024]{1,0:T(8,128)(2,1)S(1)} %pad_maximum_fusion.2), channel_id=1, source_target_pairs={{0,16},{4,20},{8,24},{12,28},{16,0},{20,4},{24,8},{28,12},{1,17},{... | collective-permute-start | bytes 1572872 | tf_op jit(solution)/shard_map/ppermute | solution.py:16
  93.1 11.9 %collective-permute-start.14 = (bf16[256,1024]{1,0:T(8,128)(2,1)S(1)}, bf16[256,1024]{1,0:T(8,128)(2,1)S(1)}, u32[]{:S(2)}, u32[]{:S(2)}) collective-permute-start(bf16[256,1024]{1,0:T(8,128)(2,1)S(1)} %pad_maximum_fusion.1), channel_id=1, source_target_pairs={{0,8},{4,12},{8,0},{12,4},{16,24},{20,28},{24,16},{28,20},{1,9},{5... | collective-permute-start | bytes 1572872 | tf_op jit(solution)/shard_map/ppermute | solution.py:16

commit v4 on v0

v4 whole, which is shorter than its diff:
```python
import functools
import math

import jax
import jax.numpy as jnp
from jax import lax
from jax.experimental import pallas as pl
from jax.experimental.pallas import tpu as pltpu
from jax.sharding import PartitionSpec as P

FREE = pl.CostEstimate(flops=0, bytes_accessed=0, transcendentals=0)
OVER_FIRST = (((0,), (0,)), ((), ()))


def xor_permute(array, axis, size, mask):
    return lax.ppermute(array, axis, [(i, i ^ mask) for i in range(size)])


def cut_kernel(planes, masks, place_ref, windows_ref, out_grad_ref, *refs):
    *target_refs, sems = refs
    plane, core, chip = place_ref[0], place_ref[1], place_ref[2]
    half, width = target_refs[-1].shape
    copies = []
    for mask, target_ref in zip(masks, target_refs):
        device = (chip ^ mask) * 2 + (core ^ lax.rem(plane, 2))
        copies.append(pltpu.make_async_copy(windows_ref.at[device], target_ref, sems.at[len(copies)]))
    for mask, target_ref in zip(range(1, planes), target_refs[len(masks) :]):
        rows = pl.ds(pl.multiple_of(core * half, half), half)
        columns = pl.ds(pl.multiple_of((plane ^ mask) * width, width), width)
        copies.append(pltpu.make_async_copy(out_grad_ref.at[rows, columns], target_ref, sems.at[len(copies)]))
    for copy in copies:
        copy.start()
    for copy in copies:
        copy.wait()


def cut(place, windows, out_grad, planes, masks):
    tokens, width = out_grad.shape[0], out_grad.shape[1] // planes
    anywhere = pl.BlockSpec(memory_space=pl.ANY)
    pieces = len(masks) + planes - 1
    out = pl.pallas_call(
        functools.partial(cut_kernel, planes, masks),
        out_shape=[pltpu.VMEM(windows.shape[1:], windows.dtype)] * len(masks)
        + [pltpu.VMEM((tokens // 2, width), out_grad.dtype)] * (planes - 1),
        in_specs=[pl.BlockSpec(memory_space=pltpu.SMEM), anywhere, anywhere],
        out_specs=[pl.BlockSpec(memory_space=pltpu.VMEM)] * pieces,
        scratch_shapes=[pltpu.SemaphoreType.DMA((pieces,))],
        compiler_params=pltpu.CompilerParams(vmem_limit_bytes=8 * 1024 * 1024),
        cost_estimate=FREE,
    )(place, *[pltpu.with_memory_space_constraint(x, pltpu.HBM) for x in (windows, out_grad)])
    return out[: len(masks)], out[len(masks) :]


def adam_kernel(planes, scale, cuts, waits, place_ref, own_ref, *refs):
    crossed = planes - 1
    fetched_refs, swapped_refs = refs[:crossed], refs[crossed : 2 * crossed]
    hidden_ref, *state_refs = refs[2 * crossed : 2 * crossed + 4]
    *out_refs, weights_ref, columns_ref, rows_ref, held_ref, row_sem, in_sems, out_sems = refs[2 * crossed + 4 + waits :]
    base = cuts[0]
    rows_copy = pltpu.make_async_copy(hidden_ref, rows_ref, row_sem)
    copies_in, copies_out = [], []
    for i, (low, high) in enumerate(zip(cuts, cuts[1:])):
        here, there = slice(low - base, high - base), slice(low, high)
        copies_in.append(
            [
                pltpu.make_async_copy(ref.at[there], held_ref.at[k, here], in_sems.at[i, k])
                for k, ref in enumerate(state_refs)
            ]
        )
        copies_out.append(
            [
                pltpu.make_async_copy(held_ref.at[k, here], ref.at[there], out_sems.at[i, k])
                for k, ref in enumerate(out_refs)
            ]
        )
    rows_copy.start()
    for copies in copies_in[:2]:
        for copy in copies:
            copy.start()

    tokens = own_ref.shape[0]
    half = tokens // 2
    plane, core = place_ref[0], place_ref[1]
    columns_ref[pl.ds(pl.multiple_of(plane * tokens, tokens), tokens), :] = own_ref[...]
    for mask in range(1, planes):
        start = (plane ^ mask) * tokens
        mine = pl.multiple_of(start + core * half, half)
        other = pl.multiple_of(start + (1 - core) * half, half)
        columns_ref[pl.ds(mine, half), :] = fetched_refs[mask - 1][...]
        columns_ref[pl.ds(other, half), :] = swapped_refs[mask - 1][...]

    rows_copy.wait()
    for i, (low, high) in enumerate(zip(cuts, cuts[1:])):
        here = slice(low - base, high - base)
        grad = jnp.dot(rows_ref[here], columns_ref[...], preferred_element_type=jnp.float32)
        grad = grad * scale
        for copy in copies_in[i]:
            copy.wait()
        for copy in copies_in[i + 2] if i + 2 < len(copies_in) else ():
            copy.start()
        new_first = 0.9 * held_ref[1, here] + 0.1 * grad
        new_second = 0.95 * held_ref[2, here] + 0.05 * grad * grad
        new_master = held_ref[0, here] - 0.002 * new_first / (jnp.sqrt(new_second) + 1e-08)
        weights_ref[here] = new_master.astype(jnp.bfloat16)
        for k, new in enumerate((new_master, new_first, new_second)):
            held_ref[k, here] = new
            copies_out[i][k].start()
    for copies in copies_out:
        for copy in copies:
            copy.wait()


def adam(place, planes, hidden, own, fetched, swapped, state, cuts, before):
    count, tokens_all = hidden.shape
    rows, width = state[0].shape
    full = pltpu.HBM((rows, width), jnp.float32)
    inside = pl.BlockSpec(memory_space=pltpu.VMEM)
    outside = pl.BlockSpec(memory_space=pl.ANY)
    near = [own, *fetched, *swapped]
    far = [pltpu.with_memory_space_constraint(x, pltpu.HBM) for x in (hidden, *state, *before)]
    return pl.pallas_call(
        functools.partial(adam_kernel, planes, 1.0 / math.sqrt(tokens_all), cuts, len(before)),
        out_shape=[full] * 3 + [jax.ShapeDtypeStruct((count, width), jnp.bfloat16)],
        in_specs=[pl.BlockSpec(memory_space=pltpu.SMEM)] + [inside] * len(near) + [outside] * len(far),
        out_specs=[outside] * 3 + [inside],
        scratch_shapes=[
            pltpu.VMEM((tokens_all, width), jnp.bfloat16),
            pltpu.VMEM((count, tokens_all), jnp.bfloat16),
            pltpu.VMEM((3, count, width), jnp.float32),
            pltpu.SemaphoreType.DMA,
            pltpu.SemaphoreType.DMA((len(cuts) - 1, 3)),
            pltpu.SemaphoreType.DMA((len(cuts) - 1, 3)),
        ],
        input_output_aliases={1 + len(near) + 4 + i: i for i in range(len(before))},
        compiler_params=pltpu.CompilerParams(vmem_limit_bytes=28 * 1024 * 1024),
        cost_estimate=FREE,
    )(place, *near, *far)


def product_kernel(crossed, parts, place_ref, *refs):
    own_refs, other_refs, out_refs = refs[-2 * parts - 2 : -parts - 2], refs[-parts - 2 : -2], refs[-2:]
    held_refs = refs[: -2 * parts - 2]
    parity, core = lax.rem(place_ref[0], 2), place_ref[1]
    cut = held_refs[0].shape[0] if crossed else 0

    def dot(weights_refs, low, high, read):
        total, at = 0.0, 0
        for ref in weights_refs:
            begin, end = max(low, at), min(high, at + ref.shape[0])
            if begin < end:
                total = total + lax.dot_general(
                    read(begin, end), ref[begin - at : end - at], OVER_FIRST, preferred_element_type=jnp.float32
                )
            at += ref.shape[0]
        return total

    def write(first_refs, second_refs):
        block = sum(ref.shape[0] for ref in own_refs)
        total = 0.0
        if crossed:
            total = dot(first_refs, 0, cut, lambda begin, end: held_refs[0][begin:end])
            total = total + dot(second_refs, 0, cut, lambda begin, end: held_refs[1][begin:end])
        if cut < block:
            straight_ref = held_refs[-1]
            total = total + dot(own_refs, cut, block, lambda begin, end: straight_ref[core, begin - cut : end - cut])
            total = total + dot(
                other_refs, cut, block, lambda begin, end: straight_ref[1 - core, begin - cut : end - cut]
            )
        half = out_refs[0].shape[0]
        out_refs[0][...] = total[:half].astype(out_refs[0].dtype)
        out_refs[1][...] = total[half:].astype(out_refs[1].dtype)

    if crossed:
        pl.when(parity == 0)(lambda: write(own_refs, other_refs))
        pl.when(parity != 0)(lambda: write(other_refs, own_refs))
    else:
        write(own_refs, other_refs)


def product(place, crossed, straight, own, other, dtype, cost):
    width = own[0].shape[1]
    rows = (*crossed, *straight)[0].shape[-1]
    operands = [*crossed, *straight, *own, *other]
    operands = [pltpu.with_memory_space_constraint(x, pltpu.VMEM) for x in operands]
    inside = pl.BlockSpec(memory_space=pltpu.VMEM)
    return pl.pallas_call(
        functools.partial(product_kernel, bool(crossed), len(own)),
        out_shape=[jax.ShapeDtypeStruct((rows // 2, width), dtype)] * 2,
        in_specs=[pl.BlockSpec(memory_space=pltpu.SMEM)] + [inside] * len(operands),
        out_specs=[inside, inside],
        compiler_params=pltpu.CompilerParams(vmem_limit_bytes=12 * 1024 * 1024),
        cost_estimate=cost,
    )(place, *operands)


def add_kernel(lows, mine_low_ref, mine_high_ref, *refs):
    half = mine_low_ref.shape[0]
    low, high = mine_low_ref[...], mine_high_ref[...]
    for i, ref in enumerate(refs[:-1]):
        if i < lows:
            low = low + ref[...].astype(jnp.float32)
        else:
            high = high + ref[...].astype(jnp.float32)
    refs[-1][:half] = low.astype(refs[-1].dtype)
    refs[-1][half:] = high.astype(refs[-1].dtype)


def add(mine, low, high):
    half, width = mine[0].shape
    inside = pl.BlockSpec(memory_space=pltpu.VMEM)
    return pl.pallas_call(
        functools.partial(add_kernel, len(low)),
        out_shape=jax.ShapeDtypeStruct((2 * half, width), jnp.bfloat16),
        in_specs=[inside] * (2 + len(low) + len(high)),
        out_specs=inside,
        compiler_params=pltpu.CompilerParams(vmem_limit_bytes=12 * 1024 * 1024),
        cost_estimate=FREE,
    )(*mine, *low, *high)


def hold(token, *arrays, flops=5 * 10**10):
    anywhere = pl.BlockSpec(memory_space=pl.ANY)
    return pl.pallas_call(
        lambda *refs: None,
        out_shape=jax.ShapeDtypeStruct(token.shape, token.dtype),
        in_specs=[anywhere] * (1 + len(arrays)),
        out_specs=anywhere,
        input_output_aliases={0: 0},
        compiler_params=pltpu.CompilerParams(vmem_limit_bytes=1024 * 1024),
        cost_estimate=pl.CostEstimate(flops=flops, bytes_accessed=0, transcendentals=0),
    )(token, *arrays)


def after(token, arrays):
    return lax.optimization_barrier((token, arrays))


def per_device(train_hidden, out_grad, master, first_moment, second_moment, decode_hidden):
    devices, planes = lax.axis_size("replica"), lax.axis_size("tensor")
    chips = devices // 2
    plane, device = lax.axis_index("tensor"), lax.axis_index("replica")
    chip, core = lax.div(device, 2), lax.rem(device, 2)
    parity = lax.rem(plane, 2)
    rows, hidden = decode_hidden.shape
    block = hidden // devices
    tokens, width = out_grad.shape[0], out_grad.shape[1] // planes
    token = jnp.stack([plane, core, chip]).astype(jnp.int32)

    near = 1
    sides = [mask for mask in range(2, chips) if mask % 2 == 0]
    fars = [mask for mask in range(2, chips) if mask % 2 == 1]

    def to_peer(array, mask, cross=0):
        return xor_permute(array, "replica", devices, 2 * mask + cross)

    windows = decode_hidden.T.reshape(devices, block, rows)

    def part(mask, to_core):
        return lax.dynamic_index_in_dim(windows, (chip ^ mask) * 2 + to_core, 0, keepdims=False)

    far_cuts, column_cuts = cut(token, windows, out_grad, planes, fars)
    shared = {mask: to_peer(piece, mask) for mask, piece in zip(fars, far_cuts, strict=True)}
    pieces = [xor_permute(piece, "tensor", planes, mask + 1) for mask, piece in enumerate(column_cuts)]
    token = hold(token, *far_cuts, *column_cuts)

    first = block * 5 // 8 // 16 * 16

    def straight_part(mask, low):
        return lax.dynamic_slice(windows, ((chip ^ mask) * 2, low, 0), (2, block - low, rows))

    token, (windows, train) = after(token, (windows, train_hidden.T))
    own_columns = lax.dynamic_slice(out_grad, (0, plane * width), (tokens, width))
    cuts = [*range(0, block, min(160, block)), block]
    middle = cuts[len(cuts) // 2] if len(cuts) > 2 else block
    trains = [train[:middle], train[middle:]]
    near_cut = part(near, core ^ parity)[:first]
    side_cuts = {mask: straight_part(mask, 0) for mask in sides}
    rest_cut = straight_part(near, first)
    shared[near] = to_peer(near_cut, near)
    straight = {mask: to_peer(piece, mask) for mask, piece in side_cuts.items()}
    token = hold(token, near_cut, rest_cut, *side_cuts.values(), *trains, own_columns)

    passed = {}
    for mask in fars:
        token, shared[mask] = after(token, shared[mask])
        passed[mask] = xor_permute(shared[mask], "tensor", planes, 1)
    token = hold(token, *(shared[mask] for mask in fars))

    token, (pieces, rest_cut) = after(token, (pieces, rest_cut))
    straight[near] = to_peer(rest_cut, near)
    swapped = [to_peer(piece, 0, 1) for piece in pieces]
    state = (master, first_moment, second_moment)
    def step(at, before):
        rows = [cut for cut in cuts if (cut <= middle if at == 0 else cut >= middle)]
        return list(adam(token, planes, trains[at], own_columns, pieces, swapped, state, rows, before))

    out = step(0, [])
    weights = [out[3]]
    shared[near], out[0] = lax.optimization_barrier((shared[near], out[0]))
    passed[near] = xor_permute(shared[near], "tensor", planes, 1)
    if middle < block:
        out = step(1, out[:3])
        weights.append(out[3])
    new_master, new_first, new_second = out[:3]

    other = [to_peer(array, 0, 1) for array in weights]
    token = hold(token, *(passed[mask] for mask in fars), flops=2 * 10**9)
    token = hold(token, passed[near], *straight.values(), flops=10**11)

    low = {near: [], **{mask: [] for mask in sides}}
    high = {near: [], **{mask: [] for mask in sides}}
    for mask in fars:
        out = product(token, (shared[mask], passed[mask]), (), weights, other, jnp.bfloat16, FREE)
        low[mask ^ near].append(to_peer(out[0], near))
        high[near].append(to_peer(out[1], mask ^ near))
    back = []
    for mask in (near, *sides):
        crossed = (shared[near], passed[near]) if mask == near else ()
        out = product(token, crossed, (straight[mask],), weights, other, jnp.float32, FREE)
        back.append(to_peer(add(out, low[mask], high[mask]), mask))
    cost = pl.CostEstimate(flops=4 * rows * block * width, bytes_accessed=4 * block * width, transcendentals=0)
    mine = lax.dynamic_slice(windows, (chip * 2, 0, 0), (2, block, rows))
    total = product(token, (), (mine,), weights, other, jnp.float32, cost)
    total = lax.optimization_barrier(jnp.concatenate(total, axis=0))
    for sums in back:
        total = total + sums.astype(jnp.float32)
    decoded = total.astype(jnp.bfloat16)
    return (new_master, new_first, new_second, decoded)


def solution(mesh):
    placed = (
        P(None, "replica"),
        P("tensor", None),
        P("replica", "tensor"),
        P("replica", "tensor"),
        P("replica", "tensor"),
        P("replica", None),
    )
    return jax.shard_map(
        per_device,
        mesh=mesh,
        in_specs=placed,
        out_specs=(
            P("replica", "tensor"),
            P("replica", "tensor"),
            P("replica", "tensor"),
            P("replica", "tensor"),
        ),
        check_vma=False,
    )
```

time: 259 us -> 96.8 us (0.37)
  waiting for transfers between devices: 146 us -> 19.6 us
  blocking collectives: 54.5 us -> 0 us
  Pallas kernels: 0 us -> 41 us
  matrix products: 36.4 us -> 0 us
  starting transfers between devices: 0.04 us -> 21.5 us
  between operations: 14 us -> 0.82 us
  local copies, waits for them, and re-layouts: 7.56 us -> 12.1 us
    all_gather x1 -> x0, waiting for transfers between devices: 146 us -> none  [per_device(): lax.all_gather(weights, 'replica', axis=0, tiled=True)]
    all_to_all x1 -> x0, blocking collectives: 54.5 us -> none  [per_device(): lax.all_to_all(out_grad, 'tensor', split_axis=1, concat_axis=0, tiled=True)]
    pallas_call x0 -> x14, Pallas kernels: none -> 41 us  [the longest x2 24.8 us: adam(): pl.pallas_call(functools.partial(adam_kernel, planes, 1.0 / math.sqrt(tok...]
    dot_general x2 -> x0, matrix products: 36.4 us -> none  [the longest x1 20.5 us: per_device(): lax.dot_general(train_hidden, columns, (((0,), (0,)), ((), ())), preferre...]
    ppermute x0 -> x18, starting transfers between devices: none -> 21.5 us  [xor_permute(): return lax.ppermute(array, axis, [(i, i ^ mask) for i in range(size)])]
    ppermute x0 -> x18, waiting for transfers between devices: none -> 19.6 us  [xor_permute(): return lax.ppermute(array, axis, [(i, i ^ mask) for i in range(size)])]
    slice x0 -> x3, local copies, waits for them, and re-layouts: none -> 7.2 us  [the longest x2 5.27 us: per_device(): trains = [train[:middle], train[middle:]]]
    unnamed x2 -> x4, local copies, waits for them, and re-layouts: 5.08 us -> 0.15 us
  transfers between devices with their start and end apart: 1 -> 18, of which waited for: 1 -> 7; matrix products, arithmetic and copies ran while one was open for 0% -> 12% of each run, Pallas kernels for 0% -> 36%
where the time goes in v4:
time: 96.8 us; the launch traced here: 96.3 us
  Pallas kernels  41 us (42%)
  starting transfers between devices  21.5 us (22%)
  waiting for transfers between devices  19.6 us (20%)
  local copies, waits for them, and re-layouts  12.1 us (12%)
  other arithmetic  1.22 us (1%)
    pallas_call x2, Pallas kernels, adam(): pl.pallas_call(functools.partial(adam_kernel, planes, 1.0 / math.sqrt(tok...  24.8 us
    ppermute x18, starting transfers between devices, xor_permute(): return lax.ppermute(array, axis, [(i, i ^ mask) for i in range(size)])  21.5 us
    ppermute x18, waiting for transfers between devices, xor_permute(): return lax.ppermute(array, axis, [(i, i ^ mask) for i in range(size)])  19.6 us
    pallas_call x4, Pallas kernels, product(): pl.pallas_call(functools.partial(product_kernel, bool(crossed), len(own))...  12.9 us
    slice x2, local copies, waits for them, and re-layouts, per_device(): trains = [train[:middle], train[middle:]]  5.27 us
    pallas_call x1, Pallas kernels, cut(): pl.pallas_call(functools.partial(cut_kernel, planes, masks), out_shape=[p...  3.16 us
    dynamic_slice x1, local copies, waits for them, and re-layouts, per_device(): mine = lax.dynamic_slice(windows, (chip * 2, 0, 0), (2, block, rows))  2.47 us
  transfers between devices with their start and end apart: 18, of which 7 were waited for; matrix products, arithmetic and copies ran while one was open for 12% of the time, Pallas kernels for 36%

profile of v4, /device:TPU:0, one launch (start us, length us, event | category | flops | bytes accessed | tf_op | source)
XLA Modules:
  0.0 96.3 jit_solution(14107764628313193786)
XLA Ops:
  0.7 3.2 %shard_map.93 = (bf16[1848,256]{1,0:T(8,128)(2,1)}, bf16[128,1024]{1,0:T(8,128)(2,1)}, bf16[128,1024]{1,0:T(8,128)(2,1)}, bf16[128,1024]{1,0:T(8,128)(2,1)}) custom-call(s32[3]{0:T(128)S(1)} %pad_add_fusion.place_ref.refs_0_, bf16[8,1848,256]{2,1,0:T(8,128)(2,1)} %bitcast.9, bf16[256,4096]{1,0:T(8,128)(2,1)} %out_grad_ref.1), custom_call_target="tpu_custom_call" | custom-call | tf_op jit(solution)/shard_map/pallas_call | solution.py:41
  3.9 4.0 %collective-permute-start = (bf16[1848,256]{1,0:T(8,128)(2,1)}, bf16[1848,256]{1,0:T(8,128)(2,1)}, u32[]{:S(2)}, u32[]{:S(2)}) collective-permute-start(bf16[1848,256]{1,0:T(8,128)(2,1)} %get-tuple-element.36.refs_1_), channel_id=1, source_target_pairs={{0,24},{4,28},{8,16},{12,20},{16,8},{20,12},{24,0},{28,4},{1,25},{... | collective-permute-start | bytes 2838536 | tf_op jit(solution)/shard_map/ppermute | solution.py:16
  7.8 1.6 %collective-permute-start.1 = (bf16[128,1024]{1,0:T(8,128)(2,1)}, bf16[128,1024]{1,0:T(8,128)(2,1)S(1)}, u32[]{:S(2)}, u32[]{:S(2)}) collective-permute-start(bf16[128,1024]{1,0:T(8,128)(2,1)} %get-tuple-element.37.refs_2_), channel_id=1, source_target_pairs={{0,1},{1,0},{2,3},{3,2},{4,5},{5,4},{6,7},{7,6},{8,9},{9,8},{10,11... | collective-permute-start | bytes 786440 | tf_op jit(solution)/shard_map/ppermute | solution.py:16
  9.4 2.6 %collective-permute-start.2 = (bf16[128,1024]{1,0:T(8,128)(2,1)}, bf16[128,1024]{1,0:T(8,128)(2,1)}, u32[]{:S(2)}, u32[]{:S(2)}) collective-permute-start(bf16[128,1024]{1,0:T(8,128)(2,1)} %get-tuple-element.38.refs_3_), channel_id=1, source_target_pairs={{0,2},{1,3},{2,0},{3,1},{4,6},{5,7},{6,4},{7,5},{8,10},{9,11},{10,... | collective-permute-start | bytes 786440 | tf_op jit(solution)/shard_map/ppermute | solution.py:16
  12.2 1.9 %dynamic-slice_bitcast_fusion.refs_1_ = bf16[1152,256]{1,0:T(8,128)(2,1)} fusion(bf16[8,1848,256]{2,1,0:T(8,128)(2,1)} %bitcast.10, s32[]{:T(128)S(6)} %select_n.16), kind=kLoop, calls=%fused_computation.2 | loop fusion | bytes 1179652 | tf_op jit(solution)/shard_map/slice | solution.py:276
  14.7 1.7 %slice.14.refs_4_.refs_6_ = bf16[960,1024]{1,0:T(8,128)(2,1)S(1)} slice(bf16[1848,1024]{1,0:T(8,128)(2,1)} %bitcast.13), slice={[0:960], [0:1024]} | slice | bytes 3932160 | tf_op jit(solution)/shard_map/slice | solution.py:275
  16.4 3.6 %slice.15.refs_5_.refs_6_ = bf16[888,1024]{1,0:T(8,128)(2,1)} slice(bf16[1848,1024]{1,0:T(8,128)(2,1)} %bitcast.14), slice={[960:1848], [0:1024]} | slice | bytes 3637248 | tf_op jit(solution)/shard_map/slice | solution.py:275
  20.0 1.2 %constant_dynamic-slice_fusion.3.refs_2_ = bf16[2,696,256]{2,1,0:T(8,128)(2,1)S(1)} fusion(bf16[8,1848,256]{2,1,0:T(8,128)(2,1)} %bitcast.11, s32[]{:T(128)S(6)} %select_n.17), kind=kLoop, calls=%fused_computation.6 | loop fusion | bytes 1425412 | tf_op jit(solution)/shard_map/dynamic_slice | solution.py:269
  22.2 2.5 %constant_dynamic-slice_fusion = (bf16[2,1848,256]{2,1,0:T(8,128)(2,1)S(1)}, bf16[2,1848,256]{2,1,0:T(8,128)(2,1)S(1)}) fusion(bf16[8,1848,256]{2,1,0:T(8,128)(2,1)} %bitcast.12, s32[]{:T(128)S(6)} %select_n.20, s32[]{:T(128)S(6)} %select_n.18), kind=kLoop, calls=%fused_computation.3 | loop fusion | bytes 7569416 | tf_op jit(solution)/shard_map/dynamic_slice | solution.py:322
  24.9 5.1 %collective-permute-done.refs_1_.refs_0_ = bf16[1848,256]{1,0:T(8,128)(2,1)} collective-permute-done((bf16[1848,256]{1,0:T(8,128)(2,1)}, bf16[1848,256]{1,0:T(8,128)(2,1)}, u32[]{:S(2)}, u32[]{:S(2)}) %collective-permute-start) | collective-permute-done | bytes 946208 | tf_op jit(solution)/shard_map/ppermute | solution.py:16
  30.0 2.0 %collective-permute-start.10 = (bf16[2,1848,256]{2,1,0:T(8,128)(2,1)S(1)}, bf16[2,1848,256]{2,1,0:T(8,128)(2,1)S(1)}, u32[]{:S(2)}, u32[]{:S(2)}) collective-permute-start(bf16[2,1848,256]{2,1,0:T(8,128)(2,1)S(1)} %get-tuple-element.69.refs_3_), channel_id=1, source_target_pairs={{0,16},{4,20},{8,24},{12,28},{16,0},{20,4},{24,8},{28,12},{1,17},{... | collective-permute-start | bytes 5677064 | tf_op jit(solution)/shard_map/ppermute | solution.py:16
  32.0 1.6 %collective-permute-start.8 = (bf16[1848,256]{1,0:T(8,128)(2,1)}, bf16[1848,256]{1,0:T(8,128)(2,1)S(1)}, u32[]{:S(2)}, u32[]{:S(2)}) collective-permute-start(bf16[1848,256]{1,0:T(8,128)(2,1)} %collective-permute-done.refs_1_.refs_0_), channel_id=1, source_target_pairs={{0,1},{1,0},{2,3},{3,2},{4,5},{5,4},{6,7},{7,6},{8,9},{9,8},{10,11... | collective-permute-start | bytes 2838536 | tf_op jit(solution)/shard_map/ppermute | solution.py:16
  35.7 1.5 %collective-permute-start.11 = (bf16[2,696,256]{2,1,0:T(8,128)(2,1)S(1)}, bf16[2,696,256]{2,1,0:T(8,128)(2,1)S(1)}, u32[]{:S(2)}, u32[]{:S(2)}) collective-permute-start(bf16[2,696,256]{2,1,0:T(8,128)(2,1)S(1)} %constant_dynamic-slice_fusion.3.refs_2_), channel_id=1, source_target_pairs={{0,8},{4,12},{8,0},{12,4},{16,24},{20,28},{24,16},{28,20},{1,9},{5... | collective-permute-start | bytes 2138120 | tf_op jit(solution)/shard_map/ppermute | solution.py:16
  37.2 12.6 %shard_map.97 = (f32[1848,1024]{1,0:T(8,128)}, f32[1848,1024]{1,0:T(8,128)}, f32[1848,1024]{1,0:T(8,128)}, bf16[960,1024]{1,0:T(8,128)(2,1)S(1)}) custom-call(s32[3]{0:T(128)S(1)} %shard_map.96.place_ref.refs_0_, bf16[256,1024]{1,0:T(8,128)(2,1)S(1)} %constant_dynamic-slice_fusion.1.refs_6_.own_ref, bf16[128,1024]{1,0:T(8,128)(2,1)S(1)} %collective-permute-done.1.refs_0_, ...), custom_call_target="tpu_custom_call" | custom-call | tf_op jit(solution)/shard_map/pallas_call | solution.py:121
  49.8 2.1 %collective-permute-start.9 = (bf16[1152,256]{1,0:T(8,128)(2,1)}, bf16[1152,256]{1,0:T(8,128)(2,1)S(1)}, u32[]{:S(2)}, u32[]{:S(2)}) collective-permute-start(bf16[1152,256]{1,0:T(8,128)(2,1)} %collective-permute-done.7.refs_0_), channel_id=1, source_target_pairs={{0,1},{1,0},{2,3},{3,2},{4,5},{5,4},{6,7},{7,6},{8,9},{9,8},{10,11... | collective-permute-start | bytes 1769480 | tf_op jit(solution)/shard_map/ppermute | solution.py:16
  51.8 12.3 %shard_map.98 = (f32[1848,1024]{1,0:T(8,128)}, f32[1848,1024]{1,0:T(8,128)}, f32[1848,1024]{1,0:T(8,128)}, bf16[888,1024]{1,0:T(8,128)(2,1)S(1)}) custom-call(s32[3]{0:T(128)S(1)} %shard_map.96.place_ref.refs_0_, bf16[256,1024]{1,0:T(8,128)(2,1)S(1)} %constant_dynamic-slice_fusion.1.refs_6_.own_ref, ...), custom_call_target="tpu_custom_call", output_to_operand_aliasing={{0}: (12, {}), {1}: (13, {}), {2}: (14, {})} | custom-call | tf_op jit(solution)/shard_map/pallas_call | solution.py:121
  65.7 5.9 %collective-permute-done.10.refs_2_.refs_0_ = bf16[2,1848,256]{2,1,0:T(8,128)(2,1)S(1)} collective-permute-done((bf16[2,1848,256]{2,1,0:T(8,128)(2,1)S(1)}, bf16[2,1848,256]{2,1,0:T(8,128)(2,1)S(1)}, u32[]{:S(2)}, u32[]{:S(2)}) %collective-permute-start.10) | collective-permute-done | bytes 1892384 | tf_op jit(solution)/shard_map/ppermute | solution.py:16
  71.6 3.6 %shard_map.103 = (bf16[128,1024]{1,0:T(8,128)(2,1)S(1)}, bf16[128,1024]{1,0:T(8,128)(2,1)S(1)}) custom-call(s32[3]{0:T(128)S(1)} %shard_map.100.place_ref, bf16[1848,256]{1,0:T(8,128)(2,1)} %collective-permute-done.refs_1_.refs_0_, bf16[1848,256]{1,0:T(8,128)(2,1)S(1)} %collective-permute-done.8.refs_1_, ...), custom_call_target="tpu_custom_call" | custom-call | tf_op jit(solution)/shard_map/pallas_call | solution.py:186
  75.2 1.4 %collective-permute-start.16 = (bf16[128,1024]{1,0:T(8,128)(2,1)S(1)}, bf16[128,1024]{1,0:T(8,128)(2,1)S(1)}, u32[]{:S(2)}, u32[]{:S(2)}) collective-permute-start(bf16[128,1024]{1,0:T(8,128)(2,1)S(1)} %get-tuple-element.67), channel_id=1, source_target_pairs={{0,8},{4,12},{8,0},{12,4},{16,24},{20,28},{24,16},{28,20},{1,9},{5... | collective-permute-start | bytes 786440 | tf_op jit(solution)/shard_map/ppermute | solution.py:16
  76.6 1.5 %collective-permute-start.14 = (bf16[128,1024]{1,0:T(8,128)(2,1)S(1)}, bf16[128,1024]{1,0:T(8,128)(2,1)S(1)}, u32[]{:S(2)}, u32[]{:S(2)}) collective-permute-start(bf16[128,1024]{1,0:T(8,128)(2,1)S(1)} %get-tuple-element.64), channel_id=1, source_target_pairs={{0,16},{4,20},{8,24},{12,28},{16,0},{20,4},{24,8},{28,12},{1,17},{... | collective-permute-start | bytes 786440 | tf_op jit(solution)/shard_map/ppermute | solution.py:16
  78.1 2.9 %shard_map.105 = (f32[128,1024]{1,0:T(8,128)S(1)}, f32[128,1024]{1,0:T(8,128)S(1)}) custom-call(s32[3]{0:T(128)S(1)} %shard_map.100.place_ref, bf16[2,1848,256]{2,1,0:T(8,128)(2,1)S(1)} %collective-permute-done.10.refs_2_.refs_0_, bf16[960,1024]{1,0:T(8,128)(2,1)S(1)} %get-tuple-element.58.refs_1_.refs_3_.refs_2_, ...), custom_call_target="tpu_custom_call" | custom-call | tf_op jit(solution)/shard_map/pallas_call | solution.py:186
  81.0 3.5 %shard_map.102 = (f32[128,1024]{1,0:T(8,128)S(1)}, f32[128,1024]{1,0:T(8,128)S(1)}) custom-call(s32[3]{0:T(128)S(1)} %shard_map.100.place_ref, bf16[1152,256]{1,0:T(8,128)(2,1)} %collective-permute-done.7.refs_0_, bf16[1152,256]{1,0:T(8,128)(2,1)S(1)} %collective-permute-done.9.refs_1_, bf16[2,696,256]{2,1,0:T(8,128)(2,1)S(1)} %collective-permute-done.11.refs_3_.refs_2_, ...), custom_call_target="tpu_custom_call" | custom-call | tf_op jit(solution)/shard_map/pallas_call | solution.py:186
  86.0 2.9 %shard_map.101 = (f32[128,1024]{1,0:T(8,128)S(1)}, f32[128,1024]{1,0:T(8,128)S(1)}) custom-call(s32[3]{0:T(128)S(1)} %shard_map.100.place_ref, bf16[2,1848,256]{2,1,0:T(8,128)(2,1)S(1)} %get-tuple-element.68.refs_0_, bf16[960,1024]{1,0:T(8,128)(2,1)S(1)} %get-tuple-element.58.refs_1_.refs_3_.refs_2_, ...), custom_call_target="tpu_custom_call" | custom-call | flops 1937768448 | bytes 7569408 | tf_op jit(solution)/shard_map/pallas_call | solution.py:186
  89.0 5.8 %collective-permute-done.17 = bf16[256,1024]{1,0:T(8,128)(2,1)S(1)} collective-permute-done((bf16[256,1024]{1,0:T(8,128)(2,1)S(1)}, bf16[256,1024]{1,0:T(8,128)(2,1)S(1)}, u32[]{:S(2)}, u32[]{:S(2)}) %collective-permute-start.17) | collective-permute-done | bytes 524320 | tf_op jit(solution)/shard_map/ppermute | solution.py:16
  (39 shorter events, 8.7 us)
Async XLA Ops:
  3.9 26.1 %collective-permute-start = (bf16[1848,256]{1,0:T(8,128)(2,1)}, bf16[1848,256]{1,0:T(8,128)(2,1)}, u32[]{:S(2)}, u32[]{:S(2)}) collective-permute-start(bf16[1848,256]{1,0:T(8,128)(2,1)} %get-tuple-element.36.refs_1_), channel_id=1, source_target_pairs={{0,24},{4,28},{8,16},{12,20},{16,8},{20,12},{24,0},{28,4},{1,25},{... | collective-permute-start | bytes 2838536 | tf_op jit(solution)/shard_map/ppermute | solution.py:16
  7.8 24.1 %collective-permute-start.1 = (bf16[128,1024]{1,0:T(8,128)(2,1)}, bf16[128,1024]{1,0:T(8,128)(2,1)S(1)}, u32[]{:S(2)}, u32[]{:S(2)}) collective-permute-start(bf16[128,1024]{1,0:T(8,128)(2,1)} %get-tuple-element.37.refs_2_), channel_id=1, source_target_pairs={{0,1},{1,0},{2,3},{3,2},{4,5},{5,4},{6,7},{7,6},{8,9},{9,8},{10,11... | collective-permute-start | bytes 786440 | tf_op jit(solution)/shard_map/ppermute | solution.py:16
  9.4 24.1 %collective-permute-start.2 = (bf16[128,1024]{1,0:T(8,128)(2,1)}, bf16[128,1024]{1,0:T(8,128)(2,1)}, u32[]{:S(2)}, u32[]{:S(2)}) collective-permute-start(bf16[128,1024]{1,0:T(8,128)(2,1)} %get-tuple-element.38.refs_3_), channel_id=1, source_target_pairs={{0,2},{1,3},{2,0},{3,1},{4,6},{5,7},{6,4},{7,5},{8,10},{9,11},{10,... | collective-permute-start | bytes 786440 | tf_op jit(solution)/shard_map/ppermute | solution.py:16
  12.0 21.6 %collective-permute-start.3 = (bf16[128,1024]{1,0:T(8,128)(2,1)}, bf16[128,1024]{1,0:T(8,128)(2,1)}, u32[]{:S(2)}, u32[]{:S(2)}) collective-permute-start(bf16[128,1024]{1,0:T(8,128)(2,1)} %get-tuple-element.39.refs_4_), channel_id=1, source_target_pairs={{0,3},{1,2},{2,1},{3,0},{4,7},{5,6},{6,5},{7,4},{8,11},{9,10},{10,... | collective-permute-start | bytes 786440 | tf_op jit(solution)/shard_map/ppermute | solution.py:16
  14.2 35.6 %collective-permute-start.7 = (bf16[1152,256]{1,0:T(8,128)(2,1)}, bf16[1152,256]{1,0:T(8,128)(2,1)}, u32[]{:S(2)}, u32[]{:S(2)}) collective-permute-start(bf16[1152,256]{1,0:T(8,128)(2,1)} %dynamic-slice_bitcast_fusion.refs_1_), channel_id=1, source_target_pairs={{0,8},{4,12},{8,0},{12,4},{16,24},{20,28},{24,16},{28,20},{1,9},{5... | collective-permute-start | bytes 1769480 | tf_op jit(solution)/shard_map/ppermute | solution.py:16
  16.4 8.3 %copy-start = (bf16[960,1024]{1,0:T(8,128)(2,1)}, bf16[960,1024]{1,0:T(8,128)(2,1)S(1)}, u32[]{:S(2)}) copy-start(bf16[960,1024]{1,0:T(8,128)(2,1)S(1)} %slice.14.refs_4_.refs_6_) | copy-start | bytes 5898244
  22.2 2.6 %copy-start.1 = (bf16[888,1024]{1,0:T(8,128)(2,1)S(1)}, bf16[888,1024]{1,0:T(8,128)(2,1)}, u32[]{:S(2)}) copy-start(bf16[888,1024]{1,0:T(8,128)(2,1)} %slice.15.refs_5_.refs_6_) | copy-start | bytes 5455876
  30.0 41.6 %collective-permute-start.10 = (bf16[2,1848,256]{2,1,0:T(8,128)(2,1)S(1)}, bf16[2,1848,256]{2,1,0:T(8,128)(2,1)S(1)}, u32[]{:S(2)}, u32[]{:S(2)}) collective-permute-start(bf16[2,1848,256]{2,1,0:T(8,128)(2,1)S(1)} %get-tuple-element.69.refs_3_), channel_id=1, source_target_pairs={{0,16},{4,20},{8,24},{12,28},{16,0},{20,4},{24,8},{28,12},{1,17},{... | collective-permute-start | bytes 5677064 | tf_op jit(solution)/shard_map/ppermute | solution.py:16
  32.0 32.1 %collective-permute-start.8 = (bf16[1848,256]{1,0:T(8,128)(2,1)}, bf16[1848,256]{1,0:T(8,128)(2,1)S(1)}, u32[]{:S(2)}, u32[]{:S(2)}) collective-permute-start(bf16[1848,256]{1,0:T(8,128)(2,1)} %collective-permute-done.refs_1_.refs_0_), channel_id=1, source_target_pairs={{0,1},{1,0},{2,3},{3,2},{4,5},{5,4},{6,7},{7,6},{8,9},{9,8},{10,11... | collective-permute-start | bytes 2838536 | tf_op jit(solution)/shard_map/ppermute | solution.py:16
  33.6 1.5 %collective-permute-start.4 = (bf16[128,1024]{1,0:T(8,128)(2,1)S(1)}, bf16[128,1024]{1,0:T(8,128)(2,1)S(1)}, u32[]{:S(2)}, u32[]{:S(2)}) collective-permute-start(bf16[128,1024]{1,0:T(8,128)(2,1)S(1)} %collective-permute-done.1.refs_0_), channel_id=1, source_target_pairs={{0,4},{4,0},{8,12},{12,8},{16,20},{20,16},{24,28},{28,24},{1,5},{5... | collective-permute-start | bytes 786440 | tf_op jit(solution)/shard_map/ppermute | solution.py:16
  33.6 2.1 %collective-permute-start.5 = (bf16[128,1024]{1,0:T(8,128)(2,1)}, bf16[128,1024]{1,0:T(8,128)(2,1)S(1)}, u32[]{:S(2)}, u32[]{:S(2)}) collective-permute-start(bf16[128,1024]{1,0:T(8,128)(2,1)} %collective-permute-done.2.refs_1_), channel_id=1, source_target_pairs={{0,4},{4,0},{8,12},{12,8},{16,20},{20,16},{24,28},{28,24},{1,5},{5... | collective-permute-start | bytes 786440 | tf_op jit(solution)/shard_map/ppermute | solution.py:16
  35.1 2.1 %collective-permute-start.6 = (bf16[128,1024]{1,0:T(8,128)(2,1)}, bf16[128,1024]{1,0:T(8,128)(2,1)S(1)}, u32[]{:S(2)}, u32[]{:S(2)}) collective-permute-start(bf16[128,1024]{1,0:T(8,128)(2,1)} %collective-permute-done.3.refs_2_), channel_id=1, source_target_pairs={{0,4},{4,0},{8,12},{12,8},{16,20},{20,16},{24,28},{28,24},{1,5},{5... | collective-permute-start | bytes 786440 | tf_op jit(solution)/shard_map/ppermute | solution.py:16
  35.7 29.0 %collective-permute-start.11 = (bf16[2,696,256]{2,1,0:T(8,128)(2,1)S(1)}, bf16[2,696,256]{2,1,0:T(8,128)(2,1)S(1)}, u32[]{:S(2)}, u32[]{:S(2)}) collective-permute-start(bf16[2,696,256]{2,1,0:T(8,128)(2,1)S(1)} %constant_dynamic-slice_fusion.3.refs_2_), channel_id=1, source_target_pairs={{0,8},{4,12},{8,0},{12,4},{16,24},{20,28},{24,16},{28,20},{1,9},{5... | collective-permute-start | bytes 2138120 | tf_op jit(solution)/shard_map/ppermute | solution.py:16
  49.8 15.9 %collective-permute-start.9 = (bf16[1152,256]{1,0:T(8,128)(2,1)}, bf16[1152,256]{1,0:T(8,128)(2,1)S(1)}, u32[]{:S(2)}, u32[]{:S(2)}) collective-permute-start(bf16[1152,256]{1,0:T(8,128)(2,1)} %collective-permute-done.7.refs_0_), channel_id=1, source_target_pairs={{0,1},{1,0},{2,3},{3,2},{4,5},{5,4},{6,7},{7,6},{8,9},{9,8},{10,11... | collective-permute-start | bytes 1769480 | tf_op jit(solution)/shard_map/ppermute | solution.py:16
  51.8 19.7 %collective-permute-start.12 = (bf16[960,1024]{1,0:T(8,128)(2,1)S(1)}, bf16[960,1024]{1,0:T(8,128)(2,1)S(1)}, u32[]{:S(2)}, u32[]{:S(2)}) collective-permute-start(bf16[960,1024]{1,0:T(8,128)(2,1)S(1)} %get-tuple-element.58.refs_1_.refs_3_.refs_2_), channel_id=1, source_target_pairs={{0,4},{4,0},{8,12},{12,8},{16,20},{20,16},{24,28},{28,24},{1,5},{5... | collective-permute-start | bytes 5898248 | tf_op jit(solution)/shard_map/ppermute | solution.py:16
  64.1 7.4 %collective-permute-start.13 = (bf16[888,1024]{1,0:T(8,128)(2,1)S(1)}, bf16[888,1024]{1,0:T(8,128)(2,1)S(1)}, u32[]{:S(2)}, u32[]{:S(2)}) collective-permute-start(bf16[888,1024]{1,0:T(8,128)(2,1)S(1)} %get-tuple-element.59.refs_2_.refs_4_.refs_3_), channel_id=1, source_target_pairs={{0,4},{4,0},{8,12},{12,8},{16,20},{20,16},{24,28},{28,24},{1,5},{5... | collective-permute-start | bytes 5455880 | tf_op jit(solution)/shard_map/ppermute | solution.py:16
  75.2 9.4 %collective-permute-start.16 = (bf16[128,1024]{1,0:T(8,128)(2,1)S(1)}, bf16[128,1024]{1,0:T(8,128)(2,1)S(1)}, u32[]{:S(2)}, u32[]{:S(2)}) collective-permute-start(bf16[128,1024]{1,0:T(8,128)(2,1)S(1)} %get-tuple-element.67), channel_id=1, source_target_pairs={{0,8},{4,12},{8,0},{12,4},{16,24},{20,28},{24,16},{28,20},{1,9},{5... | collective-permute-start | bytes 786440 | tf_op jit(solution)/shard_map/ppermute | solution.py:16
  76.6 8.6 %collective-permute-start.14 = (bf16[128,1024]{1,0:T(8,128)(2,1)S(1)}, bf16[128,1024]{1,0:T(8,128)(2,1)S(1)}, u32[]{:S(2)}, u32[]{:S(2)}) collective-permute-start(bf16[128,1024]{1,0:T(8,128)(2,1)S(1)} %get-tuple-element.64), channel_id=1, source_target_pairs={{0,16},{4,20},{8,24},{12,28},{16,0},{20,4},{24,8},{28,12},{1,17},{... | collective-permute-start | bytes 786440 | tf_op jit(solution)/shard_map/ppermute | solution.py:16
  84.6 10.2 %collective-permute-start.17 = (bf16[256,1024]{1,0:T(8,128)(2,1)S(1)}, bf16[256,1024]{1,0:T(8,128)(2,1)S(1)}, u32[]{:S(2)}, u32[]{:S(2)}) collective-permute-start(bf16[256,1024]{1,0:T(8,128)(2,1)S(1)} %shard_map.106), channel_id=1, source_target_pairs={{0,16},{4,20},{8,24},{12,28},{16,0},{20,4},{24,8},{28,12},{1,17},{... | collective-permute-start | bytes 1572872 | tf_op jit(solution)/shard_map/ppermute | solution.py:16
  85.3 9.9 %collective-permute-start.15 = (bf16[256,1024]{1,0:T(8,128)(2,1)S(1)}, bf16[256,1024]{1,0:T(8,128)(2,1)S(1)}, u32[]{:S(2)}, u32[]{:S(2)}) collective-permute-start(bf16[256,1024]{1,0:T(8,128)(2,1)S(1)} %shard_map.104), channel_id=1, source_target_pairs={{0,8},{4,12},{8,0},{12,4},{16,24},{20,28},{24,16},{28,20},{1,9},{5... | collective-permute-start | bytes 1572872 | tf_op jit(solution)/shard_map/ppermute | solution.py:16

commit v5 on v4

--- a/solution.py
+++ b/solution.py
@@ -51,11 +51,13 @@
     return out[: len(masks)], out[len(masks) :]
 
 
-def adam_kernel(planes, scale, cuts, waits, place_ref, own_ref, *refs):
+def adam_kernel(planes, scale, cuts, parts, waits, place_ref, own_ref, *refs):
     crossed = planes - 1
     fetched_refs, swapped_refs = refs[:crossed], refs[crossed : 2 * crossed]
     hidden_ref, *state_refs = refs[2 * crossed : 2 * crossed + 4]
-    *out_refs, weights_ref, columns_ref, rows_ref, held_ref, row_sem, in_sems, out_sems = refs[2 * crossed + 4 + waits :]
+    refs = refs[2 * crossed + 4 + waits :]
+    out_refs, weights_refs = refs[:3], refs[3 : 3 + parts]
+    columns_ref, rows_ref, held_ref, row_sem, in_sems, out_sems = refs[3 + parts :]
     base = cuts[0]
     rows_copy = pltpu.make_async_copy(hidden_ref, rows_ref, row_sem)
     copies_in, copies_out = [], []
@@ -101,7 +103,8 @@
         new_first = 0.9 * held_ref[1, here] + 0.1 * grad
         new_second = 0.95 * held_ref[2, here] + 0.05 * grad * grad
         new_master = held_ref[0, here] - 0.002 * new_first / (jnp.sqrt(new_second) + 1e-08)
-        weights_ref[here] = new_master.astype(jnp.bfloat16)
+        part, at = divmod(low - base, weights_refs[0].shape[0])
+        weights_refs[part][at : at + high - low] = new_master.astype(jnp.bfloat16)
         for k, new in enumerate((new_master, new_first, new_second)):
             held_ref[k, here] = new
             copies_out[i][k].start()
@@ -110,7 +113,7 @@
             copy.wait()
 
 
-def adam(place, planes, hidden, own, fetched, swapped, state, cuts, before):
+def adam(place, planes, hidden, own, fetched, swapped, state, cuts, parts, before):
     count, tokens_all = hidden.shape
     rows, width = state[0].shape
     full = pltpu.HBM((rows, width), jnp.float32)
@@ -119,10 +122,10 @@
     near = [own, *fetched, *swapped]
     far = [pltpu.with_memory_space_constraint(x, pltpu.HBM) for x in (hidden, *state, *before)]
     return pl.pallas_call(
-        functools.partial(adam_kernel, planes, 1.0 / math.sqrt(tokens_all), cuts, len(before)),
-        out_shape=[full] * 3 + [jax.ShapeDtypeStruct((count, width), jnp.bfloat16)],
+        functools.partial(adam_kernel, planes, 1.0 / math.sqrt(tokens_all), cuts, parts, len(before)),
+        out_shape=[full] * 3 + [jax.ShapeDtypeStruct((count // parts, width), jnp.bfloat16)] * parts,
         in_specs=[pl.BlockSpec(memory_space=pltpu.SMEM)] + [inside] * len(near) + [outside] * len(far),
-        out_specs=[outside] * 3 + [inside],
+        out_specs=[outside] * 3 + [inside] * parts,
         scratch_shapes=[
             pltpu.VMEM((tokens_all, width), jnp.bfloat16),
             pltpu.VMEM((count, tokens_all), jnp.bfloat16),
@@ -193,6 +196,40 @@
     )(place, *operands)
 
 
+def products_kernel(count, parts, place_ref, *refs):
+    held_refs, out_refs = refs[:count], refs[count + 2 * parts :]
+    own_refs, other_refs = refs[count : count + parts], refs[count + parts : count + 2 * parts]
+    core = place_ref[1]
+    half = out_refs[0].shape[0]
+    for first in range(0, count, 2):
+        pair_refs = held_refs[first : first + 2]
+        total = 0.0
+        for weights_refs, of_core in ((own_refs, core), (other_refs, 1 - core)):
+            at = 0
+            for ref in weights_refs:
+                rows = slice(at, at + ref.shape[0])
+                held = jnp.concatenate([held_ref[of_core, rows] for held_ref in pair_refs], axis=1)
+                total = total + lax.dot_general(held, ref[...], OVER_FIRST, preferred_element_type=jnp.float32)
+                at += ref.shape[0]
+        for i in range(2 * len(pair_refs)):
+            out_refs[2 * first + i][...] = total[i * half : (i + 1) * half]
+
+
+def products(place, held, own, other):
+    width, rows = own[0].shape[1], held[0].shape[-1]
+    operands = [pltpu.with_memory_space_constraint(x, pltpu.VMEM) for x in (*held, *own, *other)]
+    inside = pl.BlockSpec(memory_space=pltpu.VMEM)
+    out = pl.pallas_call(
+        functools.partial(products_kernel, len(held), len(own)),
+        out_shape=[jax.ShapeDtypeStruct((rows // 2, width), jnp.float32)] * (2 * len(held)),
+        in_specs=[pl.BlockSpec(memory_space=pltpu.SMEM)] + [inside] * len(operands),
+        out_specs=[inside] * (2 * len(held)),
+        compiler_params=pltpu.CompilerParams(vmem_limit_bytes=20 * 1024 * 1024),
+        cost_estimate=FREE,
+    )(place, *operands)
+    return [out[2 * i : 2 * i + 2] for i in range(len(held))]
+
+
 def add_kernel(lows, mine_low_ref, mine_high_ref, *refs):
     half = mine_low_ref.shape[0]
     low, high = mine_low_ref[...], mine_high_ref[...]
@@ -263,22 +300,18 @@
     pieces = [xor_permute(piece, "tensor", planes, mask + 1) for mask, piece in enumerate(column_cuts)]
     token = hold(token, *far_cuts, *column_cuts)
 
-    first = block * 5 // 8 // 16 * 16
-
-    def straight_part(mask, low):
-        return lax.dynamic_slice(windows, ((chip ^ mask) * 2, low, 0), (2, block - low, rows))
+    def both_parts(mask):
+        return lax.dynamic_slice(windows, ((chip ^ mask) * 2, 0, 0), (2, block, rows))
 
     token, (windows, train) = after(token, (windows, train_hidden.T))
     own_columns = lax.dynamic_slice(out_grad, (0, plane * width), (tokens, width))
     cuts = [*range(0, block, min(160, block)), block]
-    middle = cuts[len(cuts) // 2] if len(cuts) > 2 else block
-    trains = [train[:middle], train[middle:]]
-    near_cut = part(near, core ^ parity)[:first]
-    side_cuts = {mask: straight_part(mask, 0) for mask in sides}
-    rest_cut = straight_part(near, first)
-    shared[near] = to_peer(near_cut, near)
-    straight = {mask: to_peer(piece, mask) for mask, piece in side_cuts.items()}
-    token = hold(token, near_cut, rest_cut, *side_cuts.values(), *trains, own_columns)
+    middle = cuts[len(cuts) * 2 // 3] if len(cuts) > 2 else block
+    parts = 2 if middle % (2 * cuts[1]) == 0 else 1
+    trains = [train[:middle], train[middle:]] if middle < block else [train]
+    straight_cuts = {mask: both_parts(mask) for mask in (near, *sides)}
+    straight = {mask: to_peer(piece, mask) for mask, piece in straight_cuts.items()}
+    token = hold(token, *straight_cuts.values(), *trains, own_columns)
 
     passed = {}
     for mask in fars:
@@ -286,41 +319,39 @@
         passed[mask] = xor_permute(shared[mask], "tensor", planes, 1)
     token = hold(token, *(shared[mask] for mask in fars))
 
-    token, (pieces, rest_cut) = after(token, (pieces, rest_cut))
-    straight[near] = to_peer(rest_cut, near)
+    token, pieces = after(token, pieces)
     swapped = [to_peer(piece, 0, 1) for piece in pieces]
     state = (master, first_moment, second_moment)
     def step(at, before):
         rows = [cut for cut in cuts if (cut <= middle if at == 0 else cut >= middle)]
-        return list(adam(token, planes, trains[at], own_columns, pieces, swapped, state, rows, before))
+        return list(adam(token, planes, trains[at], own_columns, pieces, swapped, state, rows, parts if at == 0 else 1, before))
 
     out = step(0, [])
-    weights = [out[3]]
-    shared[near], out[0] = lax.optimization_barrier((shared[near], out[0]))
-    passed[near] = xor_permute(shared[near], "tensor", planes, 1)
+    weights = out[3:]
     if middle < block:
         out = step(1, out[:3])
         weights.append(out[3])
     new_master, new_first, new_second = out[:3]
 
     other = [to_peer(array, 0, 1) for array in weights]
-    token = hold(token, *(passed[mask] for mask in fars), flops=2 * 10**9)
-    token = hold(token, passed[near], *straight.values(), flops=10**11)
+    far_token = hold(token, *(passed[mask] for mask in fars), flops=8 * 10**9)
+    token = hold(token, *straight.values(), flops=35 * 10**8)
 
     low = {near: [], **{mask: [] for mask in sides}}
     high = {near: [], **{mask: [] for mask in sides}}
     for mask in fars:
-        out = product(token, (shared[mask], passed[mask]), (), weights, other, jnp.bfloat16, FREE)
+        out = product(far_token, (shared[mask], passed[mask]), (), weights, other, jnp.bfloat16, FREE)
         low[mask ^ near].append(to_peer(out[0], near))
         high[near].append(to_peer(out[1], mask ^ near))
     back = []
-    for mask in (near, *sides):
-        crossed = (shared[near], passed[near]) if mask == near else ()
-        out = product(token, crossed, (straight[mask],), weights, other, jnp.float32, FREE)
+    order = (near, *sides)
+    outs = []
+    for at in range(0, len(order), 2):
+        outs += products(token, [straight[mask] for mask in order[at : at + 2]], weights, other)
+    for mask, out in zip(order, outs, strict=True):
         back.append(to_peer(add(out, low[mask], high[mask]), mask))
     cost = pl.CostEstimate(flops=4 * rows * block * width, bytes_accessed=4 * block * width, transcendentals=0)
-    mine = lax.dynamic_slice(windows, (chip * 2, 0, 0), (2, block, rows))
-    total = product(token, (), (mine,), weights, other, jnp.float32, cost)
+    total = product(token, (), (both_parts(0),), weights, other, jnp.float32, cost)
     total = lax.optimization_barrier(jnp.concatenate(total, axis=0))
     for sums in back:
         total = total + sums.astype(jnp.float32)

time: 96.8 us -> 93.7 us (0.968)
  local copies, waits for them, and re-layouts: 12.1 us -> 9.21 us
  starting transfers between devices: 21.5 us -> 19.4 us
  waiting for transfers between devices: 19.6 us -> 20.7 us
  Pallas kernels: 41 us -> 42 us
    pallas_call x0 -> x1, Pallas kernels: none -> 6.61 us  [products(): pl.pallas_call(functools.partial(products_kernel, len(held), len(own)), o...]
    slice x3 -> x2, local copies, waits for them, and re-layouts: 7.2 us -> 1.44 us  [per_device(): trains = [train[:middle], train[middle:]] if middle < block else [train]]
    pallas_call x4 -> x2, Pallas kernels: 12.9 us -> 7.26 us  [product(): pl.pallas_call(functools.partial(product_kernel, bool(crossed), len(own))...]
    ppermute x18 -> x17, starting transfers between devices: 21.5 us -> 19.4 us  [xor_permute(): return lax.ppermute(array, axis, [(i, i ^ mask) for i in range(size)])]
    dynamic_slice x2 -> x1, local copies, waits for them, and re-layouts: 3.62 us -> 5.36 us  [both_parts(): lax.dynamic_slice(windows, ((chip ^ mask) * 2, 0, 0), (2, block, rows))]
    unnamed x4 -> x9, local copies, waits for them, and re-layouts: 0.15 us -> 1.27 us
    ppermute x18 -> x17, waiting for transfers between devices: 19.6 us -> 20.7 us  [xor_permute(): return lax.ppermute(array, axis, [(i, i ^ mask) for i in range(size)])]
  transfers between devices with their start and end apart: 18 -> 17, of which waited for: 7 -> 8; matrix products, arithmetic and copies ran while one was open for 12% -> 9% of each run, Pallas kernels for 36% -> 42%
where the time goes in v5:
time: 93.7 us; the launch traced here: 93.3 us
  Pallas kernels  42 us (45%)
  waiting for transfers between devices  20.7 us (22%)
  starting transfers between devices  19.4 us (21%)
  local copies, waits for them, and re-layouts  9.21 us (10%)
  other arithmetic  1.22 us (1%)
    pallas_call x2, Pallas kernels, adam(): pl.pallas_call(functools.partial(adam_kernel, planes, 1.0 / math.sqrt(tok...  24.9 us
    ppermute x17, waiting for transfers between devices, xor_permute(): return lax.ppermute(array, axis, [(i, i ^ mask) for i in range(size)])  20.7 us
    ppermute x17, starting transfers between devices, xor_permute(): return lax.ppermute(array, axis, [(i, i ^ mask) for i in range(size)])  19.4 us
    pallas_call x2, Pallas kernels, product(): pl.pallas_call(functools.partial(product_kernel, bool(crossed), len(own))...  7.26 us
    pallas_call x1, Pallas kernels, products(): pl.pallas_call(functools.partial(products_kernel, len(held), len(own)), o...  6.61 us
    dynamic_slice x1, local copies, waits for them, and re-layouts, both_parts(): lax.dynamic_slice(windows, ((chip ^ mask) * 2, 0, 0), (2, block, rows))  5.36 us
    pallas_call x1, Pallas kernels, cut(): pl.pallas_call(functools.partial(cut_kernel, planes, masks), out_shape=[p...  3.08 us
  transfers between devices with their start and end apart: 17, of which 8 were waited for; matrix products, arithmetic and copies ran while one was open for 9% of the time, Pallas kernels for 42%

profile of v5, /device:TPU:0, one launch (start us, length us, event | category | flops | bytes accessed | tf_op | source)
XLA Modules:
  0.0 93.3 jit_solution(16199550585985901146)
XLA Ops:
  0.7 3.1 %shard_map.93 = (bf16[1848,256]{1,0:T(8,128)(2,1)}, bf16[128,1024]{1,0:T(8,128)(2,1)S(1)}, bf16[128,1024]{1,0:T(8,128)(2,1)}, bf16[128,1024]{1,0:T(8,128)(2,1)}) custom-call(s32[3]{0:T(128)S(1)} %pad_add_fusion.place_ref.refs_0_, bf16[8,1848,256]{2,1,0:T(8,128)(2,1)} %bitcast.7, bf16[256,4096]{1,0:T(8,128)(2,1)} %out_grad_ref.1), custom_call_target="tpu_custom_call" | custom-call | tf_op jit(solution)/shard_map/pallas_call | solution.py:41
  3.8 4.0 %collective-permute-start = (bf16[1848,256]{1,0:T(8,128)(2,1)}, bf16[1848,256]{1,0:T(8,128)(2,1)}, u32[]{:S(2)}, u32[]{:S(2)}) collective-permute-start(bf16[1848,256]{1,0:T(8,128)(2,1)} %get-tuple-element.34.refs_1_), channel_id=1, source_target_pairs={{0,24},{4,28},{8,16},{12,20},{16,8},{20,12},{24,0},{28,4},{1,25},{... | collective-permute-start | bytes 2838536 | tf_op jit(solution)/shard_map/ppermute | solution.py:16
  7.8 1.6 %collective-permute-start.1 = (bf16[128,1024]{1,0:T(8,128)(2,1)S(1)}, bf16[128,1024]{1,0:T(8,128)(2,1)S(1)}, u32[]{:S(2)}, u32[]{:S(2)}) collective-permute-start(bf16[128,1024]{1,0:T(8,128)(2,1)S(1)} %get-tuple-element.35.refs_2_), channel_id=1, source_target_pairs={{0,1},{1,0},{2,3},{3,2},{4,5},{5,4},{6,7},{7,6},{8,9},{9,8},{10,11... | collective-permute-start | bytes 786440 | tf_op jit(solution)/shard_map/ppermute | solution.py:16
  9.3 2.6 %collective-permute-start.2 = (bf16[128,1024]{1,0:T(8,128)(2,1)}, bf16[128,1024]{1,0:T(8,128)(2,1)}, u32[]{:S(2)}, u32[]{:S(2)}) collective-permute-start(bf16[128,1024]{1,0:T(8,128)(2,1)} %get-tuple-element.36.refs_3_), channel_id=1, source_target_pairs={{0,2},{1,3},{2,0},{3,1},{4,6},{5,7},{6,4},{7,5},{8,10},{9,11},{10,... | collective-permute-start | bytes 786440 | tf_op jit(solution)/shard_map/ppermute | solution.py:16
  12.1 5.4 %constant_dynamic-slice_fusion = (bf16[2,1848,256]{2,1,0:T(8,128)(2,1)}, bf16[2,1848,256]{2,1,0:T(8,128)(2,1)}, bf16[2,1848,256]{2,1,0:T(8,128)(2,1)}) fusion(bf16[8,1848,256]{2,1,0:T(8,128)(2,1)} %bitcast.8, s32[]{:T(128)S(6)} %select_n.15, s32[]{:T(128)S(6)} %select_n.13, s32[]{:T(128)S(6)} %select_n.12), kind=kLoop, calls=%fused_computation.2 | loop fusion | bytes 11354124 | tf_op jit(solution)/shard_map/dynamic_slice | solution.py:304
  18.3 1.2 %slice.7.refs_4_.refs_6_ = bf16[568,1024]{1,0:T(8,128)(2,1)} slice(bf16[1848,1024]{1,0:T(8,128)(2,1)S(1)} %bitcast.10), slice={[1280:1848], [0:1024]} | slice | bytes 2326528 | tf_op jit(solution)/shard_map/slice | solution.py:311
  19.5 1.1 %constant_dynamic-slice_fusion.1.refs_5_.own_ref = bf16[256,1024]{1,0:T(8,128)(2,1)S(1)} fusion(bf16[256,4096]{1,0:T(8,128)(2,1)} %out_grad_ref.1, s32[]{:T(128)S(6)} %select_n.14), kind=kLoop, calls=%fused_computation.3 | loop fusion | bytes 1048580 | tf_op jit(solution)/shard_map/dynamic_slice | solution.py:307
  20.6 1.3 %copy-done.2 = bf16[568,1024]{1,0:T(8,128)(2,1)S(1)} copy-done((bf16[568,1024]{1,0:T(8,128)(2,1)S(1)}, bf16[568,1024]{1,0:T(8,128)(2,1)}, u32[]{:S(2)}) %copy-start.2) | copy-done | bytes 1163288
  21.9 8.0 %collective-permute-done.refs_1_.refs_0_ = bf16[1848,256]{1,0:T(8,128)(2,1)} collective-permute-done((bf16[1848,256]{1,0:T(8,128)(2,1)}, bf16[1848,256]{1,0:T(8,128)(2,1)}, u32[]{:S(2)}, u32[]{:S(2)}) %collective-permute-start) | collective-permute-done | bytes 946208 | tf_op jit(solution)/shard_map/ppermute | solution.py:16
  29.9 2.0 %collective-permute-start.8 = (bf16[2,1848,256]{2,1,0:T(8,128)(2,1)}, bf16[2,1848,256]{2,1,0:T(8,128)(2,1)S(1)}, u32[]{:S(2)}, u32[]{:S(2)}) collective-permute-start(bf16[2,1848,256]{2,1,0:T(8,128)(2,1)} %get-tuple-element.65.refs_2_), channel_id=1, source_target_pairs={{0,16},{4,20},{8,24},{12,28},{16,0},{20,4},{24,8},{28,12},{1,17},{... | collective-permute-start | bytes 5677064 | tf_op jit(solution)/shard_map/ppermute | solution.py:16
  31.9 1.6 %collective-permute-start.12 = (bf16[1848,256]{1,0:T(8,128)(2,1)}, bf16[1848,256]{1,0:T(8,128)(2,1)S(1)}, u32[]{:S(2)}, u32[]{:S(2)}) collective-permute-start(bf16[1848,256]{1,0:T(8,128)(2,1)} %collective-permute-done.refs_1_.refs_0_), channel_id=1, source_target_pairs={{0,1},{1,0},{2,3},{3,2},{4,5},{5,4},{6,7},{7,6},{8,9},{9,8},{10,11... | collective-permute-start | bytes 2838536 | tf_op jit(solution)/shard_map/ppermute | solution.py:16
  34.0 1.0 %collective-permute-done.4.refs_3_ = bf16[128,1024]{1,0:T(8,128)(2,1)S(1)} collective-permute-done((bf16[128,1024]{1,0:T(8,128)(2,1)S(1)}, bf16[128,1024]{1,0:T(8,128)(2,1)S(1)}, u32[]{:S(2)}, u32[]{:S(2)}) %collective-permute-start.4) | collective-permute-done | bytes 262176 | tf_op jit(solution)/shard_map/ppermute | solution.py:16
  35.6 1.2 %collective-permute-done.6.refs_5_ = bf16[128,1024]{1,0:T(8,128)(2,1)S(1)} collective-permute-done((bf16[128,1024]{1,0:T(8,128)(2,1)}, bf16[128,1024]{1,0:T(8,128)(2,1)S(1)}, u32[]{:S(2)}, u32[]{:S(2)}) %collective-permute-start.6) | collective-permute-done | bytes 262176 | tf_op jit(solution)/shard_map/ppermute | solution.py:16
  36.8 15.5 %shard_map.97 = (f32[1848,1024]{1,0:T(8,128)}, f32[1848,1024]{1,0:T(8,128)}, f32[1848,1024]{1,0:T(8,128)}, bf16[640,1024]{1,0:T(8,128)(2,1)S(1)}, bf16[640,1024]{1,0:T(8,128)(2,1)S(1)}) custom-call(s32[3]{0:T(128)S(1)} %shard_map.96.place_ref.refs_0_, bf16[256,1024]{1,0:T(8,128)(2,1)S(1)} %constant_dynamic-slice_fusion.1.refs_5_.own_ref, ...), custom_call_target="tpu_custom_call" | custom-call | tf_op jit(solution)/shard_map/pallas_call | solution.py:124
  52.9 9.4 %shard_map.98 = (f32[1848,1024]{1,0:T(8,128)}, f32[1848,1024]{1,0:T(8,128)}, f32[1848,1024]{1,0:T(8,128)}, bf16[568,1024]{1,0:T(8,128)(2,1)S(1)}) custom-call(s32[3]{0:T(128)S(1)} %shard_map.96.place_ref.refs_0_, bf16[256,1024]{1,0:T(8,128)(2,1)S(1)} %constant_dynamic-slice_fusion.1.refs_5_.own_ref, ...), custom_call_target="tpu_custom_call", output_to_operand_aliasing={{0}: (12, {}), {1}: (13, {}), {2}: (14, {})} | custom-call | tf_op jit(solution)/shard_map/pallas_call | solution.py:124
  62.5 2.7 %collective-permute-done.11.refs_6_.refs_7_ = bf16[568,1024]{1,0:T(8,128)(2,1)S(1)} collective-permute-done((bf16[568,1024]{1,0:T(8,128)(2,1)S(1)}, bf16[568,1024]{1,0:T(8,128)(2,1)S(1)}, u32[]{:S(2)}, u32[]{:S(2)}) %collective-permute-start.11) | collective-permute-done | bytes 1163296 | tf_op jit(solution)/shard_map/ppermute | solution.py:16
  65.2 4.1 %shard_map.103 = (bf16[128,1024]{1,0:T(8,128)(2,1)S(1)}, bf16[128,1024]{1,0:T(8,128)(2,1)S(1)}) custom-call(s32[3]{0:T(128)S(1)} %shard_map.102.place_ref, bf16[1848,256]{1,0:T(8,128)(2,1)} %collective-permute-done.refs_1_.refs_0_, bf16[1848,256]{1,0:T(8,128)(2,1)S(1)} %collective-permute-done.12.refs_1_, ...), custom_call_target="tpu_custom_call" | custom-call | tf_op jit(solution)/shard_map/pallas_call | solution.py:189
  69.8 1.5 %collective-permute-start.15 = (bf16[128,1024]{1,0:T(8,128)(2,1)S(1)}, bf16[128,1024]{1,0:T(8,128)(2,1)S(1)}, u32[]{:S(2)}, u32[]{:S(2)}) collective-permute-start(bf16[128,1024]{1,0:T(8,128)(2,1)S(1)} %get-tuple-element.63), channel_id=1, source_target_pairs={{0,8},{4,12},{8,0},{12,4},{16,24},{20,28},{24,16},{28,20},{1,9},{5... | collective-permute-start | bytes 786440 | tf_op jit(solution)/shard_map/ppermute | solution.py:16
  71.7 6.6 %shard_map.101 = (f32[128,1024]{1,0:T(8,128)S(1)}, f32[128,1024]{1,0:T(8,128)S(1)}, f32[128,1024]{1,0:T(8,128)S(1)}, f32[128,1024]{1,0:T(8,128)S(1)}) custom-call(s32[3]{0:T(128)S(1)} %shard_map.99.place_ref, bf16[2,1848,256]{2,1,0:T(8,128)(2,1)} %collective-permute-done.7.refs_1_.refs_0_, bf16[2,1848,256]{2,1,0:T(8,128)(2,1)S(1)} %collective-permute-done.8.refs_2_.refs_1_, ...), custom_call_target="tpu_custom_call" | custom-call | tf_op jit(solution)/shard_map/pallas_call | solution.py:222
  78.4 1.4 %collective-permute-start.14 = (bf16[256,1024]{1,0:T(8,128)(2,1)S(1)}, bf16[256,1024]{1,0:T(8,128)(2,1)S(1)}, u32[]{:S(2)}, u32[]{:S(2)}) collective-permute-start(bf16[256,1024]{1,0:T(8,128)(2,1)S(1)} %shard_map.104), channel_id=1, source_target_pairs={{0,8},{4,12},{8,0},{12,4},{16,24},{20,28},{24,16},{28,20},{1,9},{5... | collective-permute-start | bytes 1572872 | tf_op jit(solution)/shard_map/ppermute | solution.py:16
  79.9 2.0 %collective-permute-start.16 = (bf16[256,1024]{1,0:T(8,128)(2,1)S(1)}, bf16[256,1024]{1,0:T(8,128)(2,1)S(1)}, u32[]{:S(2)}, u32[]{:S(2)}) collective-permute-start(bf16[256,1024]{1,0:T(8,128)(2,1)S(1)} %shard_map.105), channel_id=1, source_target_pairs={{0,16},{4,20},{8,24},{12,28},{16,0},{20,4},{24,8},{28,12},{1,17},{... | collective-permute-start | bytes 1572872 | tf_op jit(solution)/shard_map/ppermute | solution.py:16
  81.9 3.2 %shard_map.100 = (f32[128,1024]{1,0:T(8,128)S(1)}, f32[128,1024]{1,0:T(8,128)S(1)}) custom-call(s32[3]{0:T(128)S(1)} %shard_map.99.place_ref, bf16[2,1848,256]{2,1,0:T(8,128)(2,1)S(1)} %copy-done.1, bf16[640,1024]{1,0:T(8,128)(2,1)S(1)} %get-tuple-element.53.refs_1_.refs_2_, bf16[640,1024]{1,0:T(8,128)(2,1)S(1)} %get-tuple-element.54.refs_2_.refs_3_, ...), custom_call_target="tpu_custom_call" | custom-call | flops 1937768448 | bytes 7569408 | tf_op jit(solution)/shard_map/pallas_call | solution.py:189
  85.2 6.3 %collective-permute-done.14 = bf16[256,1024]{1,0:T(8,128)(2,1)S(1)} collective-permute-done((bf16[256,1024]{1,0:T(8,128)(2,1)S(1)}, bf16[256,1024]{1,0:T(8,128)(2,1)S(1)}, u32[]{:S(2)}, u32[]{:S(2)}) %collective-permute-start.14) | collective-permute-done | bytes 524320 | tf_op jit(solution)/shard_map/ppermute | solution.py:16
  92.3 1.0 %add_convert_fusion = bf16[256,1024]{1,0:T(8,128)(2,1)} fusion(bf16[256,1024]{1,0:T(8,128)(2,1)S(1)} %collective-permute-done.16, f32[256,1024]{1,0:T(8,128)S(1)} %pad_maximum_fusion, bf16[256,1024]{1,0:T(8,128)(2,1)S(1)} %collective-permute-done.14), kind=kLoop, calls=%fused_computation.1 | loop fusion | flops 1310720 | bytes 2621440 | tf_op jit(solution)/shard_map/convert_element_type | solution.py:358
  (39 shorter events, 4.9 us)
Async XLA Ops:
  3.8 26.1 %collective-permute-start = (bf16[1848,256]{1,0:T(8,128)(2,1)}, bf16[1848,256]{1,0:T(8,128)(2,1)}, u32[]{:S(2)}, u32[]{:S(2)}) collective-permute-start(bf16[1848,256]{1,0:T(8,128)(2,1)} %get-tuple-element.34.refs_1_), channel_id=1, source_target_pairs={{0,24},{4,28},{8,16},{12,20},{16,8},{20,12},{24,0},{28,4},{1,25},{... | collective-permute-start | bytes 2838536 | tf_op jit(solution)/shard_map/ppermute | solution.py:16
  7.8 24.1 %collective-permute-start.1 = (bf16[128,1024]{1,0:T(8,128)(2,1)S(1)}, bf16[128,1024]{1,0:T(8,128)(2,1)S(1)}, u32[]{:S(2)}, u32[]{:S(2)}) collective-permute-start(bf16[128,1024]{1,0:T(8,128)(2,1)S(1)} %get-tuple-element.35.refs_2_), channel_id=1, source_target_pairs={{0,1},{1,0},{2,3},{3,2},{4,5},{5,4},{6,7},{7,6},{8,9},{9,8},{10,11... | collective-permute-start | bytes 786440 | tf_op jit(solution)/shard_map/ppermute | solution.py:16
  9.3 24.1 %collective-permute-start.2 = (bf16[128,1024]{1,0:T(8,128)(2,1)}, bf16[128,1024]{1,0:T(8,128)(2,1)}, u32[]{:S(2)}, u32[]{:S(2)}) collective-permute-start(bf16[128,1024]{1,0:T(8,128)(2,1)} %get-tuple-element.36.refs_3_), channel_id=1, source_target_pairs={{0,2},{1,3},{2,0},{3,1},{4,6},{5,7},{6,4},{7,5},{8,10},{9,11},{10,... | collective-permute-start | bytes 786440 | tf_op jit(solution)/shard_map/ppermute | solution.py:16
  11.9 21.6 %collective-permute-start.3 = (bf16[128,1024]{1,0:T(8,128)(2,1)}, bf16[128,1024]{1,0:T(8,128)(2,1)}, u32[]{:S(2)}, u32[]{:S(2)}) collective-permute-start(bf16[128,1024]{1,0:T(8,128)(2,1)} %get-tuple-element.37.refs_4_), channel_id=1, source_target_pairs={{0,3},{1,2},{2,1},{3,0},{4,7},{5,6},{6,5},{7,4},{8,11},{9,10},{10,... | collective-permute-start | bytes 786440 | tf_op jit(solution)/shard_map/ppermute | solution.py:16
  12.1 5.9 %copy-start.3 = (bf16[1024,1848]{0,1:T(8,128)(2,1)S(1)}, bf16[1024,1848]{0,1:T(8,128)(2,1)}, u32[]{:S(2)}) copy-start(bf16[1024,1848]{0,1:T(8,128)(2,1)} %param.6) | copy-start | bytes 11354116
  17.5 53.8 %collective-permute-start.7 = (bf16[2,1848,256]{2,1,0:T(8,128)(2,1)}, bf16[2,1848,256]{2,1,0:T(8,128)(2,1)}, u32[]{:S(2)}, u32[]{:S(2)}) collective-permute-start(bf16[2,1848,256]{2,1,0:T(8,128)(2,1)} %get-tuple-element.66.refs_1_), channel_id=1, source_target_pairs={{0,8},{4,12},{8,0},{12,4},{16,24},{20,28},{24,16},{28,20},{1,9},{5... | collective-permute-start | bytes 5677064 | tf_op jit(solution)/shard_map/ppermute | solution.py:16
  18.3 3.6 %copy-start = (bf16[1280,1024]{1,0:T(8,128)(2,1)}, bf16[1280,1024]{1,0:T(8,128)(2,1)S(1)}, u32[]{:S(2)}) copy-start(bf16[1280,1024]{1,0:T(8,128)(2,1)S(1)} %slice.6.refs_3_.refs_6_) | copy-start | bytes 7864324
  20.6 1.3 %copy-start.2 = (bf16[568,1024]{1,0:T(8,128)(2,1)S(1)}, bf16[568,1024]{1,0:T(8,128)(2,1)}, u32[]{:S(2)}) copy-start(bf16[568,1024]{1,0:T(8,128)(2,1)} %slice.7.refs_4_.refs_6_) | copy-start | bytes 3489796
  29.9 41.8 %collective-permute-start.8 = (bf16[2,1848,256]{2,1,0:T(8,128)(2,1)}, bf16[2,1848,256]{2,1,0:T(8,128)(2,1)S(1)}, u32[]{:S(2)}, u32[]{:S(2)}) collective-permute-start(bf16[2,1848,256]{2,1,0:T(8,128)(2,1)} %get-tuple-element.65.refs_2_), channel_id=1, source_target_pairs={{0,16},{4,20},{8,24},{12,28},{16,0},{20,4},{24,8},{28,12},{1,17},{... | collective-permute-start | bytes 5677064 | tf_op jit(solution)/shard_map/ppermute | solution.py:16
  31.9 30.4 %collective-permute-start.12 = (bf16[1848,256]{1,0:T(8,128)(2,1)}, bf16[1848,256]{1,0:T(8,128)(2,1)S(1)}, u32[]{:S(2)}, u32[]{:S(2)}) collective-permute-start(bf16[1848,256]{1,0:T(8,128)(2,1)} %collective-permute-done.refs_1_.refs_0_), channel_id=1, source_target_pairs={{0,1},{1,0},{2,3},{3,2},{4,5},{5,4},{6,7},{7,6},{8,9},{9,8},{10,11... | collective-permute-start | bytes 2838536 | tf_op jit(solution)/shard_map/ppermute | solution.py:16
  33.5 1.5 %collective-permute-start.4 = (bf16[128,1024]{1,0:T(8,128)(2,1)S(1)}, bf16[128,1024]{1,0:T(8,128)(2,1)S(1)}, u32[]{:S(2)}, u32[]{:S(2)}) collective-permute-start(bf16[128,1024]{1,0:T(8,128)(2,1)S(1)} %collective-permute-done.1.refs_0_), channel_id=1, source_target_pairs={{0,4},{4,0},{8,12},{12,8},{16,20},{20,16},{24,28},{28,24},{1,5},{5... | collective-permute-start | bytes 786440 | tf_op jit(solution)/shard_map/ppermute | solution.py:16
  33.5 2.1 %collective-permute-start.5 = (bf16[128,1024]{1,0:T(8,128)(2,1)}, bf16[128,1024]{1,0:T(8,128)(2,1)S(1)}, u32[]{:S(2)}, u32[]{:S(2)}) collective-permute-start(bf16[128,1024]{1,0:T(8,128)(2,1)} %collective-permute-done.2.refs_1_), channel_id=1, source_target_pairs={{0,4},{4,0},{8,12},{12,8},{16,20},{20,16},{24,28},{28,24},{1,5},{5... | collective-permute-start | bytes 786440 | tf_op jit(solution)/shard_map/ppermute | solution.py:16
  35.0 1.7 %collective-permute-start.6 = (bf16[128,1024]{1,0:T(8,128)(2,1)}, bf16[128,1024]{1,0:T(8,128)(2,1)S(1)}, u32[]{:S(2)}, u32[]{:S(2)}) collective-permute-start(bf16[128,1024]{1,0:T(8,128)(2,1)} %collective-permute-done.3.refs_2_), channel_id=1, source_target_pairs={{0,4},{4,0},{8,12},{12,8},{16,20},{20,16},{24,28},{28,24},{1,5},{5... | collective-permute-start | bytes 786440 | tf_op jit(solution)/shard_map/ppermute | solution.py:16
  52.3 12.9 %collective-permute-start.10 = (bf16[640,1024]{1,0:T(8,128)(2,1)S(1)}, bf16[640,1024]{1,0:T(8,128)(2,1)S(1)}, u32[]{:S(2)}, u32[]{:S(2)}) collective-permute-start(bf16[640,1024]{1,0:T(8,128)(2,1)S(1)} %get-tuple-element.54.refs_2_.refs_3_), channel_id=1, source_target_pairs={{0,4},{4,0},{8,12},{12,8},{16,20},{20,16},{24,28},{28,24},{1,5},{5... | collective-permute-start | bytes 3932168 | tf_op jit(solution)/shard_map/ppermute | solution.py:16
  52.5 12.7 %collective-permute-start.9 = (bf16[640,1024]{1,0:T(8,128)(2,1)S(1)}, bf16[640,1024]{1,0:T(8,128)(2,1)S(1)}, u32[]{:S(2)}, u32[]{:S(2)}) collective-permute-start(bf16[640,1024]{1,0:T(8,128)(2,1)S(1)} %get-tuple-element.53.refs_1_.refs_2_), channel_id=1, source_target_pairs={{0,4},{4,0},{8,12},{12,8},{16,20},{20,16},{24,28},{28,24},{1,5},{5... | collective-permute-start | bytes 3932168 | tf_op jit(solution)/shard_map/ppermute | solution.py:16
  62.3 2.9 %collective-permute-start.11 = (bf16[568,1024]{1,0:T(8,128)(2,1)S(1)}, bf16[568,1024]{1,0:T(8,128)(2,1)S(1)}, u32[]{:S(2)}, u32[]{:S(2)}) collective-permute-start(bf16[568,1024]{1,0:T(8,128)(2,1)S(1)} %get-tuple-element.55.refs_3_.refs_4_), channel_id=1, source_target_pairs={{0,4},{4,0},{8,12},{12,8},{16,20},{20,16},{24,28},{28,24},{1,5},{5... | collective-permute-start | bytes 3489800 | tf_op jit(solution)/shard_map/ppermute | solution.py:16
  69.3 9.0 %collective-permute-start.13 = (bf16[128,1024]{1,0:T(8,128)(2,1)S(1)}, bf16[128,1024]{1,0:T(8,128)(2,1)S(1)}, u32[]{:S(2)}, u32[]{:S(2)}) collective-permute-start(bf16[128,1024]{1,0:T(8,128)(2,1)S(1)} %get-tuple-element.60), channel_id=1, source_target_pairs={{0,16},{4,20},{8,24},{12,28},{16,0},{20,4},{24,8},{28,12},{1,17},{... | collective-permute-start | bytes 786440 | tf_op jit(solution)/shard_map/ppermute | solution.py:16
  69.8 10.0 %collective-permute-start.15 = (bf16[128,1024]{1,0:T(8,128)(2,1)S(1)}, bf16[128,1024]{1,0:T(8,128)(2,1)S(1)}, u32[]{:S(2)}, u32[]{:S(2)}) collective-permute-start(bf16[128,1024]{1,0:T(8,128)(2,1)S(1)} %get-tuple-element.63), channel_id=1, source_target_pairs={{0,8},{4,12},{8,0},{12,4},{16,24},{20,28},{24,16},{28,20},{1,9},{5... | collective-permute-start | bytes 786440 | tf_op jit(solution)/shard_map/ppermute | solution.py:16
  78.3 3.6 %copy-start.1 = (bf16[2,1848,256]{2,1,0:T(8,128)(2,1)S(1)}, bf16[2,1848,256]{2,1,0:T(8,128)(2,1)}, u32[]{:S(2)}) copy-start(bf16[2,1848,256]{2,1,0:T(8,128)(2,1)} %get-tuple-element.64.refs_0_) | copy-start | bytes 5677060
  78.4 13.1 %collective-permute-start.14 = (bf16[256,1024]{1,0:T(8,128)(2,1)S(1)}, bf16[256,1024]{1,0:T(8,128)(2,1)S(1)}, u32[]{:S(2)}, u32[]{:S(2)}) collective-permute-start(bf16[256,1024]{1,0:T(8,128)(2,1)S(1)} %shard_map.104), channel_id=1, source_target_pairs={{0,8},{4,12},{8,0},{12,4},{16,24},{20,28},{24,16},{28,20},{1,9},{5... | collective-permute-start | bytes 1572872 | tf_op jit(solution)/shard_map/ppermute | solution.py:16
  79.9 12.4 %collective-permute-start.16 = (bf16[256,1024]{1,0:T(8,128)(2,1)S(1)}, bf16[256,1024]{1,0:T(8,128)(2,1)S(1)}, u32[]{:S(2)}, u32[]{:S(2)}) collective-permute-start(bf16[256,1024]{1,0:T(8,128)(2,1)S(1)} %shard_map.105), channel_id=1, source_target_pairs={{0,16},{4,20},{8,24},{12,28},{16,0},{20,4},{24,8},{28,12},{1,17},{... | collective-permute-start | bytes 1572872 | tf_op jit(solution)/shard_map/ppermute | solution.py:16

commit v6 on v5

--- a/solution.py
+++ b/solution.py
@@ -319,7 +319,7 @@
         passed[mask] = xor_permute(shared[mask], "tensor", planes, 1)
     token = hold(token, *(shared[mask] for mask in fars))
 
-    token, pieces = after(token, pieces)
+    token, pieces[-1] = after(token, pieces[-1])
     swapped = [to_peer(piece, 0, 1) for piece in pieces]
     state = (master, first_moment, second_moment)
     def step(at, before):

time: 93.7 us -> 93.2 us (level)
  starting transfers between devices: 19.4 us -> 17.3 us
  waiting for transfers between devices: 20.7 us -> 22.5 us
    ppermute x17, starting transfers between devices: 19.4 us -> 17.3 us  [xor_permute(): return lax.ppermute(array, axis, [(i, i ^ mask) for i in range(size)])]
    ppermute x17, waiting for transfers between devices: 20.7 us -> 22.5 us  [xor_permute(): return lax.ppermute(array, axis, [(i, i ^ mask) for i in range(size)])]
where the time goes in v6:
time: 93.2 us; the launch traced here: 92.8 us
  Pallas kernels  41.8 us (45%)
  waiting for transfers between devices  22.5 us (24%)
  starting transfers between devices  17.3 us (19%)
  local copies, waits for them, and re-layouts  9.21 us (10%)
  other arithmetic  1.22 us (1%)
    pallas_call x2, Pallas kernels, adam(): pl.pallas_call(functools.partial(adam_kernel, planes, 1.0 / math.sqrt(tok...  24.8 us
    ppermute x17, waiting for transfers between devices, xor_permute(): return lax.ppermute(array, axis, [(i, i ^ mask) for i in range(size)])  22.5 us
    ppermute x17, starting transfers between devices, xor_permute(): return lax.ppermute(array, axis, [(i, i ^ mask) for i in range(size)])  17.3 us
    pallas_call x2, Pallas kernels, product(): pl.pallas_call(functools.partial(product_kernel, bool(crossed), len(own))...  7.26 us
    pallas_call x1, Pallas kernels, products(): pl.pallas_call(functools.partial(products_kernel, len(held), len(own)), o...  6.61 us
    dynamic_slice x1, local copies, waits for them, and re-layouts, both_parts(): lax.dynamic_slice(windows, ((chip ^ mask) * 2, 0, 0), (2, block, rows))  5.36 us
    pallas_call x1, Pallas kernels, cut(): pl.pallas_call(functools.partial(cut_kernel, planes, masks), out_shape=[p...  3.08 us
  transfers between devices with their start and end apart: 17, of which 8 were waited for; matrix products, arithmetic and copies ran while one was open for 9% of the time, Pallas kernels for 42%

profile of v6, /device:TPU:0, one launch (start us, length us, event | category | flops | bytes accessed | tf_op | source)
XLA Modules:
  0.0 92.8 jit_solution(9483690126077392481)
XLA Ops:
  0.7 3.1 %shard_map.93 = (bf16[1848,256]{1,0:T(8,128)(2,1)}, bf16[128,1024]{1,0:T(8,128)(2,1)}, bf16[128,1024]{1,0:T(8,128)(2,1)}, bf16[128,1024]{1,0:T(8,128)(2,1)S(1)}) custom-call(s32[3]{0:T(128)S(1)} %pad_add_fusion.place_ref.refs_0_, bf16[8,1848,256]{2,1,0:T(8,128)(2,1)} %bitcast.7, bf16[256,4096]{1,0:T(8,128)(2,1)} %out_grad_ref.1), custom_call_target="tpu_custom_call" | custom-call | tf_op jit(solution)/shard_map/pallas_call | solution.py:41
  3.8 4.0 %collective-permute-start = (bf16[1848,256]{1,0:T(8,128)(2,1)}, bf16[1848,256]{1,0:T(8,128)(2,1)}, u32[]{:S(2)}, u32[]{:S(2)}) collective-permute-start(bf16[1848,256]{1,0:T(8,128)(2,1)} %get-tuple-element.32.refs_1_), channel_id=1, source_target_pairs={{0,24},{4,28},{8,16},{12,20},{16,8},{20,12},{24,0},{28,4},{1,25},{... | collective-permute-start | bytes 2838536 | tf_op jit(solution)/shard_map/ppermute | solution.py:16
  7.8 3.6 %collective-permute-start.1 = (bf16[128,1024]{1,0:T(8,128)(2,1)S(1)}, bf16[128,1024]{1,0:T(8,128)(2,1)S(1)}, u32[]{:S(2)}, u32[]{:S(2)}) collective-permute-start(bf16[128,1024]{1,0:T(8,128)(2,1)S(1)} %get-tuple-element.35.refs_4_), channel_id=1, source_target_pairs={{0,3},{1,2},{2,1},{3,0},{4,7},{5,6},{6,5},{7,4},{8,11},{9,10},{10,... | collective-permute-start | bytes 786440 | tf_op jit(solution)/shard_map/ppermute | solution.py:16
  12.1 5.4 %constant_dynamic-slice_fusion = (bf16[2,1848,256]{2,1,0:T(8,128)(2,1)}, bf16[2,1848,256]{2,1,0:T(8,128)(2,1)}, bf16[2,1848,256]{2,1,0:T(8,128)(2,1)}) fusion(bf16[8,1848,256]{2,1,0:T(8,128)(2,1)} %bitcast.8, s32[]{:T(128)S(6)} %select_n.15, s32[]{:T(128)S(6)} %select_n.13, s32[]{:T(128)S(6)} %select_n.12), kind=kLoop, calls=%fused_computation.2 | loop fusion | bytes 11354124 | tf_op jit(solution)/shard_map/dynamic_slice | solution.py:304
  18.3 1.2 %slice.7.refs_4_.refs_6_ = bf16[568,1024]{1,0:T(8,128)(2,1)} slice(bf16[1848,1024]{1,0:T(8,128)(2,1)S(1)} %bitcast.10), slice={[1280:1848], [0:1024]} | slice | bytes 2326528 | tf_op jit(solution)/shard_map/slice | solution.py:311
  19.5 1.1 %constant_dynamic-slice_fusion.1.refs_5_.own_ref = bf16[256,1024]{1,0:T(8,128)(2,1)S(1)} fusion(bf16[256,4096]{1,0:T(8,128)(2,1)} %out_grad_ref.1, s32[]{:T(128)S(6)} %select_n.14), kind=kLoop, calls=%fused_computation.3 | loop fusion | bytes 1048580 | tf_op jit(solution)/shard_map/dynamic_slice | solution.py:307
  20.6 1.3 %copy-done.2 = bf16[568,1024]{1,0:T(8,128)(2,1)S(1)} copy-done((bf16[568,1024]{1,0:T(8,128)(2,1)S(1)}, bf16[568,1024]{1,0:T(8,128)(2,1)}, u32[]{:S(2)}) %copy-start.2) | copy-done | bytes 1163288
  21.9 2.0 %collective-permute-done.2.refs_0_ = bf16[128,1024]{1,0:T(8,128)(2,1)S(1)} collective-permute-done((bf16[128,1024]{1,0:T(8,128)(2,1)}, bf16[128,1024]{1,0:T(8,128)(2,1)S(1)}, u32[]{:S(2)}, u32[]{:S(2)}) %collective-permute-start.2) | collective-permute-done | bytes 262176 | tf_op jit(solution)/shard_map/ppermute | solution.py:16
  24.4 5.4 %collective-permute-done.refs_1_.refs_0_ = bf16[1848,256]{1,0:T(8,128)(2,1)} collective-permute-done((bf16[1848,256]{1,0:T(8,128)(2,1)}, bf16[1848,256]{1,0:T(8,128)(2,1)}, u32[]{:S(2)}, u32[]{:S(2)}) %collective-permute-start) | collective-permute-done | bytes 946208 | tf_op jit(solution)/shard_map/ppermute | solution.py:16
  29.9 2.1 %collective-permute-start.12 = (bf16[1848,256]{1,0:T(8,128)(2,1)}, bf16[1848,256]{1,0:T(8,128)(2,1)S(1)}, u32[]{:S(2)}, u32[]{:S(2)}) collective-permute-start(bf16[1848,256]{1,0:T(8,128)(2,1)} %collective-permute-done.refs_1_.refs_0_), channel_id=1, source_target_pairs={{0,1},{1,0},{2,3},{3,2},{4,5},{5,4},{6,7},{7,6},{8,9},{9,8},{10,11... | collective-permute-start | bytes 2838536 | tf_op jit(solution)/shard_map/ppermute | solution.py:16
  32.0 1.5 %collective-permute-done.3.refs_1_ = bf16[128,1024]{1,0:T(8,128)(2,1)} collective-permute-done((bf16[128,1024]{1,0:T(8,128)(2,1)}, bf16[128,1024]{1,0:T(8,128)(2,1)}, u32[]{:S(2)}, u32[]{:S(2)}) %collective-permute-start.3) | collective-permute-done | bytes 262176 | tf_op jit(solution)/shard_map/ppermute | solution.py:16
  34.0 1.5 %collective-permute-done.5.refs_4_ = bf16[128,1024]{1,0:T(8,128)(2,1)S(1)} collective-permute-done((bf16[128,1024]{1,0:T(8,128)(2,1)}, bf16[128,1024]{1,0:T(8,128)(2,1)S(1)}, u32[]{:S(2)}, u32[]{:S(2)}) %collective-permute-start.5) | collective-permute-done | bytes 262176 | tf_op jit(solution)/shard_map/ppermute | solution.py:16
  35.5 15.4 %shard_map.97 = (f32[1848,1024]{1,0:T(8,128)}, f32[1848,1024]{1,0:T(8,128)}, f32[1848,1024]{1,0:T(8,128)}, bf16[640,1024]{1,0:T(8,128)(2,1)S(1)}, bf16[640,1024]{1,0:T(8,128)(2,1)S(1)}) custom-call(s32[3]{0:T(128)S(1)} %shard_map.96.place_ref.refs_0_, bf16[256,1024]{1,0:T(8,128)(2,1)S(1)} %constant_dynamic-slice_fusion.1.refs_5_.own_ref, ...), custom_call_target="tpu_custom_call" | custom-call | tf_op jit(solution)/shard_map/pallas_call | solution.py:124
  51.5 9.3 %shard_map.98 = (f32[1848,1024]{1,0:T(8,128)}, f32[1848,1024]{1,0:T(8,128)}, f32[1848,1024]{1,0:T(8,128)}, bf16[568,1024]{1,0:T(8,128)(2,1)S(1)}) custom-call(s32[3]{0:T(128)S(1)} %shard_map.96.place_ref.refs_0_, bf16[256,1024]{1,0:T(8,128)(2,1)S(1)} %constant_dynamic-slice_fusion.1.refs_5_.own_ref, ...), custom_call_target="tpu_custom_call", output_to_operand_aliasing={{0}: (12, {}), {1}: (13, {}), {2}: (14, {})} | custom-call | tf_op jit(solution)/shard_map/pallas_call | solution.py:124
  61.1 2.7 %collective-permute-done.11.refs_6_.refs_7_ = bf16[568,1024]{1,0:T(8,128)(2,1)S(1)} collective-permute-done((bf16[568,1024]{1,0:T(8,128)(2,1)S(1)}, bf16[568,1024]{1,0:T(8,128)(2,1)S(1)}, u32[]{:S(2)}, u32[]{:S(2)}) %collective-permute-start.11) | collective-permute-done | bytes 1163296 | tf_op jit(solution)/shard_map/ppermute | solution.py:16
  63.8 4.1 %shard_map.103 = (bf16[128,1024]{1,0:T(8,128)(2,1)S(1)}, bf16[128,1024]{1,0:T(8,128)(2,1)S(1)}) custom-call(s32[3]{0:T(128)S(1)} %shard_map.102.place_ref, bf16[1848,256]{1,0:T(8,128)(2,1)} %collective-permute-done.refs_1_.refs_0_, bf16[1848,256]{1,0:T(8,128)(2,1)S(1)} %collective-permute-done.12.refs_1_, ...), custom_call_target="tpu_custom_call" | custom-call | tf_op jit(solution)/shard_map/pallas_call | solution.py:189
  68.4 0.9 collective-permute-start.15
  69.9 6.6 %shard_map.101 = (f32[128,1024]{1,0:T(8,128)S(1)}, f32[128,1024]{1,0:T(8,128)S(1)}, f32[128,1024]{1,0:T(8,128)S(1)}, f32[128,1024]{1,0:T(8,128)S(1)}) custom-call(s32[3]{0:T(128)S(1)} %shard_map.99.place_ref, bf16[2,1848,256]{2,1,0:T(8,128)(2,1)} %collective-permute-done.7.refs_1_.refs_0_, bf16[2,1848,256]{2,1,0:T(8,128)(2,1)S(1)} %collective-permute-done.8.refs_2_.refs_1_, ...), custom_call_target="tpu_custom_call" | custom-call | tf_op jit(solution)/shard_map/pallas_call | solution.py:222
  76.6 1.6 %collective-permute-start.14 = (bf16[256,1024]{1,0:T(8,128)(2,1)S(1)}, bf16[256,1024]{1,0:T(8,128)(2,1)S(1)}, u32[]{:S(2)}, u32[]{:S(2)}) collective-permute-start(bf16[256,1024]{1,0:T(8,128)(2,1)S(1)} %shard_map.104), channel_id=1, source_target_pairs={{0,8},{4,12},{8,0},{12,4},{16,24},{20,28},{24,16},{28,20},{1,9},{5... | collective-permute-start | bytes 1572872 | tf_op jit(solution)/shard_map/ppermute | solution.py:16
  78.2 1.5 %collective-permute-start.16 = (bf16[256,1024]{1,0:T(8,128)(2,1)S(1)}, bf16[256,1024]{1,0:T(8,128)(2,1)S(1)}, u32[]{:S(2)}, u32[]{:S(2)}) collective-permute-start(bf16[256,1024]{1,0:T(8,128)(2,1)S(1)} %shard_map.105), channel_id=1, source_target_pairs={{0,16},{4,20},{8,24},{12,28},{16,0},{20,4},{24,8},{28,12},{1,17},{... | collective-permute-start | bytes 1572872 | tf_op jit(solution)/shard_map/ppermute | solution.py:16
  79.7 3.2 %shard_map.100 = (f32[128,1024]{1,0:T(8,128)S(1)}, f32[128,1024]{1,0:T(8,128)S(1)}) custom-call(s32[3]{0:T(128)S(1)} %shard_map.99.place_ref, bf16[2,1848,256]{2,1,0:T(8,128)(2,1)S(1)} %copy-done.1, bf16[640,1024]{1,0:T(8,128)(2,1)S(1)} %get-tuple-element.49.refs_1_.refs_2_, bf16[640,1024]{1,0:T(8,128)(2,1)S(1)} %get-tuple-element.50.refs_2_.refs_3_, ...), custom_call_target="tpu_custom_call" | custom-call | flops 1937768448 | bytes 7569408 | tf_op jit(solution)/shard_map/pallas_call | solution.py:189
  83.0 7.2 %collective-permute-done.14 = bf16[256,1024]{1,0:T(8,128)(2,1)S(1)} collective-permute-done((bf16[256,1024]{1,0:T(8,128)(2,1)S(1)}, bf16[256,1024]{1,0:T(8,128)(2,1)S(1)}, u32[]{:S(2)}, u32[]{:S(2)}) %collective-permute-start.14) | collective-permute-done | bytes 524320 | tf_op jit(solution)/shard_map/ppermute | solution.py:16
  90.2 1.5 %collective-permute-done.16 = bf16[256,1024]{1,0:T(8,128)(2,1)S(1)} collective-permute-done((bf16[256,1024]{1,0:T(8,128)(2,1)S(1)}, bf16[256,1024]{1,0:T(8,128)(2,1)S(1)}, u32[]{:S(2)}, u32[]{:S(2)}) %collective-permute-start.16) | collective-permute-done | bytes 524320 | tf_op jit(solution)/shard_map/ppermute | solution.py:16
  91.8 1.0 %add_convert_fusion = bf16[256,1024]{1,0:T(8,128)(2,1)} fusion(bf16[256,1024]{1,0:T(8,128)(2,1)S(1)} %collective-permute-done.16, f32[256,1024]{1,0:T(8,128)S(1)} %pad_maximum_fusion, bf16[256,1024]{1,0:T(8,128)(2,1)S(1)} %collective-permute-done.14), kind=kLoop, calls=%fused_computation.1 | loop fusion | flops 1310720 | bytes 2621440 | tf_op jit(solution)/shard_map/convert_element_type | solution.py:358
  (39 shorter events, 4.8 us)
Async XLA Ops:
  3.8 26.1 %collective-permute-start = (bf16[1848,256]{1,0:T(8,128)(2,1)}, bf16[1848,256]{1,0:T(8,128)(2,1)}, u32[]{:S(2)}, u32[]{:S(2)}) collective-permute-start(bf16[1848,256]{1,0:T(8,128)(2,1)} %get-tuple-element.32.refs_1_), channel_id=1, source_target_pairs={{0,24},{4,28},{8,16},{12,20},{16,8},{20,12},{24,0},{28,4},{1,25},{... | collective-permute-start | bytes 2838536 | tf_op jit(solution)/shard_map/ppermute | solution.py:16
  7.8 22.1 %collective-permute-start.1 = (bf16[128,1024]{1,0:T(8,128)(2,1)S(1)}, bf16[128,1024]{1,0:T(8,128)(2,1)S(1)}, u32[]{:S(2)}, u32[]{:S(2)}) collective-permute-start(bf16[128,1024]{1,0:T(8,128)(2,1)S(1)} %get-tuple-element.35.refs_4_), channel_id=1, source_target_pairs={{0,3},{1,2},{2,1},{3,0},{4,7},{5,6},{6,5},{7,4},{8,11},{9,10},{10,... | collective-permute-start | bytes 786440 | tf_op jit(solution)/shard_map/ppermute | solution.py:16
  11.4 12.6 %collective-permute-start.2 = (bf16[128,1024]{1,0:T(8,128)(2,1)}, bf16[128,1024]{1,0:T(8,128)(2,1)S(1)}, u32[]{:S(2)}, u32[]{:S(2)}) collective-permute-start(bf16[128,1024]{1,0:T(8,128)(2,1)} %get-tuple-element.33.refs_2_), channel_id=1, source_target_pairs={{0,1},{1,0},{2,3},{3,2},{4,5},{5,4},{6,7},{7,6},{8,9},{9,8},{10,11... | collective-permute-start | bytes 786440 | tf_op jit(solution)/shard_map/ppermute | solution.py:16
  11.4 22.1 %collective-permute-start.3 = (bf16[128,1024]{1,0:T(8,128)(2,1)}, bf16[128,1024]{1,0:T(8,128)(2,1)}, u32[]{:S(2)}, u32[]{:S(2)}) collective-permute-start(bf16[128,1024]{1,0:T(8,128)(2,1)} %get-tuple-element.34.refs_3_), channel_id=1, source_target_pairs={{0,2},{1,3},{2,0},{3,1},{4,6},{5,7},{6,4},{7,5},{8,10},{9,11},{10,... | collective-permute-start | bytes 786440 | tf_op jit(solution)/shard_map/ppermute | solution.py:16
  12.1 5.9 %copy-start.3 = (bf16[1024,1848]{0,1:T(8,128)(2,1)S(1)}, bf16[1024,1848]{0,1:T(8,128)(2,1)}, u32[]{:S(2)}) copy-start(bf16[1024,1848]{0,1:T(8,128)(2,1)} %param.6) | copy-start | bytes 11354116
  17.5 52.4 %collective-permute-start.7 = (bf16[2,1848,256]{2,1,0:T(8,128)(2,1)}, bf16[2,1848,256]{2,1,0:T(8,128)(2,1)}, u32[]{:S(2)}, u32[]{:S(2)}) collective-permute-start(bf16[2,1848,256]{2,1,0:T(8,128)(2,1)} %get-tuple-element.62.refs_1_), channel_id=1, source_target_pairs={{0,8},{4,12},{8,0},{12,4},{16,24},{20,28},{24,16},{28,20},{1,9},{5... | collective-permute-start | bytes 5677064 | tf_op jit(solution)/shard_map/ppermute | solution.py:16
  18.3 3.6 %copy-start = (bf16[1280,1024]{1,0:T(8,128)(2,1)}, bf16[1280,1024]{1,0:T(8,128)(2,1)S(1)}, u32[]{:S(2)}) copy-start(bf16[1280,1024]{1,0:T(8,128)(2,1)S(1)} %slice.6.refs_3_.refs_6_) | copy-start | bytes 7864324
  20.6 1.3 %copy-start.2 = (bf16[568,1024]{1,0:T(8,128)(2,1)S(1)}, bf16[568,1024]{1,0:T(8,128)(2,1)}, u32[]{:S(2)}) copy-start(bf16[568,1024]{1,0:T(8,128)(2,1)} %slice.7.refs_4_.refs_6_) | copy-start | bytes 3489796
  23.9 45.9 %collective-permute-start.8 = (bf16[2,1848,256]{2,1,0:T(8,128)(2,1)}, bf16[2,1848,256]{2,1,0:T(8,128)(2,1)S(1)}, u32[]{:S(2)}, u32[]{:S(2)}) collective-permute-start(bf16[2,1848,256]{2,1,0:T(8,128)(2,1)} %get-tuple-element.61.refs_2_), channel_id=1, source_target_pairs={{0,16},{4,20},{8,24},{12,28},{16,0},{20,4},{24,8},{28,12},{1,17},{... | collective-permute-start | bytes 5677064 | tf_op jit(solution)/shard_map/ppermute | solution.py:16
  29.9 3.6 %collective-permute-start.4 = (bf16[128,1024]{1,0:T(8,128)(2,1)S(1)}, bf16[128,1024]{1,0:T(8,128)(2,1)S(1)}, u32[]{:S(2)}, u32[]{:S(2)}) collective-permute-start(bf16[128,1024]{1,0:T(8,128)(2,1)S(1)} %collective-permute-done.2.refs_0_), channel_id=1, source_target_pairs={{0,4},{4,0},{8,12},{12,8},{16,20},{20,16},{24,28},{28,24},{1,5},{5... | collective-permute-start | bytes 786440 | tf_op jit(solution)/shard_map/ppermute | solution.py:16
  29.9 31.0 %collective-permute-start.12 = (bf16[1848,256]{1,0:T(8,128)(2,1)}, bf16[1848,256]{1,0:T(8,128)(2,1)S(1)}, u32[]{:S(2)}, u32[]{:S(2)}) collective-permute-start(bf16[1848,256]{1,0:T(8,128)(2,1)} %collective-permute-done.refs_1_.refs_0_), channel_id=1, source_target_pairs={{0,1},{1,0},{2,3},{3,2},{4,5},{5,4},{6,7},{7,6},{8,9},{9,8},{10,11... | collective-permute-start | bytes 2838536 | tf_op jit(solution)/shard_map/ppermute | solution.py:16
  33.5 2.0 %collective-permute-start.5 = (bf16[128,1024]{1,0:T(8,128)(2,1)}, bf16[128,1024]{1,0:T(8,128)(2,1)S(1)}, u32[]{:S(2)}, u32[]{:S(2)}) collective-permute-start(bf16[128,1024]{1,0:T(8,128)(2,1)} %collective-permute-done.3.refs_1_), channel_id=1, source_target_pairs={{0,4},{4,0},{8,12},{12,8},{16,20},{20,16},{24,28},{28,24},{1,5},{5... | collective-permute-start | bytes 786440 | tf_op jit(solution)/shard_map/ppermute | solution.py:16
  33.5 2.0 %collective-permute-start.6 = (bf16[128,1024]{1,0:T(8,128)(2,1)S(1)}, bf16[128,1024]{1,0:T(8,128)(2,1)S(1)}, u32[]{:S(2)}, u32[]{:S(2)}) collective-permute-start(bf16[128,1024]{1,0:T(8,128)(2,1)S(1)} %collective-permute-done.1.refs_2_), channel_id=1, source_target_pairs={{0,4},{4,0},{8,12},{12,8},{16,20},{20,16},{24,28},{28,24},{1,5},{5... | collective-permute-start | bytes 786440 | tf_op jit(solution)/shard_map/ppermute | solution.py:16
  51.0 12.8 %collective-permute-start.10 = (bf16[640,1024]{1,0:T(8,128)(2,1)S(1)}, bf16[640,1024]{1,0:T(8,128)(2,1)S(1)}, u32[]{:S(2)}, u32[]{:S(2)}) collective-permute-start(bf16[640,1024]{1,0:T(8,128)(2,1)S(1)} %get-tuple-element.50.refs_2_.refs_3_), channel_id=1, source_target_pairs={{0,4},{4,0},{8,12},{12,8},{16,20},{20,16},{24,28},{28,24},{1,5},{5... | collective-permute-start | bytes 3932168 | tf_op jit(solution)/shard_map/ppermute | solution.py:16
  51.2 12.6 %collective-permute-start.9 = (bf16[640,1024]{1,0:T(8,128)(2,1)S(1)}, bf16[640,1024]{1,0:T(8,128)(2,1)S(1)}, u32[]{:S(2)}, u32[]{:S(2)}) collective-permute-start(bf16[640,1024]{1,0:T(8,128)(2,1)S(1)} %get-tuple-element.49.refs_1_.refs_2_), channel_id=1, source_target_pairs={{0,4},{4,0},{8,12},{12,8},{16,20},{20,16},{24,28},{28,24},{1,5},{5... | collective-permute-start | bytes 3932168 | tf_op jit(solution)/shard_map/ppermute | solution.py:16
  60.9 2.9 %collective-permute-start.11 = (bf16[568,1024]{1,0:T(8,128)(2,1)S(1)}, bf16[568,1024]{1,0:T(8,128)(2,1)S(1)}, u32[]{:S(2)}, u32[]{:S(2)}) collective-permute-start(bf16[568,1024]{1,0:T(8,128)(2,1)S(1)} %get-tuple-element.51.refs_3_.refs_4_), channel_id=1, source_target_pairs={{0,4},{4,0},{8,12},{12,8},{16,20},{20,16},{24,28},{28,24},{1,5},{5... | collective-permute-start | bytes 3489800 | tf_op jit(solution)/shard_map/ppermute | solution.py:16
  67.9 8.6 %collective-permute-start.13 = (bf16[128,1024]{1,0:T(8,128)(2,1)S(1)}, bf16[128,1024]{1,0:T(8,128)(2,1)S(1)}, u32[]{:S(2)}, u32[]{:S(2)}) collective-permute-start(bf16[128,1024]{1,0:T(8,128)(2,1)S(1)} %get-tuple-element.56), channel_id=1, source_target_pairs={{0,16},{4,20},{8,24},{12,28},{16,0},{20,4},{24,8},{28,12},{1,17},{... | collective-permute-start | bytes 786440 | tf_op jit(solution)/shard_map/ppermute | solution.py:16
  68.4 9.7 %collective-permute-start.15 = (bf16[128,1024]{1,0:T(8,128)(2,1)S(1)}, bf16[128,1024]{1,0:T(8,128)(2,1)S(1)}, u32[]{:S(2)}, u32[]{:S(2)}) collective-permute-start(bf16[128,1024]{1,0:T(8,128)(2,1)S(1)} %get-tuple-element.59), channel_id=1, source_target_pairs={{0,8},{4,12},{8,0},{12,4},{16,24},{20,28},{24,16},{28,20},{1,9},{5... | collective-permute-start | bytes 786440 | tf_op jit(solution)/shard_map/ppermute | solution.py:16
  76.5 3.2 %copy-start.1 = (bf16[2,1848,256]{2,1,0:T(8,128)(2,1)S(1)}, bf16[2,1848,256]{2,1,0:T(8,128)(2,1)}, u32[]{:S(2)}) copy-start(bf16[2,1848,256]{2,1,0:T(8,128)(2,1)} %get-tuple-element.60.refs_0_) | copy-start | bytes 5677060
  76.6 13.6 %collective-permute-start.14 = (bf16[256,1024]{1,0:T(8,128)(2,1)S(1)}, bf16[256,1024]{1,0:T(8,128)(2,1)S(1)}, u32[]{:S(2)}, u32[]{:S(2)}) collective-permute-start(bf16[256,1024]{1,0:T(8,128)(2,1)S(1)} %shard_map.104), channel_id=1, source_target_pairs={{0,8},{4,12},{8,0},{12,4},{16,24},{20,28},{24,16},{28,20},{1,9},{5... | collective-permute-start | bytes 1572872 | tf_op jit(solution)/shard_map/ppermute | solution.py:16
  78.2 13.5 %collective-permute-start.16 = (bf16[256,1024]{1,0:T(8,128)(2,1)S(1)}, bf16[256,1024]{1,0:T(8,128)(2,1)S(1)}, u32[]{:S(2)}, u32[]{:S(2)}) collective-permute-start(bf16[256,1024]{1,0:T(8,128)(2,1)S(1)} %shard_map.105), channel_id=1, source_target_pairs={{0,16},{4,20},{8,24},{12,28},{16,0},{20,4},{24,8},{28,12},{1,17},{... | collective-permute-start | bytes 1572872 | tf_op jit(solution)/shard_map/ppermute | solution.py:16

commit v7 on v6

--- a/solution.py
+++ b/solution.py
@@ -205,12 +205,17 @@
         pair_refs = held_refs[first : first + 2]
         total = 0.0
         for weights_refs, of_core in ((own_refs, core), (other_refs, 1 - core)):
+            blocks = [ref[...] for ref in weights_refs]
+            if len(blocks) > 2:
+                cut = blocks[0].shape[0] // 256 * 256
+                blocks[1] = jnp.concatenate([weights_refs[0][cut:], blocks[1]], axis=0)
+                blocks[0] = weights_refs[0][:cut]
             at = 0
-            for ref in weights_refs:
-                rows = slice(at, at + ref.shape[0])
+            for block in blocks:
+                rows = slice(at, at + block.shape[0])
                 held = jnp.concatenate([held_ref[of_core, rows] for held_ref in pair_refs], axis=1)
-                total = total + lax.dot_general(held, ref[...], OVER_FIRST, preferred_element_type=jnp.float32)
-                at += ref.shape[0]
+                total = total + lax.dot_general(held, block, OVER_FIRST, preferred_element_type=jnp.float32)
+                at += block.shape[0]
         for i in range(2 * len(pair_refs)):
             out_refs[2 * first + i][...] = total[i * half : (i + 1) * half]
 

time: 93.2 us -> 92.7 us (level)
  transfers between devices with their start and end apart: 17 -> 17, of which waited for: 8 -> 9; matrix products, arithmetic and copies ran while one was open for 9% -> 9% of each run, Pallas kernels for 42% -> 41%
where the time goes in v7:
time: 92.7 us; the launch traced here: 92.3 us
  Pallas kernels  41.1 us (44%)
  waiting for transfers between devices  22.8 us (25%)
  starting transfers between devices  17.2 us (19%)
  local copies, waits for them, and re-layouts  9.21 us (10%)
  other arithmetic  1.22 us (1%)
    pallas_call x2, Pallas kernels, adam(): pl.pallas_call(functools.partial(adam_kernel, planes, 1.0 / math.sqrt(tok...  24.8 us
    ppermute x17, waiting for transfers between devices, xor_permute(): return lax.ppermute(array, axis, [(i, i ^ mask) for i in range(size)])  22.8 us
    ppermute x17, starting transfers between devices, xor_permute(): return lax.ppermute(array, axis, [(i, i ^ mask) for i in range(size)])  17.2 us
    pallas_call x2, Pallas kernels, product(): pl.pallas_call(functools.partial(product_kernel, bool(crossed), len(own))...  7.04 us
    pallas_call x1, Pallas kernels, products(): pl.pallas_call(functools.partial(products_kernel, len(held), len(own)), o...  6.09 us
    dynamic_slice x1, local copies, waits for them, and re-layouts, both_parts(): lax.dynamic_slice(windows, ((chip ^ mask) * 2, 0, 0), (2, block, rows))  5.36 us
    pallas_call x1, Pallas kernels, cut(): pl.pallas_call(functools.partial(cut_kernel, planes, masks), out_shape=[p...  3.08 us
  transfers between devices with their start and end apart: 17, of which 9 were waited for; matrix products, arithmetic and copies ran while one was open for 9% of the time, Pallas kernels for 41%

profile of v7, /device:TPU:0, one launch (start us, length us, event | category | flops | bytes accessed | tf_op | source)
XLA Modules:
  0.0 92.3 jit_solution(11213708839014536860)
XLA Ops:
  0.7 3.1 %shard_map.93 = (bf16[1848,256]{1,0:T(8,128)(2,1)}, bf16[128,1024]{1,0:T(8,128)(2,1)}, bf16[128,1024]{1,0:T(8,128)(2,1)}, bf16[128,1024]{1,0:T(8,128)(2,1)S(1)}) custom-call(s32[3]{0:T(128)S(1)} %pad_add_fusion.place_ref.refs_0_, bf16[8,1848,256]{2,1,0:T(8,128)(2,1)} %bitcast.7, bf16[256,4096]{1,0:T(8,128)(2,1)} %out_grad_ref.1), custom_call_target="tpu_custom_call" | custom-call | tf_op jit(solution)/shard_map/pallas_call | solution.py:41
  3.8 4.0 %collective-permute-start = (bf16[1848,256]{1,0:T(8,128)(2,1)}, bf16[1848,256]{1,0:T(8,128)(2,1)}, u32[]{:S(2)}, u32[]{:S(2)}) collective-permute-start(bf16[1848,256]{1,0:T(8,128)(2,1)} %get-tuple-element.32.refs_1_), channel_id=1, source_target_pairs={{0,24},{4,28},{8,16},{12,20},{16,8},{20,12},{24,0},{28,4},{1,25},{... | collective-permute-start | bytes 2838536 | tf_op jit(solution)/shard_map/ppermute | solution.py:16
  7.8 3.6 %collective-permute-start.1 = (bf16[128,1024]{1,0:T(8,128)(2,1)S(1)}, bf16[128,1024]{1,0:T(8,128)(2,1)S(1)}, u32[]{:S(2)}, u32[]{:S(2)}) collective-permute-start(bf16[128,1024]{1,0:T(8,128)(2,1)S(1)} %get-tuple-element.35.refs_4_), channel_id=1, source_target_pairs={{0,3},{1,2},{2,1},{3,0},{4,7},{5,6},{6,5},{7,4},{8,11},{9,10},{10,... | collective-permute-start | bytes 786440 | tf_op jit(solution)/shard_map/ppermute | solution.py:16
  12.1 5.4 %constant_dynamic-slice_fusion = (bf16[2,1848,256]{2,1,0:T(8,128)(2,1)}, bf16[2,1848,256]{2,1,0:T(8,128)(2,1)}, bf16[2,1848,256]{2,1,0:T(8,128)(2,1)}) fusion(bf16[8,1848,256]{2,1,0:T(8,128)(2,1)} %bitcast.8, s32[]{:T(128)S(6)} %select_n.15, s32[]{:T(128)S(6)} %select_n.13, s32[]{:T(128)S(6)} %select_n.12), kind=kLoop, calls=%fused_computation.2 | loop fusion | bytes 11354124 | tf_op jit(solution)/shard_map/dynamic_slice | solution.py:309
  18.3 1.2 %slice.7.refs_4_.refs_6_ = bf16[568,1024]{1,0:T(8,128)(2,1)} slice(bf16[1848,1024]{1,0:T(8,128)(2,1)S(1)} %bitcast.10), slice={[1280:1848], [0:1024]} | slice | bytes 2326528 | tf_op jit(solution)/shard_map/slice | solution.py:316
  19.5 1.1 %constant_dynamic-slice_fusion.1.refs_5_.own_ref = bf16[256,1024]{1,0:T(8,128)(2,1)S(1)} fusion(bf16[256,4096]{1,0:T(8,128)(2,1)} %out_grad_ref.1, s32[]{:T(128)S(6)} %select_n.14), kind=kLoop, calls=%fused_computation.3 | loop fusion | bytes 1048580 | tf_op jit(solution)/shard_map/dynamic_slice | solution.py:312
  20.6 1.3 %copy-done.2 = bf16[568,1024]{1,0:T(8,128)(2,1)S(1)} copy-done((bf16[568,1024]{1,0:T(8,128)(2,1)S(1)}, bf16[568,1024]{1,0:T(8,128)(2,1)}, u32[]{:S(2)}) %copy-start.2) | copy-done | bytes 1163288
  21.9 2.0 %collective-permute-done.2.refs_0_ = bf16[128,1024]{1,0:T(8,128)(2,1)S(1)} collective-permute-done((bf16[128,1024]{1,0:T(8,128)(2,1)}, bf16[128,1024]{1,0:T(8,128)(2,1)S(1)}, u32[]{:S(2)}, u32[]{:S(2)}) %collective-permute-start.2) | collective-permute-done | bytes 262176 | tf_op jit(solution)/shard_map/ppermute | solution.py:16
  24.4 5.4 %collective-permute-done.refs_1_.refs_0_ = bf16[1848,256]{1,0:T(8,128)(2,1)} collective-permute-done((bf16[1848,256]{1,0:T(8,128)(2,1)}, bf16[1848,256]{1,0:T(8,128)(2,1)}, u32[]{:S(2)}, u32[]{:S(2)}) %collective-permute-start) | collective-permute-done | bytes 946208 | tf_op jit(solution)/shard_map/ppermute | solution.py:16
  29.9 2.1 %collective-permute-start.12 = (bf16[1848,256]{1,0:T(8,128)(2,1)}, bf16[1848,256]{1,0:T(8,128)(2,1)S(1)}, u32[]{:S(2)}, u32[]{:S(2)}) collective-permute-start(bf16[1848,256]{1,0:T(8,128)(2,1)} %collective-permute-done.refs_1_.refs_0_), channel_id=1, source_target_pairs={{0,1},{1,0},{2,3},{3,2},{4,5},{5,4},{6,7},{7,6},{8,9},{9,8},{10,11... | collective-permute-start | bytes 2838536 | tf_op jit(solution)/shard_map/ppermute | solution.py:16
  32.0 1.5 %collective-permute-done.3.refs_1_ = bf16[128,1024]{1,0:T(8,128)(2,1)} collective-permute-done((bf16[128,1024]{1,0:T(8,128)(2,1)}, bf16[128,1024]{1,0:T(8,128)(2,1)}, u32[]{:S(2)}, u32[]{:S(2)}) %collective-permute-start.3) | collective-permute-done | bytes 262176 | tf_op jit(solution)/shard_map/ppermute | solution.py:16
  34.0 1.5 %collective-permute-done.5.refs_4_ = bf16[128,1024]{1,0:T(8,128)(2,1)S(1)} collective-permute-done((bf16[128,1024]{1,0:T(8,128)(2,1)}, bf16[128,1024]{1,0:T(8,128)(2,1)S(1)}, u32[]{:S(2)}, u32[]{:S(2)}) %collective-permute-start.5) | collective-permute-done | bytes 262176 | tf_op jit(solution)/shard_map/ppermute | solution.py:16
  35.5 15.4 %shard_map.97 = (f32[1848,1024]{1,0:T(8,128)}, f32[1848,1024]{1,0:T(8,128)}, f32[1848,1024]{1,0:T(8,128)}, bf16[640,1024]{1,0:T(8,128)(2,1)S(1)}, bf16[640,1024]{1,0:T(8,128)(2,1)S(1)}) custom-call(s32[3]{0:T(128)S(1)} %shard_map.96.place_ref.refs_0_, bf16[256,1024]{1,0:T(8,128)(2,1)S(1)} %constant_dynamic-slice_fusion.1.refs_5_.own_ref, ...), custom_call_target="tpu_custom_call" | custom-call | tf_op jit(solution)/shard_map/pallas_call | solution.py:124
  51.5 9.3 %shard_map.98 = (f32[1848,1024]{1,0:T(8,128)}, f32[1848,1024]{1,0:T(8,128)}, f32[1848,1024]{1,0:T(8,128)}, bf16[568,1024]{1,0:T(8,128)(2,1)S(1)}) custom-call(s32[3]{0:T(128)S(1)} %shard_map.96.place_ref.refs_0_, bf16[256,1024]{1,0:T(8,128)(2,1)S(1)} %constant_dynamic-slice_fusion.1.refs_5_.own_ref, ...), custom_call_target="tpu_custom_call", output_to_operand_aliasing={{0}: (12, {}), {1}: (13, {}), {2}: (14, {})} | custom-call | tf_op jit(solution)/shard_map/pallas_call | solution.py:124
  61.1 2.7 %collective-permute-done.11.refs_6_.refs_7_ = bf16[568,1024]{1,0:T(8,128)(2,1)S(1)} collective-permute-done((bf16[568,1024]{1,0:T(8,128)(2,1)S(1)}, bf16[568,1024]{1,0:T(8,128)(2,1)S(1)}, u32[]{:S(2)}, u32[]{:S(2)}) %collective-permute-start.11) | collective-permute-done | bytes 1163296 | tf_op jit(solution)/shard_map/ppermute | solution.py:16
  63.8 3.8 %shard_map.103 = (bf16[128,1024]{1,0:T(8,128)(2,1)S(1)}, bf16[128,1024]{1,0:T(8,128)(2,1)S(1)}) custom-call(s32[3]{0:T(128)S(1)} %shard_map.102.place_ref, bf16[1848,256]{1,0:T(8,128)(2,1)} %collective-permute-done.refs_1_.refs_0_, bf16[1848,256]{1,0:T(8,128)(2,1)S(1)} %collective-permute-done.12.refs_1_, ...), custom_call_target="tpu_custom_call" | custom-call | tf_op jit(solution)/shard_map/pallas_call | solution.py:189
  68.2 0.9 collective-permute-start.15
  69.9 6.1 %shard_map.101 = (f32[128,1024]{1,0:T(8,128)S(1)}, f32[128,1024]{1,0:T(8,128)S(1)}, f32[128,1024]{1,0:T(8,128)S(1)}, f32[128,1024]{1,0:T(8,128)S(1)}) custom-call(s32[3]{0:T(128)S(1)} %shard_map.99.place_ref, bf16[2,1848,256]{2,1,0:T(8,128)(2,1)} %collective-permute-done.7.refs_1_.refs_0_, bf16[2,1848,256]{2,1,0:T(8,128)(2,1)S(1)} %collective-permute-done.8.refs_2_.refs_1_, ...), custom_call_target="tpu_custom_call" | custom-call | tf_op jit(solution)/shard_map/pallas_call | solution.py:227
  76.1 1.5 %collective-permute-start.14 = (bf16[256,1024]{1,0:T(8,128)(2,1)S(1)}, bf16[256,1024]{1,0:T(8,128)(2,1)S(1)}, u32[]{:S(2)}, u32[]{:S(2)}) collective-permute-start(bf16[256,1024]{1,0:T(8,128)(2,1)S(1)} %shard_map.104), channel_id=1, source_target_pairs={{0,8},{4,12},{8,0},{12,4},{16,24},{20,28},{24,16},{28,20},{1,9},{5... | collective-permute-start | bytes 1572872 | tf_op jit(solution)/shard_map/ppermute | solution.py:16
  77.7 1.5 %collective-permute-start.16 = (bf16[256,1024]{1,0:T(8,128)(2,1)S(1)}, bf16[256,1024]{1,0:T(8,128)(2,1)S(1)}, u32[]{:S(2)}, u32[]{:S(2)}) collective-permute-start(bf16[256,1024]{1,0:T(8,128)(2,1)S(1)} %shard_map.105), channel_id=1, source_target_pairs={{0,16},{4,20},{8,24},{12,28},{16,0},{20,4},{24,8},{28,12},{1,17},{... | collective-permute-start | bytes 1572872 | tf_op jit(solution)/shard_map/ppermute | solution.py:16
  79.2 3.2 %shard_map.100 = (f32[128,1024]{1,0:T(8,128)S(1)}, f32[128,1024]{1,0:T(8,128)S(1)}) custom-call(s32[3]{0:T(128)S(1)} %shard_map.99.place_ref, bf16[2,1848,256]{2,1,0:T(8,128)(2,1)S(1)} %copy-done.1, bf16[640,1024]{1,0:T(8,128)(2,1)S(1)} %get-tuple-element.49.refs_1_.refs_2_, bf16[640,1024]{1,0:T(8,128)(2,1)S(1)} %get-tuple-element.50.refs_2_.refs_3_, ...), custom_call_target="tpu_custom_call" | custom-call | flops 1937768448 | bytes 7569408 | tf_op jit(solution)/shard_map/pallas_call | solution.py:189
  82.5 7.2 %collective-permute-done.14 = bf16[256,1024]{1,0:T(8,128)(2,1)S(1)} collective-permute-done((bf16[256,1024]{1,0:T(8,128)(2,1)S(1)}, bf16[256,1024]{1,0:T(8,128)(2,1)S(1)}, u32[]{:S(2)}, u32[]{:S(2)}) %collective-permute-start.14) | collective-permute-done | bytes 524320 | tf_op jit(solution)/shard_map/ppermute | solution.py:16
  89.7 1.5 %collective-permute-done.16 = bf16[256,1024]{1,0:T(8,128)(2,1)S(1)} collective-permute-done((bf16[256,1024]{1,0:T(8,128)(2,1)S(1)}, bf16[256,1024]{1,0:T(8,128)(2,1)S(1)}, u32[]{:S(2)}, u32[]{:S(2)}) %collective-permute-start.16) | collective-permute-done | bytes 524320 | tf_op jit(solution)/shard_map/ppermute | solution.py:16
  91.2 1.0 %add_convert_fusion = bf16[256,1024]{1,0:T(8,128)(2,1)} fusion(bf16[256,1024]{1,0:T(8,128)(2,1)S(1)} %collective-permute-done.16, f32[256,1024]{1,0:T(8,128)S(1)} %pad_maximum_fusion, bf16[256,1024]{1,0:T(8,128)(2,1)S(1)} %collective-permute-done.14), kind=kLoop, calls=%fused_computation.1 | loop fusion | flops 1310720 | bytes 2621440 | tf_op jit(solution)/shard_map/convert_element_type | solution.py:363
  (39 shorter events, 5.1 us)
Async XLA Ops:
  3.8 26.1 %collective-permute-start = (bf16[1848,256]{1,0:T(8,128)(2,1)}, bf16[1848,256]{1,0:T(8,128)(2,1)}, u32[]{:S(2)}, u32[]{:S(2)}) collective-permute-start(bf16[1848,256]{1,0:T(8,128)(2,1)} %get-tuple-element.32.refs_1_), channel_id=1, source_target_pairs={{0,24},{4,28},{8,16},{12,20},{16,8},{20,12},{24,0},{28,4},{1,25},{... | collective-permute-start | bytes 2838536 | tf_op jit(solution)/shard_map/ppermute | solution.py:16
  7.8 22.1 %collective-permute-start.1 = (bf16[128,1024]{1,0:T(8,128)(2,1)S(1)}, bf16[128,1024]{1,0:T(8,128)(2,1)S(1)}, u32[]{:S(2)}, u32[]{:S(2)}) collective-permute-start(bf16[128,1024]{1,0:T(8,128)(2,1)S(1)} %get-tuple-element.35.refs_4_), channel_id=1, source_target_pairs={{0,3},{1,2},{2,1},{3,0},{4,7},{5,6},{6,5},{7,4},{8,11},{9,10},{10,... | collective-permute-start | bytes 786440 | tf_op jit(solution)/shard_map/ppermute | solution.py:16
  11.4 12.6 %collective-permute-start.2 = (bf16[128,1024]{1,0:T(8,128)(2,1)}, bf16[128,1024]{1,0:T(8,128)(2,1)S(1)}, u32[]{:S(2)}, u32[]{:S(2)}) collective-permute-start(bf16[128,1024]{1,0:T(8,128)(2,1)} %get-tuple-element.33.refs_2_), channel_id=1, source_target_pairs={{0,1},{1,0},{2,3},{3,2},{4,5},{5,4},{6,7},{7,6},{8,9},{9,8},{10,11... | collective-permute-start | bytes 786440 | tf_op jit(solution)/shard_map/ppermute | solution.py:16
  11.4 22.1 %collective-permute-start.3 = (bf16[128,1024]{1,0:T(8,128)(2,1)}, bf16[128,1024]{1,0:T(8,128)(2,1)}, u32[]{:S(2)}, u32[]{:S(2)}) collective-permute-start(bf16[128,1024]{1,0:T(8,128)(2,1)} %get-tuple-element.34.refs_3_), channel_id=1, source_target_pairs={{0,2},{1,3},{2,0},{3,1},{4,6},{5,7},{6,4},{7,5},{8,10},{9,11},{10,... | collective-permute-start | bytes 786440 | tf_op jit(solution)/shard_map/ppermute | solution.py:16
  12.1 5.9 %copy-start.3 = (bf16[1024,1848]{0,1:T(8,128)(2,1)S(1)}, bf16[1024,1848]{0,1:T(8,128)(2,1)}, u32[]{:S(2)}) copy-start(bf16[1024,1848]{0,1:T(8,128)(2,1)} %param.6) | copy-start | bytes 11354116
  17.5 52.4 %collective-permute-start.7 = (bf16[2,1848,256]{2,1,0:T(8,128)(2,1)}, bf16[2,1848,256]{2,1,0:T(8,128)(2,1)}, u32[]{:S(2)}, u32[]{:S(2)}) collective-permute-start(bf16[2,1848,256]{2,1,0:T(8,128)(2,1)} %get-tuple-element.62.refs_1_), channel_id=1, source_target_pairs={{0,8},{4,12},{8,0},{12,4},{16,24},{20,28},{24,16},{28,20},{1,9},{5... | collective-permute-start | bytes 5677064 | tf_op jit(solution)/shard_map/ppermute | solution.py:16
  18.3 3.6 %copy-start = (bf16[1280,1024]{1,0:T(8,128)(2,1)}, bf16[1280,1024]{1,0:T(8,128)(2,1)S(1)}, u32[]{:S(2)}) copy-start(bf16[1280,1024]{1,0:T(8,128)(2,1)S(1)} %slice.6.refs_3_.refs_6_) | copy-start | bytes 7864324
  20.6 1.3 %copy-start.2 = (bf16[568,1024]{1,0:T(8,128)(2,1)S(1)}, bf16[568,1024]{1,0:T(8,128)(2,1)}, u32[]{:S(2)}) copy-start(bf16[568,1024]{1,0:T(8,128)(2,1)} %slice.7.refs_4_.refs_6_) | copy-start | bytes 3489796
  23.9 45.9 %collective-permute-start.8 = (bf16[2,1848,256]{2,1,0:T(8,128)(2,1)}, bf16[2,1848,256]{2,1,0:T(8,128)(2,1)S(1)}, u32[]{:S(2)}, u32[]{:S(2)}) collective-permute-start(bf16[2,1848,256]{2,1,0:T(8,128)(2,1)} %get-tuple-element.61.refs_2_), channel_id=1, source_target_pairs={{0,16},{4,20},{8,24},{12,28},{16,0},{20,4},{24,8},{28,12},{1,17},{... | collective-permute-start | bytes 5677064 | tf_op jit(solution)/shard_map/ppermute | solution.py:16
  29.9 3.6 %collective-permute-start.4 = (bf16[128,1024]{1,0:T(8,128)(2,1)S(1)}, bf16[128,1024]{1,0:T(8,128)(2,1)S(1)}, u32[]{:S(2)}, u32[]{:S(2)}) collective-permute-start(bf16[128,1024]{1,0:T(8,128)(2,1)S(1)} %collective-permute-done.2.refs_0_), channel_id=1, source_target_pairs={{0,4},{4,0},{8,12},{12,8},{16,20},{20,16},{24,28},{28,24},{1,5},{5... | collective-permute-start | bytes 786440 | tf_op jit(solution)/shard_map/ppermute | solution.py:16
  29.9 31.0 %collective-permute-start.12 = (bf16[1848,256]{1,0:T(8,128)(2,1)}, bf16[1848,256]{1,0:T(8,128)(2,1)S(1)}, u32[]{:S(2)}, u32[]{:S(2)}) collective-permute-start(bf16[1848,256]{1,0:T(8,128)(2,1)} %collective-permute-done.refs_1_.refs_0_), channel_id=1, source_target_pairs={{0,1},{1,0},{2,3},{3,2},{4,5},{5,4},{6,7},{7,6},{8,9},{9,8},{10,11... | collective-permute-start | bytes 2838536 | tf_op jit(solution)/shard_map/ppermute | solution.py:16
  33.5 2.0 %collective-permute-start.5 = (bf16[128,1024]{1,0:T(8,128)(2,1)}, bf16[128,1024]{1,0:T(8,128)(2,1)S(1)}, u32[]{:S(2)}, u32[]{:S(2)}) collective-permute-start(bf16[128,1024]{1,0:T(8,128)(2,1)} %collective-permute-done.3.refs_1_), channel_id=1, source_target_pairs={{0,4},{4,0},{8,12},{12,8},{16,20},{20,16},{24,28},{28,24},{1,5},{5... | collective-permute-start | bytes 786440 | tf_op jit(solution)/shard_map/ppermute | solution.py:16
  33.5 2.0 %collective-permute-start.6 = (bf16[128,1024]{1,0:T(8,128)(2,1)S(1)}, bf16[128,1024]{1,0:T(8,128)(2,1)S(1)}, u32[]{:S(2)}, u32[]{:S(2)}) collective-permute-start(bf16[128,1024]{1,0:T(8,128)(2,1)S(1)} %collective-permute-done.1.refs_2_), channel_id=1, source_target_pairs={{0,4},{4,0},{8,12},{12,8},{16,20},{20,16},{24,28},{28,24},{1,5},{5... | collective-permute-start | bytes 786440 | tf_op jit(solution)/shard_map/ppermute | solution.py:16
  51.0 12.8 %collective-permute-start.10 = (bf16[640,1024]{1,0:T(8,128)(2,1)S(1)}, bf16[640,1024]{1,0:T(8,128)(2,1)S(1)}, u32[]{:S(2)}, u32[]{:S(2)}) collective-permute-start(bf16[640,1024]{1,0:T(8,128)(2,1)S(1)} %get-tuple-element.50.refs_2_.refs_3_), channel_id=1, source_target_pairs={{0,4},{4,0},{8,12},{12,8},{16,20},{20,16},{24,28},{28,24},{1,5},{5... | collective-permute-start | bytes 3932168 | tf_op jit(solution)/shard_map/ppermute | solution.py:16
  51.2 12.6 %collective-permute-start.9 = (bf16[640,1024]{1,0:T(8,128)(2,1)S(1)}, bf16[640,1024]{1,0:T(8,128)(2,1)S(1)}, u32[]{:S(2)}, u32[]{:S(2)}) collective-permute-start(bf16[640,1024]{1,0:T(8,128)(2,1)S(1)} %get-tuple-element.49.refs_1_.refs_2_), channel_id=1, source_target_pairs={{0,4},{4,0},{8,12},{12,8},{16,20},{20,16},{24,28},{28,24},{1,5},{5... | collective-permute-start | bytes 3932168 | tf_op jit(solution)/shard_map/ppermute | solution.py:16
  60.9 2.9 %collective-permute-start.11 = (bf16[568,1024]{1,0:T(8,128)(2,1)S(1)}, bf16[568,1024]{1,0:T(8,128)(2,1)S(1)}, u32[]{:S(2)}, u32[]{:S(2)}) collective-permute-start(bf16[568,1024]{1,0:T(8,128)(2,1)S(1)} %get-tuple-element.51.refs_3_.refs_4_), channel_id=1, source_target_pairs={{0,4},{4,0},{8,12},{12,8},{16,20},{20,16},{24,28},{28,24},{1,5},{5... | collective-permute-start | bytes 3489800 | tf_op jit(solution)/shard_map/ppermute | solution.py:16
  67.7 8.4 %collective-permute-start.13 = (bf16[128,1024]{1,0:T(8,128)(2,1)S(1)}, bf16[128,1024]{1,0:T(8,128)(2,1)S(1)}, u32[]{:S(2)}, u32[]{:S(2)}) collective-permute-start(bf16[128,1024]{1,0:T(8,128)(2,1)S(1)} %get-tuple-element.56), channel_id=1, source_target_pairs={{0,16},{4,20},{8,24},{12,28},{16,0},{20,4},{24,8},{28,12},{1,17},{... | collective-permute-start | bytes 786440 | tf_op jit(solution)/shard_map/ppermute | solution.py:16
  68.2 9.4 %collective-permute-start.15 = (bf16[128,1024]{1,0:T(8,128)(2,1)S(1)}, bf16[128,1024]{1,0:T(8,128)(2,1)S(1)}, u32[]{:S(2)}, u32[]{:S(2)}) collective-permute-start(bf16[128,1024]{1,0:T(8,128)(2,1)S(1)} %get-tuple-element.59), channel_id=1, source_target_pairs={{0,8},{4,12},{8,0},{12,4},{16,24},{20,28},{24,16},{28,20},{1,9},{5... | collective-permute-start | bytes 786440 | tf_op jit(solution)/shard_map/ppermute | solution.py:16
  76.0 3.2 %copy-start.1 = (bf16[2,1848,256]{2,1,0:T(8,128)(2,1)S(1)}, bf16[2,1848,256]{2,1,0:T(8,128)(2,1)}, u32[]{:S(2)}) copy-start(bf16[2,1848,256]{2,1,0:T(8,128)(2,1)} %get-tuple-element.60.refs_0_) | copy-start | bytes 5677060
  76.1 13.6 %collective-permute-start.14 = (bf16[256,1024]{1,0:T(8,128)(2,1)S(1)}, bf16[256,1024]{1,0:T(8,128)(2,1)S(1)}, u32[]{:S(2)}, u32[]{:S(2)}) collective-permute-start(bf16[256,1024]{1,0:T(8,128)(2,1)S(1)} %shard_map.104), channel_id=1, source_target_pairs={{0,8},{4,12},{8,0},{12,4},{16,24},{20,28},{24,16},{28,20},{1,9},{5... | collective-permute-start | bytes 1572872 | tf_op jit(solution)/shard_map/ppermute | solution.py:16
  77.7 13.5 %collective-permute-start.16 = (bf16[256,1024]{1,0:T(8,128)(2,1)S(1)}, bf16[256,1024]{1,0:T(8,128)(2,1)S(1)}, u32[]{:S(2)}, u32[]{:S(2)}) collective-permute-start(bf16[256,1024]{1,0:T(8,128)(2,1)S(1)} %shard_map.105), channel_id=1, source_target_pairs={{0,16},{4,20},{8,24},{12,28},{16,0},{20,4},{24,8},{28,12},{1,17},{... | collective-permute-start | bytes 1572872 | tf_op jit(solution)/shard_map/ppermute | solution.py:16
